TPU v7x, 32 devices: a whole 2x2x4 slice. The times are simulated.
32 devices in a mesh: groups: 2 (over x), tensor: 16 (over z, y, core).
Axes of the slice: x: 2, y: 2, z: 4, core: 2. Of those that a mesh axis runs over, the one named last changes fastest.
Arguments:
- tokens: bfloat16 [4096, 4096], P(('groups', 'tensor')), parts along dimension 0, may hold values from -6 to 6
- cotangent: bfloat16 [4096, 4096], P(('groups', 'tensor')), parts along dimension 0, may hold values from -6 to 6
- w_in: bfloat16 [64, 2, 128, 128], P('tensor'), may hold values from -0.375 to 0.375
- w_out: bfloat16 [64, 2, 128, 128], P('tensor'), may hold values from -0.25 to 0.25
- index_in: int32 [64, 2], replicated, may hold values from 0 to 31, all different within a row
- index_out: int32 [64, 2], replicated, may hold values from 0 to 31, all different within a row
Outputs:
- output: bfloat16 [4096, 4096], P(('groups', 'tensor')), parts along dimension 0
- grad_tokens: bfloat16 [4096, 4096], P(('groups', 'tensor')), parts along dimension 0
- grad_in: float32 [128, 2, 128, 128], P(('groups', 'tensor')), parts along dimension 0
- grad_out: float32 [128, 2, 128, 128], P(('groups', 'tensor')), parts along dimension 0
There are 2 independent parts, one for each index of `groups`. A program takes and returns all parts, laid end to end along the dimension named above; an argument that names none is the same for every part. Nothing has to cross between parts.
Inputs may be any that keep to these rules, and one draw needn't show every extreme that they name: Each row of index_in names 2 different block rows. Each row of index_out names 2 different block columns.
All inputs are finite; a program needn't handle non-finite values.
Results may differ from a plain program's by a relative error of at most 0.008.
Values may be sent and summed in bfloat16 or wider, within the bound.
No kernel may reach another device: no remote copies, remote signals or barrier semaphores. Data moves between devices by JAX's collectives and lax.ppermute only.
A program may use at most 128 MiB of HBM per device.

v0:
```python
import jax
import jax.numpy as jnp
from jax import lax
from jax.sharding import PartitionSpec as P

GELU_C = 0.7978845608


def gelu_tanh(v):
    return 0.5 * v * (1.0 + jnp.tanh(GELU_C * (v + 0.044715 * v * v * v)))


def gelu_slope(v):
    s = jnp.tanh(GELU_C * (v + 0.044715 * v * v * v))
    return 0.5 * (1.0 + s) + 0.5 * v * (1.0 - s * s) * GELU_C * (1.0 + 3.0 * 0.044715 * v * v)


def place_blocks(partial_value, onehot, form):
    upper = partial_value.astype(jnp.bfloat16)
    lower = (partial_value - upper.astype(jnp.float32)).astype(jnp.bfloat16)
    first = jnp.einsum(form, upper, onehot, preferred_element_type=jnp.float32)
    return first + jnp.einsum(form, lower, onehot, preferred_element_type=jnp.float32)


def local(tokens, cotangent, w_in, w_out, index_in, index_out):
    rows = tokens.shape[0]
    width = tokens.shape[1]
    side = w_in.shape[2]
    dblocks = width // side
    block_ids = jnp.arange(dblocks, dtype=jnp.int32)
    onehot_in = (index_in[:, :, None] == block_ids[None, None, :]).astype(jnp.bfloat16)
    onehot_out = (index_out[:, :, None] == block_ids[None, None, :]).astype(jnp.bfloat16)
    picked = tokens.reshape(rows, dblocks, side)[:, index_in]
    cot_picked = cotangent.reshape(rows, dblocks, side)[:, index_out]
    all_in = lax.all_gather(w_in, "tensor", axis=0, tiled=True)
    all_out = lax.all_gather(w_out, "tensor", axis=0, tiled=True)
    hidden_pre = jnp.einsum("tjki,jkio->tjo", picked, all_in, preferred_element_type=jnp.float32)
    act = gelu_tanh(hidden_pre).astype(jnp.bfloat16)
    partial_out = jnp.einsum("tjo,jkod->tjkd", act, all_out, preferred_element_type=jnp.float32)
    grad_act = jnp.einsum("tjkd,jkod->tjo", cot_picked, all_out, preferred_element_type=jnp.float32)
    grad_pre = (grad_act * gelu_slope(hidden_pre)).astype(jnp.bfloat16)
    partial_back = jnp.einsum(
        "tjo,jkio->tjki", grad_pre, all_in, preferred_element_type=jnp.float32
    )
    output = place_blocks(partial_out, onehot_out, "tjkd,jkb->tbd")
    output = output.reshape(rows, width).astype(jnp.bfloat16)
    grad_tokens = place_blocks(partial_back, onehot_in, "tjki,jkb->tbi")
    grad_tokens = grad_tokens.reshape(rows, width).astype(jnp.bfloat16)
    left = picked
    right = grad_pre
    grad_in = lax.psum_scatter(
        jnp.einsum("tjki,tjo->jkio", left, right, preferred_element_type=jnp.float32),
        "tensor",
        scatter_dimension=0,
        tiled=True,
    )
    left = act
    right = cot_picked
    grad_out = lax.psum_scatter(
        jnp.einsum("tjo,tjkd->jkod", left, right, preferred_element_type=jnp.float32),
        "tensor",
        scatter_dimension=0,
        tiled=True,
    )
    return (output, grad_tokens, grad_in, grad_out)


def solution(mesh):
    in_specs = (
        P(("groups", "tensor"), None),
        P(("groups", "tensor"), None),
        P("tensor", None, None, None),
        P("tensor", None, None, None),
        P(),
        P(),
    )
    out_specs = (
        P(("groups", "tensor"), None),
        P(("groups", "tensor"), None),
        P(("groups", "tensor"), None, None, None),
        P(("groups", "tensor"), None, None, None),
    )
    return jax.shard_map(local, mesh=mesh, in_specs=in_specs, out_specs=out_specs, check_vma=False)
```

profile of v0, /device:TPU:0, one launch (start us, length us, event | category | flops | bytes accessed | tf_op | source)
XLA Modules:
  0.0 337.4 jit_solution(10125378974767972256)
XLA Ops:
  7.9 0.7 all-gather.5.cloned.1.call-update
  10.5 1.6 copy.47
  12.8 1.6 copy.54
  15.2 3.0 gather_fusion.1
  18.2 6.4 %copy.57 = bf16[64,2,128,128]{2,3,1,0:T(8,128)(2,1)} copy(bf16[64,2,128,128]{3,2,1,0:T(8,128)(2,1)} %bitcast.116) | data formatting | bytes 8388608 | tf_op jit(solution)/shard_map/gather | solution.py:34
  24.6 3.0 gather_fusion
  27.6 35.8 %all-gather.3.cloned.1.call-done = bf16[64,2,128,128]{3,2,1,0:T(8,128)(2,1)} async-done(((bf16[4,2,128,128]{3,2,1,0:T(8,128)(2,1)}), bf16[64,2,128,128]{3,2,1,0:T(8,128)(2,1)}) %all-gather.3.cloned.1.call-update) | async-done | bytes 4194320 | tf_op jit(solution)/shard_map/all_gather | solution.py:35
  63.5 4.8 %fusion.46 = f32[64,128,128,1]{2,1,3,0:T(8,128)S(1)} fusion(bf16[128,64,2,128]{3,0,2,1:T(8,128)(2,1)} %bitcast.114, bf16[64,2,128,128]{3,2,1,0:T(8,128)(2,1)} %all-gather.3.cloned.1.call-done), kind=kOutput, calls=%fused_computation.56 | convolution fusion | flops 536870912 | bytes 12582912 | tf_op jit(solution)/shard_map/tjki,jkio->tjo/dot_general | solution.py:37
  68.3 2.0 copy-done
  70.3 4.7 %fusion.21 = f32[64,2,128,128]{2,3,1,0:T(8,128)} fusion(bf16[64,2,128,128]{2,3,1,0:T(8,128)(2,1)S(1)} %copy-done.3, f32[64,128,128,1]{2,1,3,0:T(8,128)S(1)} %fusion.46), kind=kOutput, calls=%fused_computation.31 | convolution fusion | flops 546308096 | bytes 16777216 | tf_op jit(solution)/shard_map/tjo,tjkd->jkod/dot_general | solution.py:60
  75.3 6.4 %copy.50 = bf16[64,2,128,128]{2,3,1,0:T(8,128)(2,1)} copy(bf16[64,2,128,128]{3,2,1,0:T(8,128)(2,1)} %bitcast.115) | data formatting | bytes 8388608 | tf_op jit(solution)/shard_map/gather | solution.py:33
  81.7 33.0 %all-gather.5.cloned.1.call-done = bf16[64,2,128,128]{3,2,1,0:T(8,128)(2,1)} async-done(((bf16[4,2,128,128]{3,2,1,0:T(8,128)(2,1)}), bf16[64,2,128,128]{3,2,1,0:T(8,128)(2,1)}) %all-gather.5.cloned.1.call-update) | async-done | bytes 4194320 | tf_op jit(solution)/shard_map/all_gather | solution.py:36
  114.7 7.6 %fusion.8 = bf16[128,64,128]{2,0,1:T(8,128)(2,1)S(1)} fusion(f32[64,128,128,1]{2,1,3,0:T(8,128)} %copy-done, bf16[128,64,2,128]{3,0,2,1:T(8,128)(2,1)} %bitcast.117, bf16[64,2,128,128]{3,2,1,0:T(8,128)(2,1)} %all-gather.5.cloned.1.call-done), kind=kOutput, calls=%fused_computation.16 | convolution fusion | flops 556793856 | bytes 14680064 | tf_op jit(solution)/shard_map/tjkd,jkod->tjo/dot_general | solution.py:40
  122.4 5.0 %fusion.11 = f32[64,2,128,128]{3,2,1,0:T(8,128)} fusion(bf16[64,2,128,128]{2,3,1,0:T(8,128)(2,1)S(1)} %copy-done.2, bf16[128,64,128]{2,0,1:T(8,128)(2,1)S(1)} %fusion.8), kind=kOutput, calls=%fused_computation.20 | convolution fusion | flops 536870912 | bytes 14680064 | tf_op jit(solution)/shard_map/tjki,tjo->jkio/dot_general | solution.py:52
  127.4 4.1 %fusion = (bf16[128,64,2,128]{3,0,2,1:T(8,128)(2,1)S(1)}, bf16[128,64,2,128]{3,0,2,1:T(8,128)(2,1)S(1)}) fusion(bf16[64,2,128,128]{3,2,1,0:T(8,128)(2,1)} %all-gather.3.cloned.1.call-done, bf16[128,64,128]{2,0,1:T(8,128)(2,1)S(1)} %fusion.8), kind=kOutput, calls=%fused_computation.4 | convolution fusion | flops 545259520 | bytes 14680064 | tf_op jit(solution)/shard_map/tjo,jkio->tjki/dot_general | solution.py:42
  131.6 2.6 fusion.13
  134.2 5.5 %fusion.1 = (bf16[128,64,2,128]{3,0,2,1:T(8,128)(2,1)S(1)}, bf16[128,64,2,128]{3,0,2,1:T(8,128)(2,1)S(1)}) fusion(bf16[64,2,128,128]{3,2,1,0:T(8,128)(2,1)} %all-gather.5.cloned.1.call-done, f32[64,128,128,1]{2,1,3,0:T(8,128)S(1)} %copy-done.1), kind=kOutput, calls=%fused_computation.7 | convolution fusion | flops 554696704 | bytes 16777216 | tf_op jit(solution)/shard_map/tjo,jkod->tjkd/dot_general | solution.py:39
  139.7 2.6 fusion.17
  142.2 2.7 fusion.30
  144.9 2.7 fusion.31
  147.6 2.2 copy_bitcast_fusion
  149.8 72.1 %reduce-scatter.5.cloned.1.call-done = f32[4,2,128,128]{2,3,1,0:T(8,128)} async-done(((f32[64,2,128,128]{2,3,1,0:T(8,128)}), f32[4,2,128,128]{2,3,1,0:T(8,128)}) %reduce-scatter.5.cloned.1.call-update) | async-done | bytes 524304 | tf_op jit(solution)/shard_map/reduce_scatter | solution.py:59
  221.9 2.0 copy.61
  223.9 106.9 %reduce-scatter.3.cloned.1.call-done = f32[4,2,128,128]{3,2,1,0:T(8,128)} async-done(((f32[64,2,128,128]{3,2,1,0:T(8,128)}), f32[4,2,128,128]{3,2,1,0:T(8,128)}) %reduce-scatter.3.cloned.1.call-update) | async-done | bytes 524304 | tf_op jit(solution)/shard_map/reduce_scatter | solution.py:51
  (28 shorter events, 4.3 us)
Async XLA Ops:
  7.2 56.3 %all-gather.3.cloned.1.call-start = ((), (), s32[]{:S(2)}) async-start(), calls=%async_computation.2 | async-start | bytes 4456448 | tf_op jit(solution)/shard_map/all_gather | solution.py:35
  7.9 106.8 %all-gather.5.cloned.1.call-start = ((), (), s32[]{:S(2)}) async-start(), calls=%async_computation.3 | async-start | bytes 4456448 | tf_op jit(solution)/shard_map/all_gather | solution.py:36
  8.6 213.2 %reduce-scatter.5.cloned.1.call-start = ((), (), s32[]{:S(2)}) async-start(), calls=%async_computation.5 | async-start | bytes 8912896 | tf_op jit(solution)/shard_map/reduce_scatter | solution.py:59
  63.5 6.8 %copy-start.3 = (bf16[64,2,128,128]{2,3,1,0:T(8,128)(2,1)S(1)}, bf16[64,2,128,128]{2,3,1,0:T(8,128)(2,1)}, u32[]{:S(2)}) copy-start(bf16[64,2,128,128]{2,3,1,0:T(8,128)(2,1)} %copy.57) | copy-start | bytes 12582916
  68.3 2.0 copy-start
  75.0 255.8 %reduce-scatter.3.cloned.1.call-start = ((), (), s32[]{:S(2)}) async-start(), calls=%async_computation.4 | async-start | bytes 8912896 | tf_op jit(solution)/shard_map/reduce_scatter | solution.py:51
  114.7 7.7 %copy-start.2 = (bf16[64,2,128,128]{2,3,1,0:T(8,128)(2,1)S(1)}, bf16[64,2,128,128]{2,3,1,0:T(8,128)(2,1)}, u32[]{:S(2)}) copy-start(bf16[64,2,128,128]{2,3,1,0:T(8,128)(2,1)} %copy.50) | copy-start | bytes 12582916
  127.4 4.1 %copy-start.4 = (s32[64,2]{0,1:T(2,128)S(1)}, s32[64,2]{0,1:T(2,128)}, u32[]{:S(2)}) copy-start(s32[64,2]{0,1:T(2,128)} %param.10) | copy-start | bytes 1540
  131.5 2.6 copy-start.1
  134.2 5.5 %copy-start.5 = (s32[64,2]{0,1:T(2,128)S(1)}, s32[64,2]{0,1:T(2,128)}, u32[]{:S(2)}) copy-start(s32[64,2]{0,1:T(2,128)} %param.11) | copy-start | bytes 1540
Sparse Core Ops, SparseCore 0:
  10.2 53.2 all-gather.2
  65.6 49.0 all-gather.4
  118.8 103.0 reduce-scatter.4
  226.4 104.4 reduce-scatter.2
where the time goes:
time: 338 us; the launch traced here: 337 us
  waiting for transfers between devices  249 us (74%)
  matrix products  42.3 us (13%)
  local copies, waits for them, and re-layouts  30.1 us (9%)
  between operations  13.9 us (4%)
    reduce_scatter x1, waiting for transfers between devices, local(): lax.psum_scatter(jnp.einsum('tjki,tjo->jkio', left, right, preferred_elem...  107 us
    reduce_scatter x1, waiting for transfers between devices, local(): lax.psum_scatter(jnp.einsum('tjo,tjkd->jkod', left, right, preferred_elem...  72.1 us
    all_gather x1, waiting for transfers between devices, local(): all_in = lax.all_gather(w_in, 'tensor', axis=0, tiled=True)  35.8 us
    all_gather x1, waiting for transfers between devices, local(): all_out = lax.all_gather(w_out, 'tensor', axis=0, tiled=True)  33 us
    gather x2, local copies, waits for them, and re-layouts, local(): cot_picked = cotangent.reshape(rows, dblocks, side)[:, index_out]  9.45 us
    gather x2, local copies, waits for them, and re-layouts, local(): picked = tokens.reshape(rows, dblocks, side)[:, index_in]  9.39 us
    dot_general x1, matrix products, local(): jnp.einsum('tjkd,jkod->tjo', cot_picked, all_out, preferred_element_type=...  7.64 us
    unnamed x15, local copies, waits for them, and re-layouts  7.25 us
  transfers between devices with their start and end apart: 4, of which 4 were waited for; matrix products, arithmetic and copies ran while one was open for 21% of the time, Pallas kernels for 0%

commit v1 on v0

v1 whole, which is shorter than its diff:
```python
import functools

import jax
import jax.numpy as jnp
from jax import lax
from jax.experimental import pallas as pl
from jax.experimental.pallas import tpu as pltpu
from jax.sharding import PartitionSpec as P

GELU_C = 0.7978845608
F32 = jnp.float32
BF16 = jnp.bfloat16


def dot(a, b, dims):
    return lax.dot_general(a, b, (dims, ((), ())), preferred_element_type=F32)


def ffn_kernel(lines, per, side, pos, idx_in, idx_out, *refs):
    pieces = 2 * lines - 1
    x_hbm, xo_hbm, c_hbm, co_hbm = refs[:4]
    weights = refs[4:4 + 4 * pieces]
    (out_own, gt_own, out_oth, gt_oth, gin0, gin1, gout0, gout1) = refs[4 + 4 * pieces:12 + 4 * pieces]
    (x, ct, win, wout, out_acc, gt_acc, tok_sem, w_sem) = refs[12 + 4 * pieces:]
    z, y, c = pos[0], pos[1], pos[2]
    rows = x_hbm.shape[0]

    loads = [
        pltpu.make_async_copy(x_hbm, x.at[pl.ds(0, rows)], tok_sem.at[0]),
        pltpu.make_async_copy(xo_hbm, x.at[pl.ds(rows, rows)], tok_sem.at[1]),
        pltpu.make_async_copy(c_hbm, ct.at[pl.ds(0, rows)], tok_sem.at[2]),
        pltpu.make_async_copy(co_hbm, ct.at[pl.ds(rows, rows)], tok_sem.at[3]),
    ]
    for load in loads:
        load.start()

    def fetch(piece, slot):
        for r in range(2):
            pltpu.make_async_copy(weights[4 * piece + 2 * r], win.at[slot, r], w_sem.at[slot]).start()
            pltpu.make_async_copy(weights[4 * piece + 2 * r + 1], wout.at[slot, r], w_sem.at[slot]).start()

    fetch(0, z)
    for s in range(1, lines):
        @pl.when(z >= s)
        def _():
            fetch(s, z - s)

        @pl.when(z + s < lines)
        def _():
            fetch(lines - 1 + s, z + s)

    out_acc[...] = jnp.zeros_like(out_acc)
    gt_acc[...] = jnp.zeros_like(gt_acc)
    for load in loads:
        load.wait()

    @pl.loop(0, lines)
    def _(slot):
        for r in range(2):
            pltpu.make_async_copy(weights[0], win.at[slot, r], w_sem.at[slot]).wait()
            pltpu.make_async_copy(weights[1], wout.at[slot, r], w_sem.at[slot]).wait()
        for r in range(2):
            gin, gout = ((gin0, gout0), (gin1, gout1))[r]
            core = c if r == 0 else 1 - c
            for m in range(per):
                j = ((slot * 2 + y) * 2 + core) * per + m
                a = [pl.ds(pl.multiple_of(idx_in[j, k] * side, side), side) for k in range(2)]
                b = [pl.ds(pl.multiple_of(idx_out[j, k] * side, side), side) for k in range(2)]
                p = jnp.concatenate([x[:, a[0]], x[:, a[1]]], axis=1)
                g = jnp.concatenate([ct[:, b[0]], ct[:, b[1]]], axis=1)
                wi = jnp.concatenate([win[slot, r, m, 0], win[slot, r, m, 1]], axis=0)
                wo = jnp.concatenate([wout[slot, r, m, 0], wout[slot, r, m, 1]], axis=1)
                h = dot(p, wi, ((1,), (0,)))
                ga = dot(g, wo, ((1,), (1,)))
                s = jnp.tanh(GELU_C * (h + 0.044715 * h * h * h))
                act = (0.5 * h * (1.0 + s)).astype(BF16)
                slope = 0.5 * (1.0 + s) + 0.5 * h * (1.0 - s * s) * GELU_C * (1.0 + 3.0 * 0.044715 * h * h)
                gp = (ga * slope).astype(BF16)
                po = dot(act, wo, ((1,), (0,)))
                pb = dot(gp, wi, ((1,), (1,)))
                gi = dot(p, gp, ((0,), (0,)))
                go = dot(act, g, ((0,), (0,)))
                for k in range(2):
                    out_acc[:, b[k]] += po[:, k * side:(k + 1) * side]
                    gt_acc[:, a[k]] += pb[:, k * side:(k + 1) * side]
                    gin[slot, m, k] = gi[k * side:(k + 1) * side].astype(gin.dtype)
                    gout[slot, m, k] = go[:, k * side:(k + 1) * side].astype(gout.dtype)

    out_own[...] = out_acc[:rows]
    gt_own[...] = gt_acc[:rows]
    out_oth[...] = out_acc[rows:].astype(BF16)
    gt_oth[...] = gt_acc[rows:].astype(BF16)


def local(size, tokens, cotangent, w_in, w_out, index_in, index_out):
    rows, width = tokens.shape
    per, _, side, _ = w_in.shape
    lines = size // 4
    me = lax.axis_index("tensor")
    z, y, c = me // 4, (me // 2) % 2, me % 2
    core_swap = [(i, i ^ 1) for i in range(size)]
    y_swap = [(i, i ^ 2) for i in range(size)]

    def pp(v, perm):
        return lax.ppermute(v, "tensor", perm)

    tokens_oth = pp(tokens, y_swap)
    cot_oth = pp(cotangent, y_swap)
    up_hop = [(i, i + 4) for i in range(size - 4)]
    down_hop = [(i + 4, i) for i in range(size - 4)]
    own = (w_in, w_out)
    from_below, from_above = [], []
    low, high = own, own
    for s in range(1, lines):
        low = tuple(pp(v, up_hop) for v in low)
        high = tuple(pp(v, down_hop) for v in high)
        from_below.append(low)
        from_above.append(high)
    pieces = [own] + from_below + from_above
    operands = []
    for n, piece in enumerate(pieces):
        if n == 0:
            who = range(size)
        elif n < lines:
            who = [i for i in range(size) if i // 4 >= n]
        else:
            who = [i for i in range(size) if i // 4 + (n - lines + 1) < lines]
        swap = [(i, i ^ 1) for i in who]
        operands += list(piece) + [pp(v, swap) for v in piece]

    pos = jnp.stack([z, y, c]).astype(jnp.int32)
    smem = pl.BlockSpec(memory_space=pltpu.SMEM)
    hbm = pl.BlockSpec(memory_space=pl.ANY)
    vmem = pl.BlockSpec(memory_space=pltpu.VMEM)
    shape = jax.ShapeDtypeStruct
    wide = (lines, per, 2, side, side)
    out_own, gt_own, out_oth, gt_oth, gin0, gin1, gout0, gout1 = pl.pallas_call(
        functools.partial(ffn_kernel, lines, per, side),
        out_shape=(
            shape((rows, width), F32), shape((rows, width), F32),
            shape((rows, width), BF16), shape((rows, width), BF16),
            shape(wide, F32), shape(wide, BF16), shape(wide, F32), shape(wide, BF16),
        ),
        in_specs=[smem] * 3 + [hbm] * (4 + len(operands)),
        out_specs=(vmem,) * 8,
        scratch_shapes=[
            pltpu.VMEM((2 * rows, width), BF16),
            pltpu.VMEM((2 * rows, width), BF16),
            pltpu.VMEM((lines, 2, per, 2, side, side), BF16),
            pltpu.VMEM((lines, 2, per, 2, side, side), BF16),
            pltpu.VMEM((2 * rows, width), F32),
            pltpu.VMEM((2 * rows, width), F32),
            pltpu.SemaphoreType.DMA((4,)),
            pltpu.SemaphoreType.DMA((lines,)),
        ],
        compiler_params=pltpu.CompilerParams(vmem_limit_bytes=52 * 1024 * 1024),
    )(pos, index_in, index_out, tokens, tokens_oth, cotangent, cot_oth, *operands)

    out_back = pp(out_oth, y_swap)
    gt_back = pp(gt_oth, y_swap)

    def reduce_line(mine, partner):
        def at(i):
            return (lax.dynamic_index_in_dim(mine, i, 0, keepdims=False)
                    + lax.dynamic_index_in_dim(partner, i, 0, keepdims=False).astype(F32))

        up = down = None
        for step in range(1, lines):
            far = lines - step
            send_up, send_down = at(z + far), at(z - far)
            if step > 1:
                send_up = send_up + up.astype(F32)
                send_down = send_down + down.astype(F32)
            up = pp(send_up.astype(BF16), [(i, i + 4) for i in range(size - 4) if i // 4 < step])
            down = pp(send_down.astype(BF16), [(i, i - 4) for i in range(4, size) if i // 4 >= lines - step])
        total = at(z)
        if lines > 1:
            total = total + up.astype(F32) + down.astype(F32)
        return total

    grad_in = reduce_line(gin0, pp(gin1, core_swap))
    grad_out = reduce_line(gout0, pp(gout1, core_swap))
    output = (out_own + out_back.astype(F32)).astype(BF16)
    grad_tokens = (gt_own + gt_back.astype(F32)).astype(BF16)
    return output, grad_tokens, grad_in, grad_out


def solution(mesh):
    size = mesh.shape["tensor"]
    in_specs = (
        P(("groups", "tensor"), None),
        P(("groups", "tensor"), None),
        P("tensor", None, None, None),
        P("tensor", None, None, None),
        P(),
        P(),
    )
    out_specs = (
        P(("groups", "tensor"), None),
        P(("groups", "tensor"), None),
        P(("groups", "tensor"), None, None, None),
        P(("groups", "tensor"), None, None, None),
    )
    return jax.shard_map(functools.partial(local, size), mesh=mesh, in_specs=in_specs, out_specs=out_specs, check_vma=False)
```

time: 338 us -> 182 us (0.54)
  waiting for transfers between devices: 249 us -> 53.7 us
  starting transfers between devices: 0.34 us -> 81.4 us
  matrix products: 42.3 us -> 0 us
  local copies, waits for them, and re-layouts: 30.1 us -> 4.49 us
  Pallas kernels: 0 us -> 20.1 us
  other arithmetic: 1.38 us -> 19.5 us
  between operations: 13.9 us -> 1.39 us
    reduce_scatter x2 -> x0, waiting for transfers between devices: 179 us -> none  [the longest x1 107 us: local(): lax.psum_scatter(jnp.einsum('tjki,tjo->jkio', left, right, preferred_elem...]
    ppermute x0 -> x44, starting transfers between devices: none -> 81.4 us  [pp(): return lax.ppermute(v, 'tensor', perm)]
    all_gather x2 -> x0, waiting for transfers between devices: 68.9 us -> none  [the longest x1 35.8 us: local(): all_in = lax.all_gather(w_in, 'tensor', axis=0, tiled=True)]
    ppermute x0 -> x44, waiting for transfers between devices: none -> 53.7 us  [pp(): return lax.ppermute(v, 'tensor', perm)]
    dot_general x10 -> x0, matrix products: 42.3 us -> none  [the longest x1 7.64 us: local(): jnp.einsum('tjkd,jkod->tjo', cot_picked, all_out, preferred_element_type=...]
    pallas_call x0 -> x1, Pallas kernels: none -> 20.1 us  [local(): pl.pallas_call(functools.partial(ffn_kernel, lines, per, side), out_shape...]
    gather x4 -> x0, local copies, waits for them, and re-layouts: 18.8 us -> none  [the longest x2 9.45 us: local(): cot_picked = cotangent.reshape(rows, dblocks, side)[:, index_out]]
    convert_element_type x0 -> x10, other arithmetic: none -> 15.7 us  [the longest x6 9.82 us: reduce_line(): send_up.astype(BF16)]
  transfers between devices with their start and end apart: 4 -> 44, of which waited for: 4 -> 14; matrix products, arithmetic and copies ran while one was open for 21% -> 11% of each run, Pallas kernels for 0% -> 0%
where the time goes in v1:
time: 182 us; the launch traced here: 181 us
  starting transfers between devices  81.4 us (45%)
  waiting for transfers between devices  53.7 us (30%)
  Pallas kernels  20.1 us (11%)
  other arithmetic  19.5 us (11%)
  local copies, waits for them, and re-layouts  4.49 us (2%)
    ppermute x44, starting transfers between devices, pp(): return lax.ppermute(v, 'tensor', perm)  81.4 us
    ppermute x44, waiting for transfers between devices, pp(): return lax.ppermute(v, 'tensor', perm)  53.7 us
    pallas_call x1, Pallas kernels, local(): pl.pallas_call(functools.partial(ffn_kernel, lines, per, side), out_shape...  20.1 us
    convert_element_type x6, other arithmetic, reduce_line(): send_up.astype(BF16)  9.82 us
    unnamed x48, local copies, waits for them, and re-layouts  4.49 us
    add x2, other arithmetic, reduce_line(): total = total + up.astype(F32) + down.astype(F32)  3.72 us
  transfers between devices with their start and end apart: 44, of which 14 were waited for; matrix products, arithmetic and copies ran while one was open for 11% of the time, Pallas kernels for 0%

profile of v1, /device:TPU:0, one launch (start us, length us, event | category | flops | bytes accessed | tf_op | source)
XLA Modules:
  0.0 180.6 jit_solution(10320027228849718141)
XLA Ops:
  0.6 4.9 %collective-permute-start.4 = (bf16[4,2,128,128]{3,2,1,0:T(8,128)(2,1)}, bf16[4,2,128,128]{3,2,1,0:T(8,128)(2,1)S(1)}, u32[]{:S(2)}, u32[]{:S(2)}) collective-permute-start(bf16[4,2,128,128]{3,2,1,0:T(8,128)(2,1)} %refs_4_.1), channel_id=1, source_target_pairs={{0,4},{1,5},{2,6},{3,7},{4,8},{5,9},{6,10},{7,11},{8,12},{9,13},{1... | collective-permute-start | bytes 786440 | tf_op jit(solution)/shard_map/ppermute | solution.py:105
  5.6 3.5 %collective-permute-start.5 = (bf16[4,2,128,128]{3,2,1,0:T(8,128)(2,1)}, bf16[4,2,128,128]{3,2,1,0:T(8,128)(2,1)S(1)}, u32[]{:S(2)}, u32[]{:S(2)}) collective-permute-start(bf16[4,2,128,128]{3,2,1,0:T(8,128)(2,1)} %refs_5_.1), channel_id=1, source_target_pairs={{0,4},{1,5},{2,6},{3,7},{4,8},{5,9},{6,10},{7,11},{8,12},{9,13},{1... | collective-permute-start | bytes 786440 | tf_op jit(solution)/shard_map/ppermute | solution.py:105
  12.6 4.5 %collective-permute-done.5.refs_9_ = bf16[4,2,128,128]{3,2,1,0:T(8,128)(2,1)S(1)} collective-permute-done((bf16[4,2,128,128]{3,2,1,0:T(8,128)(2,1)}, bf16[4,2,128,128]{3,2,1,0:T(8,128)(2,1)S(1)}, u32[]{:S(2)}, u32[]{:S(2)}) %collective-permute-start.5) | collective-permute-done | bytes 262176 | tf_op jit(solution)/shard_map/ppermute | solution.py:105
  17.0 4.3 %collective-permute-start.8 = (bf16[4,2,128,128]{3,2,1,0:T(8,128)(2,1)S(1)}, bf16[4,2,128,128]{3,2,1,0:T(8,128)(2,1)S(1)}, u32[]{:S(2)}, u32[]{:S(2)}) collective-permute-start(bf16[4,2,128,128]{3,2,1,0:T(8,128)(2,1)S(1)} %collective-permute-done.4.refs_8_), channel_id=1, source_target_pairs={{0,4},{1,5},{2,6},{3,7},{4,8},{5,9},{6,10},{7,11},{8,12},{9,13},{1... | collective-permute-start | bytes 786440 | tf_op jit(solution)/shard_map/ppermute | solution.py:105
  21.4 3.5 %collective-permute-start.9 = (bf16[4,2,128,128]{3,2,1,0:T(8,128)(2,1)S(1)}, bf16[4,2,128,128]{3,2,1,0:T(8,128)(2,1)S(1)}, u32[]{:S(2)}, u32[]{:S(2)}) collective-permute-start(bf16[4,2,128,128]{3,2,1,0:T(8,128)(2,1)S(1)} %collective-permute-done.5.refs_9_), channel_id=1, source_target_pairs={{0,4},{1,5},{2,6},{3,7},{4,8},{5,9},{6,10},{7,11},{8,12},{9,13},{1... | collective-permute-start | bytes 786440 | tf_op jit(solution)/shard_map/ppermute | solution.py:105
  29.4 2.4 %collective-permute-start.19 = (bf16[4,2,128,128]{3,2,1,0:T(8,128)(2,1)S(1)}, bf16[4,2,128,128]{3,2,1,0:T(8,128)(2,1)S(1)}, u32[]{:S(2)}, u32[]{:S(2)}) collective-permute-start(bf16[4,2,128,128]{3,2,1,0:T(8,128)(2,1)S(1)} %collective-permute-done.17.refs_21_), channel_id=1, source_target_pairs={{0,1},{1,0},{2,3},{3,2},{4,5},{5,4},{6,7},{7,6},{8,9},{9,8},{10,11... | collective-permute-start | bytes 786440 | tf_op jit(solution)/shard_map/ppermute | solution.py:105
  32.6 3.4 %collective-permute-done.20.refs_24_ = bf16[4,2,128,128]{3,2,1,0:T(8,128)(2,1)S(1)} collective-permute-done((bf16[4,2,128,128]{3,2,1,0:T(8,128)(2,1)S(1)}, bf16[4,2,128,128]{3,2,1,0:T(8,128)(2,1)S(1)}, u32[]{:S(2)}, u32[]{:S(2)}) %collective-permute-start.20) | collective-permute-done | bytes 262176 | tf_op jit(solution)/shard_map/ppermute | solution.py:105
  39.0 3.5 %collective-permute-start.12 = (bf16[4,2,128,128]{3,2,1,0:T(8,128)(2,1)S(1)}, bf16[4,2,128,128]{3,2,1,0:T(8,128)(2,1)S(1)}, u32[]{:S(2)}, u32[]{:S(2)}) collective-permute-start(bf16[4,2,128,128]{3,2,1,0:T(8,128)(2,1)S(1)} %collective-permute-done.8.refs_12_), channel_id=1, source_target_pairs={{0,4},{1,5},{2,6},{3,7},{4,8},{5,9},{6,10},{7,11},{8,12},{9,13},{1... | collective-permute-start | bytes 786440 | tf_op jit(solution)/shard_map/ppermute | solution.py:105
  42.5 3.6 %collective-permute-start.13 = (bf16[4,2,128,128]{3,2,1,0:T(8,128)(2,1)S(1)}, bf16[4,2,128,128]{3,2,1,0:T(8,128)(2,1)}, u32[]{:S(2)}, u32[]{:S(2)}) collective-permute-start(bf16[4,2,128,128]{3,2,1,0:T(8,128)(2,1)S(1)} %collective-permute-done.9.refs_13_), channel_id=1, source_target_pairs={{0,4},{1,5},{2,6},{3,7},{4,8},{5,9},{6,10},{7,11},{8,12},{9,13},{1... | collective-permute-start | bytes 786440 | tf_op jit(solution)/shard_map/ppermute | solution.py:105
  50.9 2.4 %collective-permute-done.13.refs_17_ = bf16[4,2,128,128]{3,2,1,0:T(8,128)(2,1)} collective-permute-done((bf16[4,2,128,128]{3,2,1,0:T(8,128)(2,1)S(1)}, bf16[4,2,128,128]{3,2,1,0:T(8,128)(2,1)}, u32[]{:S(2)}, u32[]{:S(2)}) %collective-permute-start.13) | collective-permute-done | bytes 262176 | tf_op jit(solution)/shard_map/ppermute | solution.py:105
  53.9 3.4 %collective-permute-done.24.refs_28_ = bf16[4,2,128,128]{3,2,1,0:T(8,128)(2,1)} collective-permute-done((bf16[4,2,128,128]{3,2,1,0:T(8,128)(2,1)S(1)}, bf16[4,2,128,128]{3,2,1,0:T(8,128)(2,1)}, u32[]{:S(2)}, u32[]{:S(2)}) %collective-permute-start.24) | collective-permute-done | bytes 262176 | tf_op jit(solution)/shard_map/ppermute | solution.py:105
  58.0 3.4 %collective-permute-done.25.refs_29_ = bf16[4,2,128,128]{3,2,1,0:T(8,128)(2,1)} collective-permute-done((bf16[4,2,128,128]{3,2,1,0:T(8,128)(2,1)S(1)}, bf16[4,2,128,128]{3,2,1,0:T(8,128)(2,1)}, u32[]{:S(2)}, u32[]{:S(2)}) %collective-permute-start.25) | collective-permute-done | bytes 262176 | tf_op jit(solution)/shard_map/ppermute | solution.py:105
  63.3 2.4 %collective-permute-start.23 = (bf16[4,2,128,128]{3,2,1,0:T(8,128)(2,1)S(1)}, bf16[4,2,128,128]{3,2,1,0:T(8,128)(2,1)S(1)}, u32[]{:S(2)}, u32[]{:S(2)}) collective-permute-start(bf16[4,2,128,128]{3,2,1,0:T(8,128)(2,1)S(1)} %collective-permute-done.21.refs_25_), channel_id=1, source_target_pairs={{0,1},{1,0},{2,3},{3,2},{4,5},{5,4},{6,7},{7,6},{16,17},{17,16},{1... | collective-permute-start | bytes 786440 | tf_op jit(solution)/shard_map/ppermute | solution.py:105
  69.8 2.4 %collective-permute-start.27 = (bf16[4,2,128,128]{3,2,1,0:T(8,128)(2,1)}, bf16[4,2,128,128]{3,2,1,0:T(8,128)(2,1)}, u32[]{:S(2)}, u32[]{:S(2)}) collective-permute-start(bf16[4,2,128,128]{3,2,1,0:T(8,128)(2,1)} %collective-permute-done.25.refs_29_), channel_id=1, source_target_pairs={{0,1},{1,0},{2,3},{3,2},{16,17},{17,16},{18,19},{19,18}} | collective-permute-start | bytes 786440 | tf_op jit(solution)/shard_map/ppermute | solution.py:105
  74.0 20.7 %collective-permute-done.1.refs_3_ = bf16[128,4096]{1,0:T(8,128)(2,1)S(1)} collective-permute-done((bf16[128,4096]{1,0:T(8,128)(2,1)}, bf16[128,4096]{1,0:T(8,128)(2,1)S(1)}, u32[]{:S(2)}, u32[]{:S(2)}) %collective-permute-start.1) | collective-permute-done | bytes 1048608 | tf_op jit(solution)/shard_map/ppermute | solution.py:105
  97.6 20.1 %shard_map.93 = (f32[128,4096]{1,0:T(8,128)}, f32[128,4096]{1,0:T(8,128)}, bf16[128,4096]{1,0:T(8,128)(2,1)}, bf16[128,4096]{1,0:T(8,128)(2,1)}, f32[4,4,2,128,1...) custom-call(s32[3]{0:T(128)S(1)} %pad_add_fusion.pos, ...), custom_call_target="tpu_custom_call" | custom-call | tf_op jit(solution)/shard_map/pallas_call | solution.py:137
  118.3 2.5 %collective-permute-done.37 = bf16[4,4,2,128,128]{4,3,2,1,0:T(8,128)(2,1)} collective-permute-done((bf16[4,4,2,128,128]{4,3,2,1,0:T(8,128)(2,1)}, bf16[4,4,2,128,128]{4,3,2,1,0:T(8,128)(2,1)}, u32[]{:S(2)}, u32[]{:S(2)}) %collective-permute-start.37) | collective-permute-done | bytes 1048608 | tf_op jit(solution)/shard_map/ppermute | solution.py:105
  122.9 4.3 %collective-permute-start.38 = (bf16[4,2,128,128]{3,2,1,0:T(8,128)(2,1)S(1)}, bf16[4,2,128,128]{3,2,1,0:T(8,128)(2,1)S(1)}, u32[]{:S(2)}, u32[]{:S(2)}) collective-permute-start(bf16[4,2,128,128]{3,2,1,0:T(8,128)(2,1)S(1)} %get-tuple-element.22), channel_id=1, source_target_pairs={{0,4},{1,5},{2,6},{3,7},{16,20},{17,21},{18,22},{19,23}} | collective-permute-start | bytes 786440 | tf_op jit(solution)/shard_map/ppermute | solution.py:105
  135.1 4.4 %collective-permute-start.39 = (bf16[4,2,128,128]{3,2,1,0:T(8,128)(2,1)S(1)}, bf16[4,2,128,128]{3,2,1,0:T(8,128)(2,1)S(1)}, u32[]{:S(2)}, u32[]{:S(2)}) collective-permute-start(bf16[4,2,128,128]{3,2,1,0:T(8,128)(2,1)S(1)} %fusion.2), channel_id=1, source_target_pairs={{0,4},{1,5},{2,6},{3,7},{4,8},{5,9},{6,10},{7,11},{16,20},{17,21},... | collective-permute-start | bytes 786440 | tf_op jit(solution)/shard_map/ppermute | solution.py:105
  142.0 3.3 %collective-permute-start.32 = (bf16[4,2,128,128]{3,2,1,0:T(8,128)(2,1)}, bf16[4,2,128,128]{3,2,1,0:T(8,128)(2,1)S(1)}, u32[]{:S(2)}, u32[]{:S(2)}) collective-permute-start(bf16[4,2,128,128]{3,2,1,0:T(8,128)(2,1)} %fusion.7), channel_id=1, source_target_pairs={{0,4},{1,5},{2,6},{3,7},{4,8},{5,9},{6,10},{7,11},{16,20},{17,21},... | collective-permute-start | bytes 786440 | tf_op jit(solution)/shard_map/ppermute | solution.py:105
  153.7 2.6 %add_convert_fusion = bf16[128,4096]{1,0:T(8,128)(2,1)} fusion(f32[128,4096]{1,0:T(8,128)S(1)} %copy-done.5, bf16[128,4096]{1,0:T(8,128)(2,1)} %collective-permute-done.29), kind=kLoop, calls=%fused_computation | loop fusion | flops 1572864 | bytes 4194304 | tf_op jit(solution)/shard_map/convert_element_type | solution.py:184
  156.3 3.5 %collective-permute-start.40 = (bf16[4,2,128,128]{3,2,1,0:T(8,128)(2,1)S(1)}, bf16[4,2,128,128]{3,2,1,0:T(8,128)(2,1)S(1)}, u32[]{:S(2)}, u32[]{:S(2)}) collective-permute-start(bf16[4,2,128,128]{3,2,1,0:T(8,128)(2,1)S(1)} %get-tuple-element.20), channel_id=1, source_target_pairs={{0,4},{1,5},{2,6},{3,7},{4,8},{5,9},{6,10},{7,11},{8,12},{9,13},{1... | collective-permute-start | bytes 786440 | tf_op jit(solution)/shard_map/ppermute | solution.py:105
  159.9 4.6 %collective-permute-start.33 = (bf16[4,2,128,128]{3,2,1,0:T(8,128)(2,1)S(1)}, bf16[4,2,128,128]{3,2,1,0:T(8,128)(2,1)S(1)}, u32[]{:S(2)}, u32[]{:S(2)}) collective-permute-start(bf16[4,2,128,128]{3,2,1,0:T(8,128)(2,1)S(1)} %get-tuple-element.24), channel_id=1, source_target_pairs={{0,4},{1,5},{2,6},{3,7},{4,8},{5,9},{6,10},{7,11},{8,12},{9,13},{1... | collective-permute-start | bytes 786440 | tf_op jit(solution)/shard_map/ppermute | solution.py:105
  169.2 5.8 %collective-permute-done.28 = bf16[128,4096]{1,0:T(8,128)(2,1)S(1)} collective-permute-done((bf16[128,4096]{1,0:T(8,128)(2,1)}, bf16[128,4096]{1,0:T(8,128)(2,1)S(1)}, u32[]{:S(2)}, u32[]{:S(2)}) %collective-permute-start.28) | collective-permute-done | bytes 1048608 | tf_op jit(solution)/shard_map/ppermute | solution.py:105
  (126 shorter events, 59.8 us)
Async XLA Ops:
  0.6 11.9 %collective-permute-start.4 = (bf16[4,2,128,128]{3,2,1,0:T(8,128)(2,1)}, bf16[4,2,128,128]{3,2,1,0:T(8,128)(2,1)S(1)}, u32[]{:S(2)}, u32[]{:S(2)}) collective-permute-start(bf16[4,2,128,128]{3,2,1,0:T(8,128)(2,1)} %refs_4_.1), channel_id=1, source_target_pairs={{0,4},{1,5},{2,6},{3,7},{4,8},{5,9},{6,10},{7,11},{8,12},{9,13},{1... | collective-permute-start | bytes 786440 | tf_op jit(solution)/shard_map/ppermute | solution.py:105
  5.6 11.5 %collective-permute-start.5 = (bf16[4,2,128,128]{3,2,1,0:T(8,128)(2,1)}, bf16[4,2,128,128]{3,2,1,0:T(8,128)(2,1)S(1)}, u32[]{:S(2)}, u32[]{:S(2)}) collective-permute-start(bf16[4,2,128,128]{3,2,1,0:T(8,128)(2,1)} %refs_5_.1), channel_id=1, source_target_pairs={{0,4},{1,5},{2,6},{3,7},{4,8},{5,9},{6,10},{7,11},{8,12},{9,13},{1... | collective-permute-start | bytes 786440 | tf_op jit(solution)/shard_map/ppermute | solution.py:105
  9.1 12.3 %collective-permute-start.16 = (bf16[4,2,128,128]{3,2,1,0:T(8,128)(2,1)}, bf16[4,2,128,128]{3,2,1,0:T(8,128)(2,1)S(1)}, u32[]{:S(2)}, u32[]{:S(2)}) collective-permute-start(bf16[4,2,128,128]{3,2,1,0:T(8,128)(2,1)} %refs_4_.1), channel_id=1, source_target_pairs={{4,0},{5,1},{6,2},{7,3},{8,4},{9,5},{10,6},{11,7},{12,8},{13,9},{1... | collective-permute-start | bytes 786440 | tf_op jit(solution)/shard_map/ppermute | solution.py:105
  10.4 14.5 %collective-permute-start.17 = (bf16[4,2,128,128]{3,2,1,0:T(8,128)(2,1)}, bf16[4,2,128,128]{3,2,1,0:T(8,128)(2,1)S(1)}, u32[]{:S(2)}, u32[]{:S(2)}) collective-permute-start(bf16[4,2,128,128]{3,2,1,0:T(8,128)(2,1)} %refs_5_.1), channel_id=1, source_target_pairs={{4,0},{5,1},{6,2},{7,3},{8,4},{9,5},{10,6},{11,7},{12,8},{13,9},{1... | collective-permute-start | bytes 786440 | tf_op jit(solution)/shard_map/ppermute | solution.py:105
  11.7 14.5 %collective-permute-start.2 = (bf16[4,2,128,128]{3,2,1,0:T(8,128)(2,1)}, bf16[4,2,128,128]{3,2,1,0:T(8,128)(2,1)S(1)}, u32[]{:S(2)}, u32[]{:S(2)}) collective-permute-start(bf16[4,2,128,128]{3,2,1,0:T(8,128)(2,1)} %refs_4_.1), channel_id=1, source_target_pairs={{0,1},{1,0},{2,3},{3,2},{4,5},{5,4},{6,7},{7,6},{8,9},{9,8},{10,11... | collective-permute-start | bytes 786440 | tf_op jit(solution)/shard_map/ppermute | solution.py:105
  12.6 14.9 %collective-permute-start.3 = (bf16[4,2,128,128]{3,2,1,0:T(8,128)(2,1)}, bf16[4,2,128,128]{3,2,1,0:T(8,128)(2,1)S(1)}, u32[]{:S(2)}, u32[]{:S(2)}) collective-permute-start(bf16[4,2,128,128]{3,2,1,0:T(8,128)(2,1)} %refs_5_.1), channel_id=1, source_target_pairs={{0,1},{1,0},{2,3},{3,2},{4,5},{5,4},{6,7},{7,6},{8,9},{9,8},{10,11... | collective-permute-start | bytes 786440 | tf_op jit(solution)/shard_map/ppermute | solution.py:105
  17.0 12.4 %collective-permute-start.8 = (bf16[4,2,128,128]{3,2,1,0:T(8,128)(2,1)S(1)}, bf16[4,2,128,128]{3,2,1,0:T(8,128)(2,1)S(1)}, u32[]{:S(2)}, u32[]{:S(2)}) collective-permute-start(bf16[4,2,128,128]{3,2,1,0:T(8,128)(2,1)S(1)} %collective-permute-done.4.refs_8_), channel_id=1, source_target_pairs={{0,4},{1,5},{2,6},{3,7},{4,8},{5,9},{6,10},{7,11},{8,12},{9,13},{1... | collective-permute-start | bytes 786440 | tf_op jit(solution)/shard_map/ppermute | solution.py:105
  26.2 12.8 %collective-permute-start.21 = (bf16[4,2,128,128]{3,2,1,0:T(8,128)(2,1)S(1)}, bf16[4,2,128,128]{3,2,1,0:T(8,128)(2,1)S(1)}, u32[]{:S(2)}, u32[]{:S(2)}) collective-permute-start(bf16[4,2,128,128]{3,2,1,0:T(8,128)(2,1)S(1)} %collective-permute-done.17.refs_21_), channel_id=1, source_target_pairs={{4,0},{5,1},{6,2},{7,3},{8,4},{9,5},{10,6},{11,7},{12,8},{13,9},{1... | collective-permute-start | bytes 786440 | tf_op jit(solution)/shard_map/ppermute | solution.py:105
  27.5 15.0 %collective-permute-start.18 = (bf16[4,2,128,128]{3,2,1,0:T(8,128)(2,1)S(1)}, bf16[4,2,128,128]{3,2,1,0:T(8,128)(2,1)S(1)}, u32[]{:S(2)}, u32[]{:S(2)}) collective-permute-start(bf16[4,2,128,128]{3,2,1,0:T(8,128)(2,1)S(1)} %collective-permute-done.16.refs_20_), channel_id=1, source_target_pairs={{0,1},{1,0},{2,3},{3,2},{4,5},{5,4},{6,7},{7,6},{8,9},{9,8},{10,11... | collective-permute-start | bytes 786440 | tf_op jit(solution)/shard_map/ppermute | solution.py:105
  29.4 16.7 %collective-permute-start.19 = (bf16[4,2,128,128]{3,2,1,0:T(8,128)(2,1)S(1)}, bf16[4,2,128,128]{3,2,1,0:T(8,128)(2,1)S(1)}, u32[]{:S(2)}, u32[]{:S(2)}) collective-permute-start(bf16[4,2,128,128]{3,2,1,0:T(8,128)(2,1)S(1)} %collective-permute-done.17.refs_21_), channel_id=1, source_target_pairs={{0,1},{1,0},{2,3},{3,2},{4,5},{5,4},{6,7},{7,6},{8,9},{9,8},{10,11... | collective-permute-start | bytes 786440 | tf_op jit(solution)/shard_map/ppermute | solution.py:105
  31.9 15.5 %collective-permute-start.6 = (bf16[4,2,128,128]{3,2,1,0:T(8,128)(2,1)S(1)}, bf16[4,2,128,128]{3,2,1,0:T(8,128)(2,1)S(1)}, u32[]{:S(2)}, u32[]{:S(2)}) collective-permute-start(bf16[4,2,128,128]{3,2,1,0:T(8,128)(2,1)S(1)} %collective-permute-done.4.refs_8_), channel_id=1, source_target_pairs={{4,5},{5,4},{6,7},{7,6},{8,9},{9,8},{10,11},{11,10},{12,13},{13,12... | collective-permute-start | bytes 786440 | tf_op jit(solution)/shard_map/ppermute | solution.py:105
  36.0 13.0 %collective-permute-start.7 = (bf16[4,2,128,128]{3,2,1,0:T(8,128)(2,1)S(1)}, bf16[4,2,128,128]{3,2,1,0:T(8,128)(2,1)S(1)}, u32[]{:S(2)}, u32[]{:S(2)}) collective-permute-start(bf16[4,2,128,128]{3,2,1,0:T(8,128)(2,1)S(1)} %collective-permute-done.5.refs_9_), channel_id=1, source_target_pairs={{4,5},{5,4},{6,7},{7,6},{8,9},{9,8},{10,11},{11,10},{12,13},{13,12... | collective-permute-start | bytes 786440 | tf_op jit(solution)/shard_map/ppermute | solution.py:105
  46.1 11.2 %collective-permute-start.24 = (bf16[4,2,128,128]{3,2,1,0:T(8,128)(2,1)S(1)}, bf16[4,2,128,128]{3,2,1,0:T(8,128)(2,1)}, u32[]{:S(2)}, u32[]{:S(2)}) collective-permute-start(bf16[4,2,128,128]{3,2,1,0:T(8,128)(2,1)S(1)} %collective-permute-done.20.refs_24_), channel_id=1, source_target_pairs={{4,0},{5,1},{6,2},{7,3},{8,4},{9,5},{10,6},{11,7},{12,8},{13,9},{1... | collective-permute-start | bytes 786440 | tf_op jit(solution)/shard_map/ppermute | solution.py:105
  47.4 26.6 %collective-permute-start = (bf16[128,4096]{1,0:T(8,128)(2,1)}, bf16[128,4096]{1,0:T(8,128)(2,1)S(1)}, u32[]{:S(2)}, u32[]{:S(2)}) collective-permute-start(bf16[128,4096]{1,0:T(8,128)(2,1)} %refs_0_.1), channel_id=1, source_target_pairs={{0,2},{1,3},{2,0},{3,1},{4,6},{5,7},{6,4},{7,5},{8,10},{9,11},{10,... | collective-permute-start | bytes 3145736 | tf_op jit(solution)/shard_map/ppermute | solution.py:105
  49.0 45.7 %collective-permute-start.1 = (bf16[128,4096]{1,0:T(8,128)(2,1)}, bf16[128,4096]{1,0:T(8,128)(2,1)S(1)}, u32[]{:S(2)}, u32[]{:S(2)}) collective-permute-start(bf16[128,4096]{1,0:T(8,128)(2,1)} %refs_2_.1), channel_id=1, source_target_pairs={{0,2},{1,3},{2,0},{3,1},{4,6},{5,7},{6,4},{7,5},{8,10},{9,11},{10,... | collective-permute-start | bytes 3145736 | tf_op jit(solution)/shard_map/ppermute | solution.py:105
  49.6 11.8 %collective-permute-start.25 = (bf16[4,2,128,128]{3,2,1,0:T(8,128)(2,1)S(1)}, bf16[4,2,128,128]{3,2,1,0:T(8,128)(2,1)}, u32[]{:S(2)}, u32[]{:S(2)}) collective-permute-start(bf16[4,2,128,128]{3,2,1,0:T(8,128)(2,1)S(1)} %collective-permute-done.21.refs_25_), channel_id=1, source_target_pairs={{4,0},{5,1},{6,2},{7,3},{8,4},{9,5},{10,6},{11,7},{12,8},{13,9},{1... | collective-permute-start | bytes 786440 | tf_op jit(solution)/shard_map/ppermute | solution.py:105
  127.3 26.4 %collective-permute-start.29 = (bf16[128,4096]{1,0:T(8,128)(2,1)}, bf16[128,4096]{1,0:T(8,128)(2,1)}, u32[]{:S(2)}, u32[]{:S(2)}) collective-permute-start(bf16[128,4096]{1,0:T(8,128)(2,1)} %get-tuple-element.15), channel_id=1, source_target_pairs={{0,2},{1,3},{2,0},{3,1},{4,6},{5,7},{6,4},{7,5},{8,10},{9,11},{10,... | collective-permute-start | bytes 3145736 | tf_op jit(solution)/shard_map/ppermute | solution.py:105
  132.1 13.2 %collective-permute-start.41 = (bf16[4,2,128,128]{3,2,1,0:T(8,128)(2,1)}, bf16[4,2,128,128]{3,2,1,0:T(8,128)(2,1)S(1)}, u32[]{:S(2)}, u32[]{:S(2)}) collective-permute-start(bf16[4,2,128,128]{3,2,1,0:T(8,128)(2,1)} %get-tuple-element.23), channel_id=1, source_target_pairs={{12,8},{13,9},{14,10},{15,11},{28,24},{29,25},{30,26},{31,27}} | collective-permute-start | bytes 786440 | tf_op jit(solution)/shard_map/ppermute | solution.py:105
  135.1 11.8 %collective-permute-start.39 = (bf16[4,2,128,128]{3,2,1,0:T(8,128)(2,1)S(1)}, bf16[4,2,128,128]{3,2,1,0:T(8,128)(2,1)S(1)}, u32[]{:S(2)}, u32[]{:S(2)}) collective-permute-start(bf16[4,2,128,128]{3,2,1,0:T(8,128)(2,1)S(1)} %fusion.2), channel_id=1, source_target_pairs={{0,4},{1,5},{2,6},{3,7},{4,8},{5,9},{6,10},{7,11},{16,20},{17,21},... | collective-permute-start | bytes 786440 | tf_op jit(solution)/shard_map/ppermute | solution.py:105
  145.4 29.6 %collective-permute-start.28 = (bf16[128,4096]{1,0:T(8,128)(2,1)}, bf16[128,4096]{1,0:T(8,128)(2,1)S(1)}, u32[]{:S(2)}, u32[]{:S(2)}) collective-permute-start(bf16[128,4096]{1,0:T(8,128)(2,1)} %get-tuple-element.13), channel_id=1, source_target_pairs={{0,2},{1,3},{2,0},{3,1},{4,6},{5,7},{6,4},{7,5},{8,10},{9,11},{10,... | collective-permute-start | bytes 3145736 | tf_op jit(solution)/shard_map/ppermute | solution.py:105
  148.5 16.0 %collective-permute-start.42 = (bf16[4,2,128,128]{3,2,1,0:T(8,128)(2,1)S(1)}, bf16[4,2,128,128]{3,2,1,0:T(8,128)(2,1)S(1)}, u32[]{:S(2)}, u32[]{:S(2)}) collective-permute-start(bf16[4,2,128,128]{3,2,1,0:T(8,128)(2,1)S(1)} %get-tuple-element.21), channel_id=1, source_target_pairs={{8,4},{9,5},{10,6},{11,7},{12,8},{13,9},{14,10},{15,11},{24,20},{2... | collective-permute-start | bytes 786440 | tf_op jit(solution)/shard_map/ppermute | solution.py:105
  151.5 15.3 %collective-permute-start.35 = (bf16[4,2,128,128]{3,2,1,0:T(8,128)(2,1)S(1)}, bf16[4,2,128,128]{3,2,1,0:T(8,128)(2,1)S(1)}, u32[]{:S(2)}, u32[]{:S(2)}) collective-permute-start(bf16[4,2,128,128]{3,2,1,0:T(8,128)(2,1)S(1)} %get-tuple-element.25), channel_id=1, source_target_pairs={{8,4},{9,5},{10,6},{11,7},{12,8},{13,9},{14,10},{15,11},{24,20},{2... | collective-permute-start | bytes 786440 | tf_op jit(solution)/shard_map/ppermute | solution.py:105
  156.3 19.8 %collective-permute-start.40 = (bf16[4,2,128,128]{3,2,1,0:T(8,128)(2,1)S(1)}, bf16[4,2,128,128]{3,2,1,0:T(8,128)(2,1)S(1)}, u32[]{:S(2)}, u32[]{:S(2)}) collective-permute-start(bf16[4,2,128,128]{3,2,1,0:T(8,128)(2,1)S(1)} %get-tuple-element.20), channel_id=1, source_target_pairs={{0,4},{1,5},{2,6},{3,7},{4,8},{5,9},{6,10},{7,11},{8,12},{9,13},{1... | collective-permute-start | bytes 786440 | tf_op jit(solution)/shard_map/ppermute | solution.py:105
  159.9 18.1 %collective-permute-start.33 = (bf16[4,2,128,128]{3,2,1,0:T(8,128)(2,1)S(1)}, bf16[4,2,128,128]{3,2,1,0:T(8,128)(2,1)S(1)}, u32[]{:S(2)}, u32[]{:S(2)}) collective-permute-start(bf16[4,2,128,128]{3,2,1,0:T(8,128)(2,1)S(1)} %get-tuple-element.24), channel_id=1, source_target_pairs={{0,4},{1,5},{2,6},{3,7},{4,8},{5,9},{6,10},{7,11},{8,12},{9,13},{1... | collective-permute-start | bytes 786440 | tf_op jit(solution)/shard_map/ppermute | solution.py:105
  (43 other events, 524.8 us)

commit v2 on v0

v2 whole, which is shorter than its diff:
```python
import functools

import jax
import jax.numpy as jnp
from jax import lax
from jax.experimental import pallas as pl
from jax.experimental.pallas import tpu as pltpu
from jax.sharding import PartitionSpec as P

GELU_C = 0.7978845608
F32 = jnp.float32
BF16 = jnp.bfloat16


def dot(a, b, dims):
    return lax.dot_general(a, b, (dims, ((), ())), preferred_element_type=F32)


def column_of(pos, lines, per, r, m):
    owner = lax.rem(pos[0] - r + lines, lines)
    return ((owner * 2 + pos[1]) * 2 + pos[2]) * per + m


def blocks_of(index, column, side):
    return [pl.ds(pl.multiple_of(index[column, k] * side, side), side) for k in range(2)]


def start_rows(parts, buf, sem):
    loads, first = [], 0
    for n, part in enumerate(parts):
        rows = part.shape[0]
        loads.append(pltpu.make_async_copy(part, buf.at[pl.ds(first, rows)], sem.at[n]))
        loads[-1].start()
        first += rows
    return loads


def store_quarters(acc, quarters, rounded, rows, sem):
    stores = []
    for n in (3, 1, 2, 0):
        part = pl.ds(n * rows, rows)
        rounded[part] = acc[part].astype(BF16)
        stores.append(pltpu.make_async_copy(rounded.at[part], quarters[n], sem.at[n]))
        stores[-1].start()
    return stores


def ffn_kernel(lines, per, side, pos, idx_in, idx_out, *refs):
    xs, cs, refs = refs[:4], refs[4:8], refs[8:]
    pieces, refs = refs[:1 + lines], refs[1 + lines:]
    outs, gts, refs = refs[:4], refs[4:8], refs[8:]
    g_own, g_send, refs = refs[0], refs[1:lines], refs[lines:]
    x, ct, w, out_acc, gt_acc, g_v, s_v, x_sem, c_sem, w_sem, o_sem, g_sem = refs
    rows = outs[0].shape[0]
    loads = start_rows(xs, x, x_sem)
    loads += start_rows(cs, ct, c_sem)
    for r in range(1, lines):
        pltpu.make_async_copy(pieces[1 + r], w.at[r], w_sem.at[r]).start()
    pltpu.make_async_copy(pieces[0], w.at[0, 0], w_sem.at[0]).start()
    pltpu.make_async_copy(pieces[1], w.at[0, 1], w_sem.at[0]).start()
    out_acc[...] = jnp.zeros_like(out_acc)
    gt_acc[...] = jnp.zeros_like(gt_acc)
    for load in loads:
        load.wait()

    def line(r, put):
        pltpu.make_async_copy(pieces[0], w.at[r, 0], w_sem.at[r]).wait()
        pltpu.make_async_copy(pieces[1], w.at[r, 1], w_sem.at[r]).wait()
        for m in range(per):
            j = column_of(pos, lines, per, r, m)
            a, b = blocks_of(idx_in, j, side), blocks_of(idx_out, j, side)
            p = jnp.concatenate([x[:, a[0]], x[:, a[1]]], axis=1)
            g = jnp.concatenate([ct[:, b[0]], ct[:, b[1]]], axis=1)
            wi = jnp.concatenate([w[r, 0, m, 0], w[r, 0, m, 1]], axis=0)
            wo = jnp.concatenate([w[r, 1, m, 0], w[r, 1, m, 1]], axis=1)
            h = dot(p, wi, ((1,), (0,)))
            ga = dot(g, wo, ((1,), (1,)))
            h2 = h * h
            s = jnp.tanh(h * (GELU_C + GELU_C * 0.044715 * h2))
            act = (0.5 * h * (1.0 + s)).astype(BF16)
            slope = 0.5 * (1.0 + s) + (0.5 * h) * (1.0 - s * s) * (GELU_C + GELU_C * 3.0 * 0.044715 * h2)
            gp = (ga * slope).astype(BF16)
            po = dot(act, wo, ((1,), (0,)))
            pb = dot(gp, wi, ((1,), (1,)))
            gi = dot(p, gp, ((0,), (0,)))
            go = dot(act, g, ((0,), (0,)))
            for k in range(2):
                out_acc[:, b[k]] += po[:, k * side:(k + 1) * side]
                gt_acc[:, a[k]] += pb[:, k * side:(k + 1) * side]
                put(m, k, gi[k * side:(k + 1) * side], go[:, k * side:(k + 1) * side])

    @pl.loop(1, lines)
    def _(r):
        def put(m, k, gi, go):
            s_v[r - 1, 0, m, k] = gi.astype(BF16)
            s_v[r - 1, 1, m, k] = go.astype(BF16)
        line(r, put)

    stores = [pltpu.make_async_copy(s_v.at[r - 1], g_send[r - 1], g_sem.at[r]) for r in range(1, lines)]
    for store in stores:
        store.start()

    def put(m, k, gi, go):
        g_v[0, m, k] = gi
        g_v[1, m, k] = go
    line(0, put)
    stores.append(pltpu.make_async_copy(g_v, g_own, g_sem.at[0]))
    stores[-1].start()
    stores += store_quarters(out_acc, outs, x, rows, o_sem.at[0])
    stores += store_quarters(gt_acc, gts, ct, rows, o_sem.at[1])
    for store in stores:
        store.wait()


def local(size, tokens, cotangent, w_in, w_out, index_in, index_out):
    rows, width = tokens.shape
    per, _, side, _ = w_in.shape
    lines = size // 4
    me = lax.axis_index("tensor")
    z, y, c = me // 4, (me // 2) % 2, me % 2
    core_swap = [(i, i ^ 1) for i in range(size)]
    y_swap = [(i, i ^ 2) for i in range(size)]

    def pp(v, perm):
        return lax.ppermute(v, "tensor", perm)

    def turn(r):
        return [(i, (i + 4 * r) % size) for i in range(size)]

    def after(v, *done):
        return lax.optimization_barrier((v, *done))[0]

    x_far = pp(tokens, y_swap)
    c_far = pp(cotangent, y_swap)
    both = jnp.stack([w_in, w_out])
    directs = [pp(both, turn(r)) for r in range(1, lines)]
    x_near = pp(after(tokens, *directs[-1:]), core_swap)
    c_near = pp(after(cotangent, *directs[-1:]), core_swap)
    x_diag = pp(after(x_far, *directs), core_swap)
    c_diag = pp(after(c_far, *directs), core_swap)
    operands = (tokens, x_near, x_far, x_diag, cotangent, c_near, c_far, c_diag, w_in, w_out, *directs)

    pos = jnp.stack([z, y, c]).astype(jnp.int32)
    smem = pl.BlockSpec(memory_space=pltpu.SMEM)
    hbm = pl.BlockSpec(memory_space=pl.ANY)
    shape = jax.ShapeDtypeStruct
    packed = (2, per, 2, side, side)
    token_buf = pltpu.VMEM((4 * rows, width), BF16)
    acc_buf = pltpu.VMEM((4 * rows, width), F32)
    dma = pltpu.SemaphoreType.DMA
    res = pl.pallas_call(
        functools.partial(ffn_kernel, lines, per, side),
        out_shape=(shape((rows, width), BF16),) * 8 + (shape(packed, F32),) + (shape(packed, BF16),) * (lines - 1),
        in_specs=[smem] * 3 + [hbm] * len(operands),
        out_specs=(hbm,) * (8 + lines),
        scratch_shapes=[token_buf, token_buf, pltpu.VMEM((lines,) + packed, BF16), acc_buf, acc_buf,
                        pltpu.VMEM(packed, F32), pltpu.VMEM((max(lines - 1, 1),) + packed, BF16),
                        dma((4,)), dma((4,)), dma((lines,)), dma((2, 4)), dma((lines,))],
        compiler_params=pltpu.CompilerParams(vmem_limit_bytes=31 * 1024 * 1024),
        cost_estimate=pl.CostEstimate(flops=24 * rows * lines * per * 2 * side * side * 2,
                                      bytes_accessed=24 << 20, transcendentals=0),
    )(pos, index_in, index_out, *operands)
    outs, gts, g_own, g_send = res[:4], res[4:8], res[8], res[9:]

    def far_sum(parts):
        return (parts[2].astype(F32) + pp(parts[3], core_swap).astype(F32)).astype(BF16)

    out_far, gt_far = far_sum(outs), far_sum(gts)
    out_near, gt_near = pp(outs[1], core_swap), pp(gts[1], core_swap)
    received = [pp(after(g_send[r - 1], out_far, gt_far, out_near, gt_near), turn(-r)) for r in range(1, lines)]
    out_back, gt_back = pp(out_far, y_swap), pp(gt_far, y_swap)
    output = (outs[0].astype(F32) + out_near.astype(F32) + out_back.astype(F32)).astype(BF16)
    total = g_own
    for recv in received:
        total = total + recv.astype(F32)
    grad_tokens = (gts[0].astype(F32) + gt_near.astype(F32) + gt_back.astype(F32)).astype(BF16)
    return output, grad_tokens, total[0], total[1]


def solution(mesh):
    in_specs = (
        P(("groups", "tensor"), None),
        P(("groups", "tensor"), None),
        P("tensor", None, None, None),
        P("tensor", None, None, None),
        P(),
        P(),
    )
    out_specs = (
        P(("groups", "tensor"), None),
        P(("groups", "tensor"), None),
        P(("groups", "tensor"), None, None, None),
        P(("groups", "tensor"), None, None, None),
    )
    fn = functools.partial(local, mesh.shape["tensor"])
    return jax.shard_map(fn, mesh=mesh, in_specs=in_specs, out_specs=out_specs, check_vma=False)
```

time: 338 us -> 139 us (0.41)
  waiting for transfers between devices: 249 us -> 95 us
  matrix products: 42.3 us -> 0 us
  local copies, waits for them, and re-layouts: 30.1 us -> 7.37 us
  Pallas kernels: 0 us -> 15.1 us
  starting transfers between devices: 0.34 us -> 15.2 us
  between operations: 13.9 us -> 0.73 us
  other arithmetic: 1.38 us -> 4.82 us
    reduce_scatter x2 -> x0, waiting for transfers between devices: 179 us -> none  [the longest x1 107 us: local(): lax.psum_scatter(jnp.einsum('tjki,tjo->jkio', left, right, preferred_elem...]
    ppermute x0 -> x18, waiting for transfers between devices: none -> 95 us  [pp(): return lax.ppermute(v, 'tensor', perm)]
    all_gather x2 -> x0, waiting for transfers between devices: 68.9 us -> none  [the longest x1 35.8 us: local(): all_in = lax.all_gather(w_in, 'tensor', axis=0, tiled=True)]
    dot_general x10 -> x0, matrix products: 42.3 us -> none  [the longest x1 7.64 us: local(): jnp.einsum('tjkd,jkod->tjo', cot_picked, all_out, preferred_element_type=...]
    gather x4 -> x0, local copies, waits for them, and re-layouts: 18.8 us -> none  [the longest x2 9.45 us: local(): cot_picked = cotangent.reshape(rows, dblocks, side)[:, index_out]]
    ppermute x0 -> x18, starting transfers between devices: none -> 15.2 us  [pp(): return lax.ppermute(v, 'tensor', perm)]
    pallas_call x0 -> x1, Pallas kernels: none -> 15.1 us  [local(): pl.pallas_call(functools.partial(ffn_kernel, lines, per, side), out_shape...]
    convert_element_type x0 -> x4, other arithmetic: none -> 3.39 us  [the longest x1 1.45 us: local(): (outs[0].astype(F32) + out_near.astype(F32) + out_back.astype(F32)).astyp...]
  transfers between devices with their start and end apart: 4 -> 18, of which waited for: 4 -> 12; matrix products, arithmetic and copies ran while one was open for 21% -> 3% of each run, Pallas kernels for 0% -> 0%
where the time goes in v2:
time: 139 us; the launch traced here: 138 us
  waiting for transfers between devices  95 us (68%)
  starting transfers between devices  15.2 us (11%)
  Pallas kernels  15.1 us (11%)
  local copies, waits for them, and re-layouts  7.37 us (5%)
  other arithmetic  4.82 us (3%)
    ppermute x18, waiting for transfers between devices, pp(): return lax.ppermute(v, 'tensor', perm)  95 us
    ppermute x18, starting transfers between devices, pp(): return lax.ppermute(v, 'tensor', perm)  15.2 us
    pallas_call x1, Pallas kernels, local(): pl.pallas_call(functools.partial(ffn_kernel, lines, per, side), out_shape...  15.1 us
    unnamed x22, local copies, waits for them, and re-layouts  6.32 us
  transfers between devices with their start and end apart: 18, of which 12 were waited for; matrix products, arithmetic and copies ran while one was open for 3% of the time, Pallas kernels for 0%

profile of v2, /device:TPU:0, one launch (start us, length us, event | category | flops | bytes accessed | tf_op | source)
XLA Modules:
  0.0 138.3 jit_solution(17746889071139386877)
XLA Ops:
  0.7 3.0 %collective-permute-start.2 = (bf16[128,4096]{1,0:T(8,128)(2,1)}, bf16[128,4096]{1,0:T(8,128)(2,1)S(1)}, u32[]{:S(2)}, u32[]{:S(2)}) collective-permute-start(bf16[128,4096]{1,0:T(8,128)(2,1)} %refs_0_.1), channel_id=1, source_target_pairs={{0,2},{1,3},{2,0},{3,1},{4,6},{5,7},{6,4},{7,5},{8,10},{9,11},{10,... | collective-permute-start | bytes 3145736 | tf_op jit(solution)/shard_map/ppermute | solution.py:125
  3.8 1.1 pad_maximum_fusion
  4.9 4.1 %collective-permute-start = (bf16[2,4,2,128,128]{4,3,2,1,0:T(8,128)(2,1)S(1)}, bf16[2,4,2,128,128]{4,3,2,1,0:T(8,128)(2,1)S(1)}, u32[]{:S(2)}, u32[]{:S(2)}) collective-permute-start(bf16[2,4,2,128,128]{4,3,2,1,0:T(8,128)(2,1)S(1)} %pad_maximum_fusion), channel_id=1, source_target_pairs={{0,12},{1,13},{2,14},{3,15},{4,0},{5,1},{6,2},{7,3},{8,4},{9,5},{1... | collective-permute-start | bytes 1572872 | tf_op jit(solution)/shard_map/ppermute | solution.py:125
  10.0 11.4 %collective-permute-done.refs_12_ = bf16[2,4,2,128,128]{4,3,2,1,0:T(8,128)(2,1)S(1)} collective-permute-done((bf16[2,4,2,128,128]{4,3,2,1,0:T(8,128)(2,1)S(1)}, bf16[2,4,2,128,128]{4,3,2,1,0:T(8,128)(2,1)S(1)}, u32[]{:S(2)}, u32[]{:S(2)}) %collective-permute-start) | collective-permute-done | bytes 524320 | tf_op jit(solution)/shard_map/ppermute | solution.py:125
  21.4 31.8 %collective-permute-done.4.refs_11_ = bf16[2,4,2,128,128]{4,3,2,1,0:T(8,128)(2,1)S(1)} collective-permute-done((bf16[2,4,2,128,128]{4,3,2,1,0:T(8,128)(2,1)S(1)}, bf16[2,4,2,128,128]{4,3,2,1,0:T(8,128)(2,1)S(1)}, u32[]{:S(2)}, u32[]{:S(2)}) %collective-permute-start.4) | collective-permute-done | bytes 524320 | tf_op jit(solution)/shard_map/ppermute | solution.py:125
  55.6 1.3 collective-permute-done.6.refs_5_
  57.0 1.3 collective-permute-done.5.refs_3_
  58.3 1.5 %collective-permute-done.8.refs_7_ = bf16[128,4096]{1,0:T(8,128)(2,1)} collective-permute-done((bf16[128,4096]{1,0:T(8,128)(2,1)S(1)}, bf16[128,4096]{1,0:T(8,128)(2,1)}, u32[]{:S(2)}, u32[]{:S(2)}) %collective-permute-start.8) | collective-permute-done | bytes 1048608 | tf_op jit(solution)/shard_map/ppermute | solution.py:125
  59.8 1.2 copy-done.2
  61.0 1.2 copy-done.3
  62.2 1.0 copy-done.5
  64.3 15.1 %shard_map.93 = (bf16[128,4096]{1,0:T(8,128)(2,1)S(1)}, bf16[128,4096]{1,0:T(8,128)(2,1)S(1)}, bf16[128,4096]{1,0:T(8,128)(2,1)S(1)}, bf16[128,4096]{1,0:T(8,128...) custom-call(s32[3]{0:T(128)S(1)} %pad_add_fusion.pos, ...), custom_call_target="tpu_custom_call" | custom-call | flops 3221225472 | bytes 25165824 | tf_op jit(solution)/shard_map/pallas_call | solution.py:151
  80.5 1.6 %collective-permute-done.10 = bf16[128,4096]{1,0:T(8,128)(2,1)S(1)} collective-permute-done((bf16[128,4096]{1,0:T(8,128)(2,1)S(1)}, bf16[128,4096]{1,0:T(8,128)(2,1)S(1)}, u32[]{:S(2)}, u32[]{:S(2)}) %collective-permute-start.10) | collective-permute-done | bytes 1048608 | tf_op jit(solution)/shard_map/ppermute | solution.py:125
  82.4 1.2 collective-permute-done.13
  83.9 1.2 collective-permute-done.9
  85.2 1.5 %collective-permute-done.12 = bf16[128,4096]{1,0:T(8,128)(2,1)S(1)} collective-permute-done((bf16[128,4096]{1,0:T(8,128)(2,1)S(1)}, bf16[128,4096]{1,0:T(8,128)(2,1)S(1)}, u32[]{:S(2)}, u32[]{:S(2)}) %collective-permute-start.12) | collective-permute-done | bytes 1048608 | tf_op jit(solution)/shard_map/ppermute | solution.py:125
  86.7 1.3 collective-permute-start.16
  88.0 2.0 %collective-permute-start.17 = (bf16[2,4,2,128,128]{4,3,2,1,0:T(8,128)(2,1)S(1)}, bf16[2,4,2,128,128]{4,3,2,1,0:T(8,128)(2,1)S(1)}, u32[]{:S(2)}, u32[]{:S(2)}) collective-permute-start(bf16[2,4,2,128,128]{4,3,2,1,0:T(8,128)(2,1)S(1)} %get-tuple-element.41), channel_id=1, source_target_pairs={{0,4},{1,5},{2,6},{3,7},{4,8},{5,9},{6,10},{7,11},{8,12},{9,13},{1... | collective-permute-start | bytes 1572872 | tf_op jit(solution)/shard_map/ppermute | solution.py:125
  90.0 1.5 %collective-permute-start.11 = (bf16[128,4096]{1,0:T(8,128)(2,1)S(1)}, bf16[128,4096]{1,0:T(8,128)(2,1)S(1)}, u32[]{:S(2)}, u32[]{:S(2)}) collective-permute-start(bf16[128,4096]{1,0:T(8,128)(2,1)S(1)} %add_convert_fusion.3), channel_id=1, source_target_pairs={{0,2},{1,3},{2,0},{3,1},{4,6},{5,7},{6,4},{7,5},{8,10},{9,11},{10,... | collective-permute-start | bytes 3145736 | tf_op jit(solution)/shard_map/ppermute | solution.py:125
  92.0 9.5 %collective-permute-done.15 = bf16[2,4,2,128,128]{4,3,2,1,0:T(8,128)(2,1)S(1)} collective-permute-done((bf16[2,4,2,128,128]{4,3,2,1,0:T(8,128)(2,1)S(1)}, bf16[2,4,2,128,128]{4,3,2,1,0:T(8,128)(2,1)S(1)}, u32[]{:S(2)}, u32[]{:S(2)}) %collective-permute-start.15) | collective-permute-done | bytes 524320 | tf_op jit(solution)/shard_map/ppermute | solution.py:125
  101.5 32.4 %collective-permute-done.16 = bf16[2,4,2,128,128]{4,3,2,1,0:T(8,128)(2,1)S(1)} collective-permute-done((bf16[2,4,2,128,128]{4,3,2,1,0:T(8,128)(2,1)S(1)}, bf16[2,4,2,128,128]{4,3,2,1,0:T(8,128)(2,1)S(1)}, u32[]{:S(2)}, u32[]{:S(2)}) %collective-permute-start.16) | collective-permute-done | bytes 524320 | tf_op jit(solution)/shard_map/ppermute | solution.py:125
  134.2 1.1 slice_bitcast_fusion
  135.3 1.5 %add_convert_fusion.2 = bf16[128,4096]{1,0:T(8,128)(2,1)} fusion(bf16[128,4096]{1,0:T(8,128)(2,1)S(1)} %collective-permute-done.11, bf16[128,4096]{1,0:T(8,128)(2,1)S(1)} %collective-permute-done.9, bf16[128,4096]{1,0:T(8,128)(2,1)S(1)} %get-tuple-element.27), kind=kLoop, calls=%fused_computation.2 | loop fusion | flops 3145728 | bytes 4194304 | tf_op jit(solution)/shard_map/convert_element_type | solution.py:172
  136.9 1.4 %add_convert_fusion = bf16[128,4096]{1,0:T(8,128)(2,1)} fusion(bf16[128,4096]{1,0:T(8,128)(2,1)S(1)} %collective-permute-done.14, bf16[128,4096]{1,0:T(8,128)(2,1)S(1)} %collective-permute-done.12, bf16[128,4096]{1,0:T(8,128)(2,1)S(1)} %get-tuple-element.31), kind=kLoop, calls=%fused_computation | loop fusion | flops 3145728 | bytes 4194304 | tf_op jit(solution)/shard_map/convert_element_type | solution.py:176
  (43 shorter events, 7.1 us)
Async XLA Ops:
  0.6 59.1 %copy-start = (bf16[4,2,128,128]{3,2,1,0:T(8,128)(2,1)S(1)}, bf16[4,2,128,128]{3,2,1,0:T(8,128)(2,1)}, u32[]{:S(2)}) copy-start(bf16[4,2,128,128]{3,2,1,0:T(8,128)(2,1)} %refs_8_.1) | copy-start | bytes 786436
  0.6 59.1 %copy-start.1 = (bf16[4,2,128,128]{3,2,1,0:T(8,128)(2,1)S(1)}, bf16[4,2,128,128]{3,2,1,0:T(8,128)(2,1)}, u32[]{:S(2)}) copy-start(bf16[4,2,128,128]{3,2,1,0:T(8,128)(2,1)} %refs_9_.1) | copy-start | bytes 786436
  0.7 54.7 %copy-start.8 = (s32[64,2]{0,1:T(2,128)S(1)}, s32[64,2]{0,1:T(2,128)}, u32[]{:S(2)}) copy-start(s32[64,2]{0,1:T(2,128)} %param.10) | copy-start | bytes 1540
  0.7 54.8 %copy-start.9 = (s32[64,2]{0,1:T(2,128)S(1)}, s32[64,2]{0,1:T(2,128)}, u32[]{:S(2)}) copy-start(s32[64,2]{0,1:T(2,128)} %param.11) | copy-start | bytes 1540
  0.7 54.1 %collective-permute-start.2 = (bf16[128,4096]{1,0:T(8,128)(2,1)}, bf16[128,4096]{1,0:T(8,128)(2,1)S(1)}, u32[]{:S(2)}, u32[]{:S(2)}) collective-permute-start(bf16[128,4096]{1,0:T(8,128)(2,1)} %refs_0_.1), channel_id=1, source_target_pairs={{0,2},{1,3},{2,0},{3,1},{4,6},{5,7},{6,4},{7,5},{8,10},{9,11},{10,... | collective-permute-start | bytes 3145736 | tf_op jit(solution)/shard_map/ppermute | solution.py:125
  3.7 51.6 %collective-permute-start.7 = (bf16[128,4096]{1,0:T(8,128)(2,1)}, bf16[128,4096]{1,0:T(8,128)(2,1)S(1)}, u32[]{:S(2)}, u32[]{:S(2)}) collective-permute-start(bf16[128,4096]{1,0:T(8,128)(2,1)} %refs_4_.1), channel_id=1, source_target_pairs={{0,2},{1,3},{2,0},{3,1},{4,6},{5,7},{6,4},{7,5},{8,10},{9,11},{10,... | collective-permute-start | bytes 3145736 | tf_op jit(solution)/shard_map/ppermute | solution.py:125
  4.9 16.5 %collective-permute-start = (bf16[2,4,2,128,128]{4,3,2,1,0:T(8,128)(2,1)S(1)}, bf16[2,4,2,128,128]{4,3,2,1,0:T(8,128)(2,1)S(1)}, u32[]{:S(2)}, u32[]{:S(2)}) collective-permute-start(bf16[2,4,2,128,128]{4,3,2,1,0:T(8,128)(2,1)S(1)} %pad_maximum_fusion), channel_id=1, source_target_pairs={{0,12},{1,13},{2,14},{3,15},{4,0},{5,1},{6,2},{7,3},{8,4},{9,5},{1... | collective-permute-start | bytes 1572872 | tf_op jit(solution)/shard_map/ppermute | solution.py:125
  8.9 44.2 %collective-permute-start.4 = (bf16[2,4,2,128,128]{4,3,2,1,0:T(8,128)(2,1)S(1)}, bf16[2,4,2,128,128]{4,3,2,1,0:T(8,128)(2,1)S(1)}, u32[]{:S(2)}, u32[]{:S(2)}) collective-permute-start(bf16[2,4,2,128,128]{4,3,2,1,0:T(8,128)(2,1)S(1)} %pad_maximum_fusion), channel_id=1, source_target_pairs={{0,8},{1,9},{2,10},{3,11},{4,12},{5,13},{6,14},{7,15},{8,0},{9,1},... | collective-permute-start | bytes 1572872 | tf_op jit(solution)/shard_map/ppermute | solution.py:125
  8.9 45.0 %collective-permute-start.3 = (bf16[2,4,2,128,128]{4,3,2,1,0:T(8,128)(2,1)S(1)}, bf16[2,4,2,128,128]{4,3,2,1,0:T(8,128)(2,1)S(1)}, u32[]{:S(2)}, u32[]{:S(2)}) collective-permute-start(bf16[2,4,2,128,128]{4,3,2,1,0:T(8,128)(2,1)S(1)} %pad_maximum_fusion), channel_id=1, source_target_pairs={{0,4},{1,5},{2,6},{3,7},{4,8},{5,9},{6,10},{7,11},{8,12},{9,13},{1... | collective-permute-start | bytes 1572872 | tf_op jit(solution)/shard_map/ppermute | solution.py:125
  21.4 34.2 %collective-permute-start.1 = (bf16[128,4096]{1,0:T(8,128)(2,1)}, bf16[128,4096]{1,0:T(8,128)(2,1)}, u32[]{:S(2)}, u32[]{:S(2)}) collective-permute-start(bf16[128,4096]{1,0:T(8,128)(2,1)} %refs_0_.1), channel_id=1, source_target_pairs={{0,1},{1,0},{2,3},{3,2},{4,5},{5,4},{6,7},{7,6},{8,9},{9,8},{10,11... | collective-permute-start | bytes 3145736 | tf_op jit(solution)/shard_map/ppermute | solution.py:125
  54.0 3.0 %collective-permute-start.6 = (bf16[128,4096]{1,0:T(8,128)(2,1)}, bf16[128,4096]{1,0:T(8,128)(2,1)}, u32[]{:S(2)}, u32[]{:S(2)}) collective-permute-start(bf16[128,4096]{1,0:T(8,128)(2,1)} %refs_4_.1), channel_id=1, source_target_pairs={{0,1},{1,0},{2,3},{3,2},{4,5},{5,4},{6,7},{7,6},{8,9},{9,8},{10,11... | collective-permute-start | bytes 3145736 | tf_op jit(solution)/shard_map/ppermute | solution.py:125
  54.8 3.5 %collective-permute-start.5 = (bf16[128,4096]{1,0:T(8,128)(2,1)S(1)}, bf16[128,4096]{1,0:T(8,128)(2,1)}, u32[]{:S(2)}, u32[]{:S(2)}) collective-permute-start(bf16[128,4096]{1,0:T(8,128)(2,1)S(1)} %collective-permute-done.2.refs_2_), channel_id=1, source_target_pairs={{0,1},{1,0},{2,3},{3,2},{4,5},{5,4},{6,7},{7,6},{8,9},{9,8},{10,11... | collective-permute-start | bytes 3145736 | tf_op jit(solution)/shard_map/ppermute | solution.py:125
  55.3 4.5 %collective-permute-start.8 = (bf16[128,4096]{1,0:T(8,128)(2,1)S(1)}, bf16[128,4096]{1,0:T(8,128)(2,1)}, u32[]{:S(2)}, u32[]{:S(2)}) collective-permute-start(bf16[128,4096]{1,0:T(8,128)(2,1)S(1)} %collective-permute-done.7.refs_6_), channel_id=1, source_target_pairs={{0,1},{1,0},{2,3},{3,2},{4,5},{5,4},{6,7},{7,6},{8,9},{9,8},{10,11... | collective-permute-start | bytes 3145736 | tf_op jit(solution)/shard_map/ppermute | solution.py:125
  59.8 1.2 copy-start.2
  61.0 1.2 copy-start.3
  79.4 2.7 %collective-permute-start.10 = (bf16[128,4096]{1,0:T(8,128)(2,1)S(1)}, bf16[128,4096]{1,0:T(8,128)(2,1)S(1)}, u32[]{:S(2)}, u32[]{:S(2)}) collective-permute-start(bf16[128,4096]{1,0:T(8,128)(2,1)S(1)} %get-tuple-element.30), channel_id=1, source_target_pairs={{0,1},{1,0},{2,3},{3,2},{4,5},{5,4},{6,7},{7,6},{8,9},{9,8},{10,11... | collective-permute-start | bytes 3145736 | tf_op jit(solution)/shard_map/ppermute | solution.py:125
  79.7 4.0 %collective-permute-start.13 = (bf16[128,4096]{1,0:T(8,128)(2,1)S(1)}, bf16[128,4096]{1,0:T(8,128)(2,1)S(1)}, u32[]{:S(2)}, u32[]{:S(2)}) collective-permute-start(bf16[128,4096]{1,0:T(8,128)(2,1)S(1)} %get-tuple-element.34), channel_id=1, source_target_pairs={{0,1},{1,0},{2,3},{3,2},{4,5},{5,4},{6,7},{7,6},{8,9},{9,8},{10,11... | collective-permute-start | bytes 3145736 | tf_op jit(solution)/shard_map/ppermute | solution.py:125
  80.0 5.1 %collective-permute-start.9 = (bf16[128,4096]{1,0:T(8,128)(2,1)S(1)}, bf16[128,4096]{1,0:T(8,128)(2,1)S(1)}, u32[]{:S(2)}, u32[]{:S(2)}) collective-permute-start(bf16[128,4096]{1,0:T(8,128)(2,1)S(1)} %get-tuple-element.28), channel_id=1, source_target_pairs={{0,1},{1,0},{2,3},{3,2},{4,5},{5,4},{6,7},{7,6},{8,9},{9,8},{10,11... | collective-permute-start | bytes 3145736 | tf_op jit(solution)/shard_map/ppermute | solution.py:125
  80.2 6.5 %collective-permute-start.12 = (bf16[128,4096]{1,0:T(8,128)(2,1)S(1)}, bf16[128,4096]{1,0:T(8,128)(2,1)S(1)}, u32[]{:S(2)}, u32[]{:S(2)}) collective-permute-start(bf16[128,4096]{1,0:T(8,128)(2,1)S(1)} %get-tuple-element.32), channel_id=1, source_target_pairs={{0,1},{1,0},{2,3},{3,2},{4,5},{5,4},{6,7},{7,6},{8,9},{9,8},{10,11... | collective-permute-start | bytes 3145736 | tf_op jit(solution)/shard_map/ppermute | solution.py:125
  86.7 14.9 %collective-permute-start.15 = (bf16[2,4,2,128,128]{4,3,2,1,0:T(8,128)(2,1)S(1)}, bf16[2,4,2,128,128]{4,3,2,1,0:T(8,128)(2,1)S(1)}, u32[]{:S(2)}, u32[]{:S(2)}) collective-permute-start(bf16[2,4,2,128,128]{4,3,2,1,0:T(8,128)(2,1)S(1)} %get-tuple-element.37), channel_id=1, source_target_pairs={{0,12},{1,13},{2,14},{3,15},{4,0},{5,1},{6,2},{7,3},{8,4},{9,5},{1... | collective-permute-start | bytes 1572872 | tf_op jit(solution)/shard_map/ppermute | solution.py:125
  86.7 47.3 %collective-permute-start.16 = (bf16[2,4,2,128,128]{4,3,2,1,0:T(8,128)(2,1)S(1)}, bf16[2,4,2,128,128]{4,3,2,1,0:T(8,128)(2,1)S(1)}, u32[]{:S(2)}, u32[]{:S(2)}) collective-permute-start(bf16[2,4,2,128,128]{4,3,2,1,0:T(8,128)(2,1)S(1)} %get-tuple-element.39), channel_id=1, source_target_pairs={{0,8},{1,9},{2,10},{3,11},{4,12},{5,13},{6,14},{7,15},{8,0},{9,1},... | collective-permute-start | bytes 1572872 | tf_op jit(solution)/shard_map/ppermute | solution.py:125
  88.0 46.0 %collective-permute-start.17 = (bf16[2,4,2,128,128]{4,3,2,1,0:T(8,128)(2,1)S(1)}, bf16[2,4,2,128,128]{4,3,2,1,0:T(8,128)(2,1)S(1)}, u32[]{:S(2)}, u32[]{:S(2)}) collective-permute-start(bf16[2,4,2,128,128]{4,3,2,1,0:T(8,128)(2,1)S(1)} %get-tuple-element.41), channel_id=1, source_target_pairs={{0,4},{1,5},{2,6},{3,7},{4,8},{5,9},{6,10},{7,11},{8,12},{9,13},{1... | collective-permute-start | bytes 1572872 | tf_op jit(solution)/shard_map/ppermute | solution.py:125
  90.0 45.3 %collective-permute-start.11 = (bf16[128,4096]{1,0:T(8,128)(2,1)S(1)}, bf16[128,4096]{1,0:T(8,128)(2,1)S(1)}, u32[]{:S(2)}, u32[]{:S(2)}) collective-permute-start(bf16[128,4096]{1,0:T(8,128)(2,1)S(1)} %add_convert_fusion.3), channel_id=1, source_target_pairs={{0,2},{1,3},{2,0},{3,1},{4,6},{5,7},{6,4},{7,5},{8,10},{9,11},{10,... | collective-permute-start | bytes 3145736 | tf_op jit(solution)/shard_map/ppermute | solution.py:125
  91.5 45.3 %collective-permute-start.14 = (bf16[128,4096]{1,0:T(8,128)(2,1)S(1)}, bf16[128,4096]{1,0:T(8,128)(2,1)S(1)}, u32[]{:S(2)}, u32[]{:S(2)}) collective-permute-start(bf16[128,4096]{1,0:T(8,128)(2,1)S(1)} %add_convert_fusion.1), channel_id=1, source_target_pairs={{0,2},{1,3},{2,0},{3,1},{4,6},{5,7},{6,4},{7,5},{8,10},{9,11},{10,... | collective-permute-start | bytes 3145736 | tf_op jit(solution)/shard_map/ppermute | solution.py:125
  (4 other events, 3.7 us)

commit v3 on v2

--- a/solution.py
+++ b/solution.py
@@ -16,13 +16,15 @@
     return lax.dot_general(a, b, (dims, ((), ())), preferred_element_type=F32)
 
 
-def column_of(pos, lines, per, r, m):
-    owner = lax.rem(pos[0] - r + lines, lines)
-    return ((owner * 2 + pos[1]) * 2 + pos[2]) * per + m
+def blocks_of(scalars, lines, per, side, r, m):
+    owner = lax.rem(scalars[0] - r + lines, lines)
+    first = 3 + 2 * (((owner * 2 + scalars[1]) * 2 + scalars[2]) * per + m)
+    count = 8 * lines * per
 
+    def block(at):
+        return pl.ds(pl.multiple_of(scalars[at] * side, side), side)
 
-def blocks_of(index, column, side):
-    return [pl.ds(pl.multiple_of(index[column, k] * side, side), side) for k in range(2)]
+    return [block(first), block(first + 1)], [block(first + count), block(first + count + 1)]
 
 
 def start_rows(parts, buf, sem):
@@ -45,30 +47,26 @@
     return stores
 
 
-def ffn_kernel(lines, per, side, pos, idx_in, idx_out, *refs):
+def ffn_kernel(lines, per, side, scalars, *refs):
     xs, cs, refs = refs[:4], refs[4:8], refs[8:]
-    pieces, refs = refs[:1 + lines], refs[1 + lines:]
-    outs, gts, refs = refs[:4], refs[4:8], refs[8:]
+    pieces, sums, refs = refs[:lines], refs[lines:lines + 4], refs[lines + 4:]
+    outs, gts = [part.at[0] for part in sums], [part.at[1] for part in sums]
     g_own, g_send, refs = refs[0], refs[1:lines], refs[lines:]
     x, ct, w, out_acc, gt_acc, g_v, s_v, x_sem, c_sem, w_sem, o_sem, g_sem = refs
     rows = outs[0].shape[0]
     loads = start_rows(xs, x, x_sem)
     loads += start_rows(cs, ct, c_sem)
-    for r in range(1, lines):
-        pltpu.make_async_copy(pieces[1 + r], w.at[r], w_sem.at[r]).start()
-    pltpu.make_async_copy(pieces[0], w.at[0, 0], w_sem.at[0]).start()
-    pltpu.make_async_copy(pieces[1], w.at[0, 1], w_sem.at[0]).start()
+    for r in [*range(1, lines), 0]:
+        pltpu.make_async_copy(pieces[r], w.at[r], w_sem.at[r]).start()
     out_acc[...] = jnp.zeros_like(out_acc)
     gt_acc[...] = jnp.zeros_like(gt_acc)
     for load in loads:
         load.wait()
 
     def line(r, put):
-        pltpu.make_async_copy(pieces[0], w.at[r, 0], w_sem.at[r]).wait()
-        pltpu.make_async_copy(pieces[1], w.at[r, 1], w_sem.at[r]).wait()
+        pltpu.make_async_copy(pieces[0], w.at[r], w_sem.at[r]).wait()
         for m in range(per):
-            j = column_of(pos, lines, per, r, m)
-            a, b = blocks_of(idx_in, j, side), blocks_of(idx_out, j, side)
+            a, b = blocks_of(scalars, lines, per, side, r, m)
             p = jnp.concatenate([x[:, a[0]], x[:, a[1]]], axis=1)
             g = jnp.concatenate([ct[:, b[0]], ct[:, b[1]]], axis=1)
             wi = jnp.concatenate([w[r, 0, m, 0], w[r, 0, m, 1]], axis=0)
@@ -134,15 +132,17 @@
     c_far = pp(cotangent, y_swap)
     both = jnp.stack([w_in, w_out])
     directs = [pp(both, turn(r)) for r in range(1, lines)]
-    x_near = pp(after(tokens, *directs[-1:]), core_swap)
-    c_near = pp(after(cotangent, *directs[-1:]), core_swap)
-    x_diag = pp(after(x_far, *directs), core_swap)
+    scalars = jnp.concatenate([jnp.stack([z, y, c]), index_in.reshape(-1), index_out.reshape(-1)]).astype(jnp.int32)
+    x_own, scalars, _ = lax.optimization_barrier((tokens, scalars, directs[-1]))
+    c_own, _ = lax.optimization_barrier((cotangent, directs[0]))
+    x_near = pp(x_own, core_swap)
+    c_near = pp(c_own, core_swap)
+    x_diag = pp(after(x_far, *directs[:1]), core_swap)
     c_diag = pp(after(c_far, *directs), core_swap)
-    operands = (tokens, x_near, x_far, x_diag, cotangent, c_near, c_far, c_diag, w_in, w_out, *directs)
+    operands = (x_own, x_near, x_far, x_diag, c_own, c_near, c_far, c_diag, both, *directs)
 
-    pos = jnp.stack([z, y, c]).astype(jnp.int32)
     smem = pl.BlockSpec(memory_space=pltpu.SMEM)
-    hbm = pl.BlockSpec(memory_space=pl.ANY)
+    hbm = pl.BlockSpec(memory_space=pltpu.HBM)
     shape = jax.ShapeDtypeStruct
     packed = (2, per, 2, side, side)
     token_buf = pltpu.VMEM((4 * rows, width), BF16)
@@ -150,30 +150,26 @@
     dma = pltpu.SemaphoreType.DMA
     res = pl.pallas_call(
         functools.partial(ffn_kernel, lines, per, side),
-        out_shape=(shape((rows, width), BF16),) * 8 + (shape(packed, F32),) + (shape(packed, BF16),) * (lines - 1),
-        in_specs=[smem] * 3 + [hbm] * len(operands),
-        out_specs=(hbm,) * (8 + lines),
+        out_shape=(shape((2, rows, width), BF16),) * 4 + (shape(packed, F32),) + (shape(packed, BF16),) * (lines - 1),
+        in_specs=[smem] + [hbm] * len(operands),
+        out_specs=(hbm,) * (4 + lines),
         scratch_shapes=[token_buf, token_buf, pltpu.VMEM((lines,) + packed, BF16), acc_buf, acc_buf,
                         pltpu.VMEM(packed, F32), pltpu.VMEM((max(lines - 1, 1),) + packed, BF16),
                         dma((4,)), dma((4,)), dma((lines,)), dma((2, 4)), dma((lines,))],
         compiler_params=pltpu.CompilerParams(vmem_limit_bytes=31 * 1024 * 1024),
         cost_estimate=pl.CostEstimate(flops=24 * rows * lines * per * 2 * side * side * 2,
                                       bytes_accessed=24 << 20, transcendentals=0),
-    )(pos, index_in, index_out, *operands)
-    outs, gts, g_own, g_send = res[:4], res[4:8], res[8], res[9:]
-
-    def far_sum(parts):
-        return (parts[2].astype(F32) + pp(parts[3], core_swap).astype(F32)).astype(BF16)
-
-    out_far, gt_far = far_sum(outs), far_sum(gts)
-    out_near, gt_near = pp(outs[1], core_swap), pp(gts[1], core_swap)
-    received = [pp(after(g_send[r - 1], out_far, gt_far, out_near, gt_near), turn(-r)) for r in range(1, lines)]
-    out_back, gt_back = pp(out_far, y_swap), pp(gt_far, y_swap)
-    output = (outs[0].astype(F32) + out_near.astype(F32) + out_back.astype(F32)).astype(BF16)
+    )(scalars, *operands)
+    own, near, far, diagonal, g_own, *g_send = res
+    far = (far.astype(F32) + pp(diagonal, core_swap).astype(F32)).astype(BF16)
+    received = [pp(after(g, far), turn(-r)) for r, g in enumerate(g_send, 1)]
+    near = pp(after(near, far), core_swap)
+    back = pp(far, y_swap)
+    output, grad_tokens = [(own[n].astype(F32) + near[n].astype(F32) + back[n].astype(F32)).astype(BF16)
+                           for n in range(2)]
     total = g_own
     for recv in received:
         total = total + recv.astype(F32)
-    grad_tokens = (gts[0].astype(F32) + gt_near.astype(F32) + gt_back.astype(F32)).astype(BF16)
     return output, grad_tokens, total[0], total[1]
 
 

time: 139 us -> 129 us (0.928)
  waiting for transfers between devices: 95 us -> 92 us
  starting transfers between devices: 15.2 us -> 12.8 us
  local copies, waits for them, and re-layouts: 7.37 us -> 5.4 us
  Pallas kernels: 15.1 us -> 13.5 us
    ppermute x18 -> x15, waiting for transfers between devices: 95 us -> 92 us  [pp(): return lax.ppermute(v, 'tensor', perm)]
    ppermute x18 -> x15, starting transfers between devices: 15.2 us -> 12.8 us  [pp(): return lax.ppermute(v, 'tensor', perm)]
    unnamed x22 -> x6, local copies, waits for them, and re-layouts: 6.32 us -> 3.99 us
    pallas_call x1, Pallas kernels: 15.1 us -> 13.5 us  [local(): pl.pallas_call(functools.partial(ffn_kernel, lines, per, side), out_shape...]
    convert_element_type x4 -> x2, other arithmetic: 3.39 us -> 3.15 us  [the longest x1 2.36 us: local(): (own[n].astype(F32) + near[n].astype(F32) + back[n].astype(F32)).astype(B...]
  transfers between devices with their start and end apart: 18 -> 15, of which waited for: 12 -> 7; matrix products, arithmetic and copies ran while one was open for 3% -> 3% of each run, Pallas kernels for 0% -> 0%
where the time goes in v3:
time: 129 us
  waiting for transfers between devices  92 us (71%)
  Pallas kernels  13.5 us (10%)
  starting transfers between devices  12.8 us (10%)
  local copies, waits for them, and re-layouts  5.4 us (4%)
  other arithmetic  4.5 us (3%)
    ppermute x15, waiting for transfers between devices, pp(): return lax.ppermute(v, 'tensor', perm)  92 us
    pallas_call x1, Pallas kernels, local(): pl.pallas_call(functools.partial(ffn_kernel, lines, per, side), out_shape...  13.5 us
    ppermute x15, starting transfers between devices, pp(): return lax.ppermute(v, 'tensor', perm)  12.8 us
    unnamed x6, local copies, waits for them, and re-layouts  3.99 us
  transfers between devices with their start and end apart: 15, of which 7 were waited for; matrix products, arithmetic and copies ran while one was open for 3% of the time, Pallas kernels for 0%

profile of v3, /device:TPU:0, one launch (start us, length us, event | category | flops | bytes accessed | tf_op | source)
XLA Modules:
  0.0 128.9 jit_solution(2255083526141968569)
XLA Ops:
  0.6 3.0 %collective-permute-start.2 = (bf16[128,4096]{1,0:T(8,128)(2,1)}, bf16[128,4096]{1,0:T(8,128)(2,1)S(1)}, u32[]{:S(2)}, u32[]{:S(2)}) collective-permute-start(bf16[128,4096]{1,0:T(8,128)(2,1)} %refs_0_), channel_id=1, source_target_pairs={{0,2},{1,3},{2,0},{3,1},{4,6},{5,7},{6,4},{7,5},{8,10},{9,11},{10,... | collective-permute-start | bytes 3145736 | tf_op jit(solution)/shard_map/ppermute | solution.py:123
  3.7 1.1 pad_maximum_fusion.refs_8_
  4.8 2.1 %collective-permute-start.3 = (bf16[2,4,2,128,128]{4,3,2,1,0:T(8,128)(2,1)S(1)}, bf16[2,4,2,128,128]{4,3,2,1,0:T(8,128)(2,1)S(1)}, u32[]{:S(2)}, u32[]{:S(2)}) collective-permute-start(bf16[2,4,2,128,128]{4,3,2,1,0:T(8,128)(2,1)S(1)} %pad_maximum_fusion.refs_8_), channel_id=1, source_target_pairs={{0,4},{1,5},{2,6},{3,7},{4,8},{5,9},{6,10},{7,11},{8,12},{9,13},{1... | collective-permute-start | bytes 1572872 | tf_op jit(solution)/shard_map/ppermute | solution.py:123
  6.9 2.1 %collective-permute-start = (bf16[2,4,2,128,128]{4,3,2,1,0:T(8,128)(2,1)S(1)}, bf16[2,4,2,128,128]{4,3,2,1,0:T(8,128)(2,1)}, u32[]{:S(2)}, u32[]{:S(2)}) collective-permute-start(bf16[2,4,2,128,128]{4,3,2,1,0:T(8,128)(2,1)S(1)} %pad_maximum_fusion.refs_8_), channel_id=1, source_target_pairs={{0,12},{1,13},{2,14},{3,15},{4,0},{5,1},{6,2},{7,3},{8,4},{9,5},{1... | collective-permute-start | bytes 1572872 | tf_op jit(solution)/shard_map/ppermute | solution.py:123
  9.0 0.9 collective-permute-start.7
  9.9 0.8 copy.12
  10.8 0.8 copy.13
  11.8 9.9 %collective-permute-done.3.refs_9_ = bf16[2,4,2,128,128]{4,3,2,1,0:T(8,128)(2,1)S(1)} collective-permute-done((bf16[2,4,2,128,128]{4,3,2,1,0:T(8,128)(2,1)S(1)}, bf16[2,4,2,128,128]{4,3,2,1,0:T(8,128)(2,1)S(1)}, u32[]{:S(2)}, u32[]{:S(2)}) %collective-permute-start.3) | collective-permute-done | bytes 524320 | tf_op jit(solution)/shard_map/ppermute | solution.py:123
  21.8 9.3 %collective-permute-done.refs_11_ = bf16[2,4,2,128,128]{4,3,2,1,0:T(8,128)(2,1)} collective-permute-done((bf16[2,4,2,128,128]{4,3,2,1,0:T(8,128)(2,1)S(1)}, bf16[2,4,2,128,128]{4,3,2,1,0:T(8,128)(2,1)}, u32[]{:S(2)}, u32[]{:S(2)}) %collective-permute-start) | collective-permute-done | bytes 524320 | tf_op jit(solution)/shard_map/ppermute | solution.py:123
  31.0 0.5 collective-permute-start.5
  31.6 22.5 %collective-permute-done.7.refs_10_ = bf16[2,4,2,128,128]{4,3,2,1,0:T(8,128)(2,1)} collective-permute-done((bf16[2,4,2,128,128]{4,3,2,1,0:T(8,128)(2,1)S(1)}, bf16[2,4,2,128,128]{4,3,2,1,0:T(8,128)(2,1)}, u32[]{:S(2)}, u32[]{:S(2)}) %collective-permute-start.7) | collective-permute-done | bytes 524320 | tf_op jit(solution)/shard_map/ppermute | solution.py:123
  54.1 2.6 %collective-permute-done.8.refs_7_ = bf16[128,4096]{1,0:T(8,128)(2,1)S(1)} collective-permute-done((bf16[128,4096]{1,0:T(8,128)(2,1)S(1)}, bf16[128,4096]{1,0:T(8,128)(2,1)S(1)}, u32[]{:S(2)}, u32[]{:S(2)}) %collective-permute-start.8) | collective-permute-done | bytes 1048608 | tf_op jit(solution)/shard_map/ppermute | solution.py:123
  56.7 1.2 copy-done
  58.0 1.2 copy-done.1
  59.2 13.5 %shard_map.93 = (bf16[2,128,4096]{2,1,0:T(8,128)(2,1)S(1)}, bf16[2,128,4096]{2,1,0:T(8,128)(2,1)S(1)}, bf16[2,128,4096]{2,1,0:T(8,128)(2,1)S(1)}, bf16[2,128,409...) custom-call(s32[259]{0:T(512)S(1)} %concatenate.3.scalars, ...), custom_call_target="tpu_custom_call" | custom-call | flops 3221225472 | bytes 25165824 | tf_op jit(solution)/shard_map/pallas_call | solution.py:151
  72.9 4.1 %collective-permute-done.9 = bf16[2,128,4096]{2,1,0:T(8,128)(2,1)S(1)} collective-permute-done((bf16[2,128,4096]{2,1,0:T(8,128)(2,1)S(1)}, bf16[2,128,4096]{2,1,0:T(8,128)(2,1)S(1)}, u32[]{:S(2)}, u32[]{:S(2)}) %collective-permute-start.9) | collective-permute-done | bytes 2097184 | tf_op jit(solution)/shard_map/ppermute | solution.py:123
  77.0 0.8 add_convert_fusion
  78.0 1.5 %collective-permute-start.11 = (bf16[2,128,4096]{2,1,0:T(8,128)(2,1)S(1)}, bf16[2,128,4096]{2,1,0:T(8,128)(2,1)S(1)}, u32[]{:S(2)}, u32[]{:S(2)}) collective-permute-start(bf16[2,128,4096]{2,1,0:T(8,128)(2,1)S(1)} %add_convert_fusion), channel_id=1, source_target_pairs={{0,2},{1,3},{2,0},{3,1},{4,6},{5,7},{6,4},{7,5},{8,10},{9,11},{10,... | collective-permute-start | bytes 6291464 | tf_op jit(solution)/shard_map/ppermute | solution.py:123
  79.4 1.6 %collective-permute-start.12 = (bf16[2,4,2,128,128]{4,3,2,1,0:T(8,128)(2,1)S(1)}, bf16[2,4,2,128,128]{4,3,2,1,0:T(8,128)(2,1)S(1)}, u32[]{:S(2)}, u32[]{:S(2)}) collective-permute-start(bf16[2,4,2,128,128]{4,3,2,1,0:T(8,128)(2,1)S(1)} %get-tuple-element.33), channel_id=1, source_target_pairs={{0,12},{1,13},{2,14},{3,15},{4,0},{5,1},{6,2},{7,3},{8,4},{9,5},{1... | collective-permute-start | bytes 1572872 | tf_op jit(solution)/shard_map/ppermute | solution.py:123
  81.1 0.6 collective-permute-start.14
  81.6 13.5 %collective-permute-done.12 = bf16[2,4,2,128,128]{4,3,2,1,0:T(8,128)(2,1)S(1)} collective-permute-done((bf16[2,4,2,128,128]{4,3,2,1,0:T(8,128)(2,1)S(1)}, bf16[2,4,2,128,128]{4,3,2,1,0:T(8,128)(2,1)S(1)}, u32[]{:S(2)}, u32[]{:S(2)}) %collective-permute-start.12) | collective-permute-done | bytes 524320 | tf_op jit(solution)/shard_map/ppermute | solution.py:123
  95.2 30.0 %collective-permute-done.13 = bf16[2,4,2,128,128]{4,3,2,1,0:T(8,128)(2,1)S(1)} collective-permute-done((bf16[2,4,2,128,128]{4,3,2,1,0:T(8,128)(2,1)S(1)}, bf16[2,4,2,128,128]{4,3,2,1,0:T(8,128)(2,1)S(1)}, u32[]{:S(2)}, u32[]{:S(2)}) %collective-permute-start.13) | collective-permute-done | bytes 524320 | tf_op jit(solution)/shard_map/ppermute | solution.py:123
  125.5 1.1 slice_bitcast_fusion
  126.5 2.4 %fusion.1 = (bf16[128,4096]{1,0:T(8,128)(2,1)}, bf16[128,4096]{1,0:T(8,128)(2,1)}) fusion(bf16[2,128,4096]{2,1,0:T(8,128)(2,1)S(1)} %collective-permute-done.11, bf16[2,128,4096]{2,1,0:T(8,128)(2,1)S(1)} %collective-permute-done.10, bf16[2,128,4096]{2,1,0:T(8,128)(2,1)S(1)} %get-tuple-element.26), kind=kLoop, calls=%fused_computation.4 | loop fusion | flops 6291456 | bytes 8388608 | tf_op jit(solution)/shard_map/convert_element_type | solution.py:168
  (21 shorter events, 1.1 us)
Async XLA Ops:
  0.6 30.9 %collective-permute-start.2 = (bf16[128,4096]{1,0:T(8,128)(2,1)}, bf16[128,4096]{1,0:T(8,128)(2,1)S(1)}, u32[]{:S(2)}, u32[]{:S(2)}) collective-permute-start(bf16[128,4096]{1,0:T(8,128)(2,1)} %refs_0_), channel_id=1, source_target_pairs={{0,2},{1,3},{2,0},{3,1},{4,6},{5,7},{6,4},{7,5},{8,10},{9,11},{10,... | collective-permute-start | bytes 3145736 | tf_op jit(solution)/shard_map/ppermute | solution.py:123
  3.7 50.4 %collective-permute-start.6 = (bf16[128,4096]{1,0:T(8,128)(2,1)}, bf16[128,4096]{1,0:T(8,128)(2,1)S(1)}, u32[]{:S(2)}, u32[]{:S(2)}) collective-permute-start(bf16[128,4096]{1,0:T(8,128)(2,1)} %refs_4_), channel_id=1, source_target_pairs={{0,2},{1,3},{2,0},{3,1},{4,6},{5,7},{6,4},{7,5},{8,10},{9,11},{10,... | collective-permute-start | bytes 3145736 | tf_op jit(solution)/shard_map/ppermute | solution.py:123
  4.8 17.0 %collective-permute-start.3 = (bf16[2,4,2,128,128]{4,3,2,1,0:T(8,128)(2,1)S(1)}, bf16[2,4,2,128,128]{4,3,2,1,0:T(8,128)(2,1)S(1)}, u32[]{:S(2)}, u32[]{:S(2)}) collective-permute-start(bf16[2,4,2,128,128]{4,3,2,1,0:T(8,128)(2,1)S(1)} %pad_maximum_fusion.refs_8_), channel_id=1, source_target_pairs={{0,4},{1,5},{2,6},{3,7},{4,8},{5,9},{6,10},{7,11},{8,12},{9,13},{1... | collective-permute-start | bytes 1572872 | tf_op jit(solution)/shard_map/ppermute | solution.py:123
  6.9 24.2 %collective-permute-start = (bf16[2,4,2,128,128]{4,3,2,1,0:T(8,128)(2,1)S(1)}, bf16[2,4,2,128,128]{4,3,2,1,0:T(8,128)(2,1)}, u32[]{:S(2)}, u32[]{:S(2)}) collective-permute-start(bf16[2,4,2,128,128]{4,3,2,1,0:T(8,128)(2,1)S(1)} %pad_maximum_fusion.refs_8_), channel_id=1, source_target_pairs={{0,12},{1,13},{2,14},{3,15},{4,0},{5,1},{6,2},{7,3},{8,4},{9,5},{1... | collective-permute-start | bytes 1572872 | tf_op jit(solution)/shard_map/ppermute | solution.py:123
  9.0 45.1 %collective-permute-start.7 = (bf16[2,4,2,128,128]{4,3,2,1,0:T(8,128)(2,1)S(1)}, bf16[2,4,2,128,128]{4,3,2,1,0:T(8,128)(2,1)}, u32[]{:S(2)}, u32[]{:S(2)}) collective-permute-start(bf16[2,4,2,128,128]{4,3,2,1,0:T(8,128)(2,1)S(1)} %pad_maximum_fusion.refs_8_), channel_id=1, source_target_pairs={{0,8},{1,9},{2,10},{3,11},{4,12},{5,13},{6,14},{7,15},{8,0},{9,1},... | collective-permute-start | bytes 1572872 | tf_op jit(solution)/shard_map/ppermute | solution.py:123
  31.0 23.1 %collective-permute-start.1 = (bf16[128,4096]{1,0:T(8,128)(2,1)}, bf16[128,4096]{1,0:T(8,128)(2,1)S(1)}, u32[]{:S(2)}, u32[]{:S(2)}) collective-permute-start(bf16[128,4096]{1,0:T(8,128)(2,1)} %refs_0_), channel_id=1, source_target_pairs={{0,1},{1,0},{2,3},{3,2},{4,5},{5,4},{6,7},{7,6},{8,9},{9,8},{10,11... | collective-permute-start | bytes 3145736 | tf_op jit(solution)/shard_map/ppermute | solution.py:123
  31.0 23.1 %collective-permute-start.5 = (bf16[128,4096]{1,0:T(8,128)(2,1)}, bf16[128,4096]{1,0:T(8,128)(2,1)S(1)}, u32[]{:S(2)}, u32[]{:S(2)}) collective-permute-start(bf16[128,4096]{1,0:T(8,128)(2,1)} %refs_4_), channel_id=1, source_target_pairs={{0,1},{1,0},{2,3},{3,2},{4,5},{5,4},{6,7},{7,6},{8,9},{9,8},{10,11... | collective-permute-start | bytes 3145736 | tf_op jit(solution)/shard_map/ppermute | solution.py:123
  31.6 22.6 %collective-permute-start.4 = (bf16[128,4096]{1,0:T(8,128)(2,1)S(1)}, bf16[128,4096]{1,0:T(8,128)(2,1)S(1)}, u32[]{:S(2)}, u32[]{:S(2)}) collective-permute-start(bf16[128,4096]{1,0:T(8,128)(2,1)S(1)} %collective-permute-done.2.refs_2_), channel_id=1, source_target_pairs={{0,1},{1,0},{2,3},{3,2},{4,5},{5,4},{6,7},{7,6},{8,9},{9,8},{10,11... | collective-permute-start | bytes 3145736 | tf_op jit(solution)/shard_map/ppermute | solution.py:123
  54.1 2.7 %collective-permute-start.8 = (bf16[128,4096]{1,0:T(8,128)(2,1)S(1)}, bf16[128,4096]{1,0:T(8,128)(2,1)S(1)}, u32[]{:S(2)}, u32[]{:S(2)}) collective-permute-start(bf16[128,4096]{1,0:T(8,128)(2,1)S(1)} %collective-permute-done.6.refs_6_), channel_id=1, source_target_pairs={{0,1},{1,0},{2,3},{3,2},{4,5},{5,4},{6,7},{7,6},{8,9},{9,8},{10,11... | collective-permute-start | bytes 3145736 | tf_op jit(solution)/shard_map/ppermute | solution.py:123
  56.7 1.2 copy-start
  58.0 1.2 copy-start.1
  72.7 4.2 %collective-permute-start.9 = (bf16[2,128,4096]{2,1,0:T(8,128)(2,1)S(1)}, bf16[2,128,4096]{2,1,0:T(8,128)(2,1)S(1)}, u32[]{:S(2)}, u32[]{:S(2)}) collective-permute-start(bf16[2,128,4096]{2,1,0:T(8,128)(2,1)S(1)} %get-tuple-element.29), channel_id=1, source_target_pairs={{0,1},{1,0},{2,3},{3,2},{4,5},{5,4},{6,7},{7,6},{8,9},{9,8},{10,11... | collective-permute-start | bytes 6291464 | tf_op jit(solution)/shard_map/ppermute | solution.py:123
  77.8 48.8 %collective-permute-start.10 = (bf16[2,128,4096]{2,1,0:T(8,128)(2,1)S(1)}, bf16[2,128,4096]{2,1,0:T(8,128)(2,1)S(1)}, u32[]{:S(2)}, u32[]{:S(2)}) collective-permute-start(bf16[2,128,4096]{2,1,0:T(8,128)(2,1)S(1)} %get-tuple-element.30), channel_id=1, source_target_pairs={{0,1},{1,0},{2,3},{3,2},{4,5},{5,4},{6,7},{7,6},{8,9},{9,8},{10,11... | collective-permute-start | bytes 6291464 | tf_op jit(solution)/shard_map/ppermute | solution.py:123
  78.0 48.6 %collective-permute-start.11 = (bf16[2,128,4096]{2,1,0:T(8,128)(2,1)S(1)}, bf16[2,128,4096]{2,1,0:T(8,128)(2,1)S(1)}, u32[]{:S(2)}, u32[]{:S(2)}) collective-permute-start(bf16[2,128,4096]{2,1,0:T(8,128)(2,1)S(1)} %add_convert_fusion), channel_id=1, source_target_pairs={{0,2},{1,3},{2,0},{3,1},{4,6},{5,7},{6,4},{7,5},{8,10},{9,11},{10,... | collective-permute-start | bytes 6291464 | tf_op jit(solution)/shard_map/ppermute | solution.py:123
  79.4 15.7 %collective-permute-start.12 = (bf16[2,4,2,128,128]{4,3,2,1,0:T(8,128)(2,1)S(1)}, bf16[2,4,2,128,128]{4,3,2,1,0:T(8,128)(2,1)S(1)}, u32[]{:S(2)}, u32[]{:S(2)}) collective-permute-start(bf16[2,4,2,128,128]{4,3,2,1,0:T(8,128)(2,1)S(1)} %get-tuple-element.33), channel_id=1, source_target_pairs={{0,12},{1,13},{2,14},{3,15},{4,0},{5,1},{6,2},{7,3},{8,4},{9,5},{1... | collective-permute-start | bytes 1572872 | tf_op jit(solution)/shard_map/ppermute | solution.py:123
  81.1 44.1 %collective-permute-start.13 = (bf16[2,4,2,128,128]{4,3,2,1,0:T(8,128)(2,1)S(1)}, bf16[2,4,2,128,128]{4,3,2,1,0:T(8,128)(2,1)S(1)}, u32[]{:S(2)}, u32[]{:S(2)}) collective-permute-start(bf16[2,4,2,128,128]{4,3,2,1,0:T(8,128)(2,1)S(1)} %get-tuple-element.35), channel_id=1, source_target_pairs={{0,8},{1,9},{2,10},{3,11},{4,12},{5,13},{6,14},{7,15},{8,0},{9,1},... | collective-permute-start | bytes 1572872 | tf_op jit(solution)/shard_map/ppermute | solution.py:123
  81.1 44.1 %collective-permute-start.14 = (bf16[2,4,2,128,128]{4,3,2,1,0:T(8,128)(2,1)S(1)}, bf16[2,4,2,128,128]{4,3,2,1,0:T(8,128)(2,1)S(1)}, u32[]{:S(2)}, u32[]{:S(2)}) collective-permute-start(bf16[2,4,2,128,128]{4,3,2,1,0:T(8,128)(2,1)S(1)} %get-tuple-element.37), channel_id=1, source_target_pairs={{0,4},{1,5},{2,6},{3,7},{4,8},{5,9},{6,10},{7,11},{8,12},{9,13},{1... | collective-permute-start | bytes 1572872 | tf_op jit(solution)/shard_map/ppermute | solution.py:123

commit v4 on v3

v4 whole, which is shorter than its diff:
```python
import functools

import jax
import jax.numpy as jnp
from jax import lax
from jax.experimental import pallas as pl
from jax.experimental.pallas import tpu as pltpu
from jax.sharding import PartitionSpec as P

GELU_C = 0.7978845608
F32 = jnp.float32
BF16 = jnp.bfloat16


def dot(a, b, dims):
    return lax.dot_general(a, b, (dims, ((), ())), preferred_element_type=F32)


def blocks_of(scalars, lines, per, side, r, m):
    owner = lax.rem(scalars[0] - r + lines, lines)
    first = 4 + 2 * (((owner * 2 + scalars[1]) * 2 + scalars[2]) * per + m)
    count = 8 * lines * per

    def block(at):
        return pl.ds(pl.multiple_of(scalars[at] * side, side), side)

    return [block(first), block(first + 1)], [block(first + count), block(first + count + 1)]


def start_rows(parts, buf, sem):
    loads, first = [], 0
    for n, part in enumerate(parts):
        rows = part.shape[0]
        loads.append(pltpu.make_async_copy(part, buf.at[pl.ds(first, rows)], sem.at[n]))
        loads[-1].start()
        first += rows
    return loads


def store_halves(acc, halves, rounded, rows, sem):
    stores = []
    for n in (1, 0):
        part = pl.ds(n * rows, rows)
        rounded[part] = acc[part].astype(BF16)
        stores.append(pltpu.make_async_copy(rounded.at[part], halves[n], sem.at[n]))
        stores[-1].start()
    return stores


def fetch_weights(lines, half, pieces, halves, w, sem):
    for r in range(1, lines):
        if r == lines // 2:
            @pl.when(half == 0)
            def _():
                pltpu.make_async_copy(halves[0], w.at[r, 0], sem.at[r]).start()
                pltpu.make_async_copy(halves[1], w.at[r, 1], sem.at[r]).start()

            @pl.when(half != 0)
            def _():
                pltpu.make_async_copy(halves[1], w.at[r, 0], sem.at[r]).start()
                pltpu.make_async_copy(halves[0], w.at[r, 1], sem.at[r]).start()
        else:
            pltpu.make_async_copy(pieces[r], w.at[r], sem.at[r]).start()
    pltpu.make_async_copy(pieces[0], w.at[0], sem.at[0]).start()


def ffn_kernel(lines, per, side, last, scalars, *refs):
    parts = 4 if last else 2
    xs, cs, refs = refs[:2], refs[2:2 + parts], refs[2 + parts:]
    halves, refs = refs[:2], refs[2:]
    pieces, refs = list(refs[:lines - 1]), refs[lines - 1:]
    pieces.insert(lines // 2, None)
    if last:
        before, sums, g_own = refs[0], refs[1:3], refs[3]
        g_send, refs = refs[4:3 + lines], refs[3 + lines:]
    else:
        sums, g_all, refs = refs[:2], refs[2], refs[3:]
    outs, gts = [part.at[0] for part in sums], [part.at[1] for part in sums]
    x, ct, w, out_acc, gt_acc, g_v, s_v, x_sem, c_sem, w_sem, b_sem, o_sem, g_sem = refs
    rows = xs[0].shape[0]
    loads = start_rows(xs, x, x_sem) + start_rows(cs, ct, c_sem)
    fetch_weights(lines, scalars[3], pieces, halves, w, w_sem)
    if last:
        for r in range(lines):
            pltpu.make_async_copy(before.at[r], g_v.at[r], b_sem.at[r]).start()
    out_acc[...] = jnp.zeros_like(out_acc)
    gt_acc[...] = jnp.zeros_like(gt_acc)
    for load in loads:
        load.wait()

    def line(r, put):
        pltpu.make_async_copy(pieces[0], w.at[r], w_sem.at[r]).wait()
        if last:
            pltpu.make_async_copy(before.at[r], g_v.at[r], b_sem.at[r]).wait()
        for m in range(per):
            a, b = blocks_of(scalars, lines, per, side, r, m)
            p = jnp.concatenate([x[:, a[0]], x[:, a[1]]], axis=1)
            g = jnp.concatenate([ct[:, b[0]], ct[:, b[1]]], axis=1)
            wi = jnp.concatenate([w[r, 0, m, 0], w[r, 0, m, 1]], axis=0)
            wo = jnp.concatenate([w[r, 1, m, 0], w[r, 1, m, 1]], axis=1)
            h = dot(p, wi, ((1,), (0,)))
            ga = dot(g, wo, ((1,), (1,)))
            h2 = h * h
            s = jnp.tanh(h * (GELU_C + GELU_C * 0.044715 * h2))
            act = (0.5 * h * (1.0 + s)).astype(BF16)
            slope = 0.5 * (1.0 + s) + (0.5 * h) * (1.0 - s * s) * (GELU_C + GELU_C * 3.0 * 0.044715 * h2)
            gp = (ga * slope).astype(BF16)
            po = dot(act, wo, ((1,), (0,)))
            pb = dot(gp, wi, ((1,), (1,)))
            gi = dot(p, gp, ((0,), (0,)))
            go = dot(act, g, ((0,), (0,)))
            for k in range(2):
                out_acc[:, b[k]] += po[:, k * side:(k + 1) * side]
                gt_acc[:, a[k]] += pb[:, k * side:(k + 1) * side]
                put(m, k, gi[k * side:(k + 1) * side], go[:, k * side:(k + 1) * side])

    def keep(r):
        def put(m, k, gi, go):
            g_v[r, 0, m, k] = g_v[r, 0, m, k] + gi if last else gi
            g_v[r, 1, m, k] = g_v[r, 1, m, k] + go if last else go
        return put

    def send(r):
        def put(m, k, gi, go):
            s_v[r - 1, 0, m, k] = (g_v[r, 0, m, k] + gi).astype(BF16)
            s_v[r - 1, 1, m, k] = (g_v[r, 1, m, k] + go).astype(BF16)
        return put

    @pl.loop(1, lines)
    def _(r):
        line(r, send(r) if last else keep(r))

    if last:
        stores = [pltpu.make_async_copy(s_v.at[r - 1], g_send[r - 1], g_sem.at[r]) for r in range(1, lines)]
        for store in stores:
            store.start()
    line(0, keep(0))
    if last:
        stores.append(pltpu.make_async_copy(g_v.at[0], g_own, g_sem.at[0]))
    else:
        stores = [pltpu.make_async_copy(g_v, g_all, g_sem.at[0])]
    stores[-1].start()
    stores += store_halves(out_acc, outs, x, rows, o_sem.at[0])
    stores += store_halves(gt_acc, gts, ct, rows, o_sem.at[1])
    for store in stores:
        store.wait()


def local(size, groups, tokens, cotangent, w_in, w_out, index_in, index_out):
    rows, width = tokens.shape
    per, _, side, _ = w_in.shape
    lines = size // 4
    me = lax.axis_index("tensor")
    half = lax.axis_index("groups") % 2
    z, y, c = me // 4, (me // 2) % 2, me % 2
    core_swap = [(i, i ^ 1) for i in range(size)]
    y_swap = [(i, i ^ 2) for i in range(size)]
    group_swap = [(i, i ^ 1) for i in range(groups)]

    def pp(v, perm, axis="tensor"):
        return lax.ppermute(v, axis, perm)

    def turn(r):
        return [(i, (i + 4 * r) % size) for i in range(size)]

    def after(v, *done):
        return lax.optimization_barrier((v, *done))[0]

    x_far = pp(tokens, y_swap)
    upper = rows * 5 // 8
    c_upper = pp(cotangent[:upper], y_swap)
    c_lower = pp(after(cotangent[upper:], c_upper), y_swap)
    both = jnp.stack([w_in, w_out])
    middle = lines // 2
    sent = [both] * lines
    sent[middle] = jnp.where(half == 0, w_in, w_out)
    first = pp(sent[middle], turn(middle))
    directs = [both]
    for r in range(1, lines):
        if r == middle:
            directs.append(first)
        else:
            directs.append(pp(after(both, first) if r > middle else both, turn(r)))
    halves = [directs[middle], pp(directs[middle], group_swap, "groups")]
    place = jnp.stack([z, y, c, half])
    scalars = jnp.concatenate([place, index_in.reshape(-1), index_out.reshape(-1)]).astype(jnp.int32)
    x_own, scalars, _, _ = lax.optimization_barrier((tokens, scalars, directs[-1], halves[1]))
    c_own = after(cotangent, directs[1])
    x_near = pp(x_own, core_swap)
    c_near = pp(c_own, core_swap)
    x_diag = pp(after(x_far, c_upper), core_swap)
    x_near = after(x_near, x_diag)

    smem = pl.BlockSpec(memory_space=pltpu.SMEM)
    hbm = pl.BlockSpec(memory_space=pltpu.HBM)
    shape = jax.ShapeDtypeStruct
    packed = (2, per, 2, side, side)
    token_buf = pltpu.VMEM((2 * rows, width), BF16)
    acc_buf = pltpu.VMEM((2 * rows, width), F32)
    dma = pltpu.SemaphoreType.DMA

    def call(last, out_shape, *operands):
        return pl.pallas_call(
            functools.partial(ffn_kernel, lines, per, side, last),
            out_shape=(shape((2, rows, width), BF16),) * 2 + out_shape,
            in_specs=[smem] + [hbm] * len(operands),
            out_specs=(hbm,) * (2 + len(out_shape)),
            scratch_shapes=[token_buf, token_buf, pltpu.VMEM((lines,) + packed, BF16), acc_buf, acc_buf,
                            pltpu.VMEM((lines,) + packed, F32), pltpu.VMEM((max(lines - 1, 1),) + packed, BF16),
                            dma((2,)), dma((4,)), dma((lines,)), dma((lines,)), dma((2, 2)), dma((lines,))],
            compiler_params=pltpu.CompilerParams(vmem_limit_bytes=24 * 1024 * 1024),
            cost_estimate=pl.CostEstimate(flops=1 << 20, bytes_accessed=1 << 20, transcendentals=0),
        )(scalars, *operands)

    weights = (*halves, *directs[:middle], *directs[middle + 1:])
    own, near, g_all = call(False, (shape((lines,) + packed, F32),), x_own, x_near, c_own, c_near, *weights)
    c_lower = after(c_lower, own)
    c_far = (c_upper, c_lower)
    c_diag = [pp(part, core_swap) for part in c_far]
    far, diagonal, g_own, *g_send = call(
        True, (shape(packed, F32),) + (shape(packed, BF16),) * (lines - 1),
        x_far, x_diag, *c_far, *c_diag, *weights, g_all)

    far = (far.astype(F32) + pp(diagonal, core_swap).astype(F32)).astype(BF16)
    received = [pp(after(g, far), turn(-r)) for r, g in enumerate(g_send, 1)]
    near = pp(after(near, far), core_swap)
    back = pp(far, y_swap)
    output, grad_tokens = [(own[n].astype(F32) + near[n].astype(F32) + back[n].astype(F32)).astype(BF16)
                           for n in range(2)]
    total = g_own
    for recv in received:
        total = total + recv.astype(F32)
    return output, grad_tokens, total[0], total[1]


def solution(mesh):
    in_specs = (
        P(("groups", "tensor"), None),
        P(("groups", "tensor"), None),
        P("tensor", None, None, None),
        P("tensor", None, None, None),
        P(),
        P(),
    )
    out_specs = (
        P(("groups", "tensor"), None),
        P(("groups", "tensor"), None),
        P(("groups", "tensor"), None, None, None),
        P(("groups", "tensor"), None, None, None),
    )
    fn = functools.partial(local, mesh.shape["tensor"], mesh.shape["groups"])
    return jax.shard_map(fn, mesh=mesh, in_specs=in_specs, out_specs=out_specs, check_vma=False)
```

time: 129 us -> 127 us (0.984)
  waiting for transfers between devices: 92 us -> 83.5 us
  Pallas kernels: 13.5 us -> 17.9 us
  starting transfers between devices: 12.8 us -> 15.1 us
    ppermute x15 -> x18, waiting for transfers between devices: 92 us -> 83.5 us  [pp(): return lax.ppermute(v, axis, perm)]
    pallas_call x1 -> x2, Pallas kernels: 13.5 us -> 17.9 us  [call(): pl.pallas_call(functools.partial(ffn_kernel, lines, per, side, last), out...]
    unnamed x6 -> x14, local copies, waits for them, and re-layouts: 3.99 us -> 1.44 us
    ppermute x15 -> x18, starting transfers between devices: 12.8 us -> 15.1 us  [pp(): return lax.ppermute(v, axis, perm)]
    slice x0 -> x2, local copies, waits for them, and re-layouts: none -> 1.99 us  [the longest x1 1.96 us: local(): c_upper = pp(cotangent[:upper], y_swap)]
  transfers between devices with their start and end apart: 15 -> 18, of which waited for: 7 -> 9; matrix products, arithmetic and copies ran while one was open for 3% -> 4% of each run, Pallas kernels for 0% -> 7%
where the time goes in v4:
time: 127 us
  waiting for transfers between devices  83.5 us (66%)
  Pallas kernels  17.9 us (14%)
  starting transfers between devices  15.1 us (12%)
  local copies, waits for them, and re-layouts  4.86 us (4%)
  other arithmetic  4.55 us (4%)
    ppermute x18, waiting for transfers between devices, pp(): return lax.ppermute(v, axis, perm)  83.5 us
    pallas_call x2, Pallas kernels, call(): pl.pallas_call(functools.partial(ffn_kernel, lines, per, side, last), out...  17.9 us
    ppermute x18, starting transfers between devices, pp(): return lax.ppermute(v, axis, perm)  15.1 us
  transfers between devices with their start and end apart: 18, of which 9 were waited for; matrix products, arithmetic and copies ran while one was open for 4% of the time, Pallas kernels for 7%

profile of v4, /device:TPU:0, one launch (start us, length us, event | category | flops | bytes accessed | tf_op | source)
XLA Modules:
  0.0 126.7 jit_solution(9739471763192308759)
XLA Ops:
  0.7 3.0 %collective-permute-start.4 = (bf16[128,4096]{1,0:T(8,128)(2,1)}, bf16[128,4096]{1,0:T(8,128)(2,1)}, u32[]{:S(2)}, u32[]{:S(2)}) collective-permute-start(bf16[128,4096]{1,0:T(8,128)(2,1)} %refs_0_), channel_id=1, source_target_pairs={{0,2},{1,3},{2,0},{3,1},{4,6},{5,7},{6,4},{7,5},{8,10},{9,11},{10,... | collective-permute-start | bytes 3145736 | tf_op jit(solution)/shard_map/ppermute | solution.py:161
  3.7 1.0 broadcast_select_fusion
  4.7 2.7 %collective-permute-start = (bf16[4,2,128,128]{3,2,1,0:T(8,128)(2,1)S(1)}, bf16[4,2,128,128]{3,2,1,0:T(8,128)(2,1)S(1)}, u32[]{:S(2)}, u32[]{:S(2)}) collective-permute-start(bf16[4,2,128,128]{3,2,1,0:T(8,128)(2,1)S(1)} %broadcast_select_fusion), channel_id=1, source_target_pairs={{0,8},{1,9},{2,10},{3,11},{4,12},{5,13},{6,14},{7,15},{8,0},{9,1},... | collective-permute-start | bytes 786440 | tf_op jit(solution)/shard_map/ppermute | solution.py:161
  7.4 2.0 %slice.30 = bf16[80,4096]{1,0:T(8,128)(2,1)} slice(bf16[128,4096]{1,0:T(8,128)(2,1)} %refs_2_), slice={[0:80], [0:4096]} | slice | bytes 1310720 | tf_op jit(solution)/shard_map/slice | solution.py:171
  9.9 1.6 %collective-permute-start.7 = (bf16[2,4,2,128,128]{4,3,2,1,0:T(8,128)(2,1)S(1)}, bf16[2,4,2,128,128]{4,3,2,1,0:T(8,128)(2,1)S(1)}, u32[]{:S(2)}, u32[]{:S(2)}) collective-permute-start(bf16[2,4,2,128,128]{4,3,2,1,0:T(8,128)(2,1)S(1)} %pad_maximum_fusion.refs_6_.refs_8_), channel_id=1, source_target_pairs={{0,4},{1,5},{2,6},{3,7},{4,8},{5,9},{6,10},{7,11},{8,12},{9,13},{1... | collective-permute-start | bytes 1572872 | tf_op jit(solution)/shard_map/ppermute | solution.py:161
  11.5 19.4 %collective-permute-done.refs_4_.refs_6_ = bf16[4,2,128,128]{3,2,1,0:T(8,128)(2,1)S(1)} collective-permute-done((bf16[4,2,128,128]{3,2,1,0:T(8,128)(2,1)S(1)}, bf16[4,2,128,128]{3,2,1,0:T(8,128)(2,1)S(1)}, u32[]{:S(2)}, u32[]{:S(2)}) %collective-permute-start) | collective-permute-done | bytes 262176 | tf_op jit(solution)/shard_map/ppermute | solution.py:161
  30.9 1.5 %collective-permute-start.2 = (bf16[4,2,128,128]{3,2,1,0:T(8,128)(2,1)S(1)}, bf16[4,2,128,128]{3,2,1,0:T(8,128)(2,1)S(1)}, u32[]{:S(2)}, u32[]{:S(2)}) collective-permute-start(bf16[4,2,128,128]{3,2,1,0:T(8,128)(2,1)S(1)} %collective-permute-done.refs_4_.refs_6_), channel_id=1, source_target_pairs={{0,16},{16,0},{1,17},{17,1},{2,18},{18,2},{3,19},{19,3},{4,20},{20... | collective-permute-start | bytes 786440 | tf_op jit(solution)/shard_map/ppermute | solution.py:161
  33.0 4.5 %collective-permute-done.2.refs_5_.refs_7_ = bf16[4,2,128,128]{3,2,1,0:T(8,128)(2,1)S(1)} collective-permute-done((bf16[4,2,128,128]{3,2,1,0:T(8,128)(2,1)S(1)}, bf16[4,2,128,128]{3,2,1,0:T(8,128)(2,1)S(1)}, u32[]{:S(2)}, u32[]{:S(2)}) %collective-permute-start.2) | collective-permute-done | bytes 262176 | tf_op jit(solution)/shard_map/ppermute | solution.py:161
  37.4 5.6 %collective-permute-done.1.refs_8_.refs_10_ = bf16[2,4,2,128,128]{4,3,2,1,0:T(8,128)(2,1)S(1)} collective-permute-done((bf16[2,4,2,128,128]{4,3,2,1,0:T(8,128)(2,1)S(1)}, bf16[2,4,2,128,128]{4,3,2,1,0:T(8,128)(2,1)S(1)}, u32[]{:S(2)}, u32[]{:S(2)}) %collective-permute-start.1) | collective-permute-done | bytes 524320 | tf_op jit(solution)/shard_map/ppermute | solution.py:161
  43.7 0.9 collective-permute-start.9
  44.7 1.2 collective-permute-done.3.refs_1_
  45.9 3.0 %collective-permute-done.6.refs_1_ = bf16[128,4096]{1,0:T(8,128)(2,1)S(1)} collective-permute-done((bf16[128,4096]{1,0:T(8,128)(2,1)}, bf16[128,4096]{1,0:T(8,128)(2,1)S(1)}, u32[]{:S(2)}, u32[]{:S(2)}) %collective-permute-start.6) | collective-permute-done | bytes 1048608 | tf_op jit(solution)/shard_map/ppermute | solution.py:161
  48.9 1.2 copy-done.1
  50.2 8.7 %shard_map.93 = (bf16[2,128,4096]{2,1,0:T(8,128)(2,1)S(1)}, bf16[2,128,4096]{2,1,0:T(8,128)(2,1)S(1)}, f32[4,2,4,2,128,128]{5,4,3,2,1,0:T(8,128)S(1)}) custom-call(s32[260]{0:T(512)S(1)} %concatenate.3.scalars, bf16[128,4096]{1,0:T(8,128)(2,1)S(1)} %copy-done.1, bf16[128,4096]{1,0:T(8,128)(2,1)S(1)} %collective-permute-done.3.refs_1_, ...), custom_call_target="tpu_custom_call" | custom-call | flops 1048576 | bytes 1048576 | tf_op jit(solution)/shard_map/pallas_call | solution.py:203
  59.0 1.6 %collective-permute-done.11.refs_5_ = bf16[48,4096]{1,0:T(8,128)(2,1)S(1)} collective-permute-done((bf16[48,4096]{1,0:T(8,128)(2,1)S(1)}, bf16[48,4096]{1,0:T(8,128)(2,1)S(1)}, u32[]{:S(2)}, u32[]{:S(2)}) %collective-permute-start.11) | collective-permute-done | bytes 393248 | tf_op jit(solution)/shard_map/ppermute | solution.py:161
  60.6 9.2 %shard_map.94 = (bf16[2,128,4096]{2,1,0:T(8,128)(2,1)S(1)}, bf16[2,128,4096]{2,1,0:T(8,128)(2,1)S(1)}, f32[2,4,2,128,128]{4,3,2,1,0:T(8,128)S(1)}, bf16[2,4,2,12...) custom-call(s32[260]{0:T(512)S(1)} %concatenate.3.scalars, ...), custom_call_target="tpu_custom_call" | custom-call | flops 1048576 | bytes 1048576 | tf_op jit(solution)/shard_map/pallas_call | solution.py:203
  70.0 4.0 %collective-permute-done.12 = bf16[2,128,4096]{2,1,0:T(8,128)(2,1)S(1)} collective-permute-done((bf16[2,128,4096]{2,1,0:T(8,128)(2,1)S(1)}, bf16[2,128,4096]{2,1,0:T(8,128)(2,1)S(1)}, u32[]{:S(2)}, u32[]{:S(2)}) %collective-permute-start.12) | collective-permute-done | bytes 2097184 | tf_op jit(solution)/shard_map/ppermute | solution.py:161
  74.1 0.8 add_convert_fusion
  75.1 0.8 collective-permute-start.14
  75.9 2.1 %collective-permute-start.15 = (bf16[2,4,2,128,128]{4,3,2,1,0:T(8,128)(2,1)S(1)}, bf16[2,4,2,128,128]{4,3,2,1,0:T(8,128)(2,1)S(1)}, u32[]{:S(2)}, u32[]{:S(2)}) collective-permute-start(bf16[2,4,2,128,128]{4,3,2,1,0:T(8,128)(2,1)S(1)} %get-tuple-element.41), channel_id=1, source_target_pairs={{0,12},{1,13},{2,14},{3,15},{4,0},{5,1},{6,2},{7,3},{8,4},{9,5},{1... | collective-permute-start | bytes 1572872 | tf_op jit(solution)/shard_map/ppermute | solution.py:161
  78.7 12.1 %collective-permute-done.15 = bf16[2,4,2,128,128]{4,3,2,1,0:T(8,128)(2,1)S(1)} collective-permute-done((bf16[2,4,2,128,128]{4,3,2,1,0:T(8,128)(2,1)S(1)}, bf16[2,4,2,128,128]{4,3,2,1,0:T(8,128)(2,1)S(1)}, u32[]{:S(2)}, u32[]{:S(2)}) %collective-permute-start.15) | collective-permute-done | bytes 524320 | tf_op jit(solution)/shard_map/ppermute | solution.py:161
  90.9 32.0 %collective-permute-done.16 = bf16[2,4,2,128,128]{4,3,2,1,0:T(8,128)(2,1)S(1)} collective-permute-done((bf16[2,4,2,128,128]{4,3,2,1,0:T(8,128)(2,1)S(1)}, bf16[2,4,2,128,128]{4,3,2,1,0:T(8,128)(2,1)S(1)}, u32[]{:S(2)}, u32[]{:S(2)}) %collective-permute-start.16) | collective-permute-done | bytes 524320 | tf_op jit(solution)/shard_map/ppermute | solution.py:161
  123.1 1.1 slice_bitcast_fusion
  124.2 2.5 %fusion.1 = (bf16[128,4096]{1,0:T(8,128)(2,1)}, bf16[128,4096]{1,0:T(8,128)(2,1)}) fusion(bf16[2,128,4096]{2,1,0:T(8,128)(2,1)S(1)} %collective-permute-done.14, bf16[2,128,4096]{2,1,0:T(8,128)(2,1)S(1)} %collective-permute-done.13, bf16[2,128,4096]{2,1,0:T(8,128)(2,1)S(1)} %get-tuple-element.31), kind=kLoop, calls=%fused_computation.4 | loop fusion | flops 6291456 | bytes 8388608 | tf_op jit(solution)/shard_map/convert_element_type | solution.py:228
  (39 shorter events, 3.5 us)
Async XLA Ops:
  0.6 9.2 %copy-start.3 = (bf16[4,2,128,128]{3,2,1,0:T(8,128)(2,1)S(1)}, bf16[4,2,128,128]{3,2,1,0:T(8,128)(2,1)}, u32[]{:S(2)}) copy-start(bf16[4,2,128,128]{3,2,1,0:T(8,128)(2,1)} %param.9) | copy-start | bytes 786436
  0.6 9.2 %copy-start.2 = (bf16[4,2,128,128]{3,2,1,0:T(8,128)(2,1)S(1)}, bf16[4,2,128,128]{3,2,1,0:T(8,128)(2,1)}, u32[]{:S(2)}) copy-start(bf16[4,2,128,128]{3,2,1,0:T(8,128)(2,1)} %param.8) | copy-start | bytes 786436
  0.7 42.9 %copy-start = (bf16[128,4096]{1,0:T(8,128)(2,1)S(1)}, bf16[128,4096]{1,0:T(8,128)(2,1)}, u32[]{:S(2)}) copy-start(bf16[128,4096]{1,0:T(8,128)(2,1)} %refs_2_) | copy-start | bytes 3145732
  0.7 31.7 %copy-start.4 = (s32[64,2]{0,1:T(2,128)S(1)}, s32[64,2]{0,1:T(2,128)}, u32[]{:S(2)}) copy-start(s32[64,2]{0,1:T(2,128)} %param.10) | copy-start | bytes 1540
  0.7 31.9 %copy-start.5 = (s32[64,2]{0,1:T(2,128)S(1)}, s32[64,2]{0,1:T(2,128)}, u32[]{:S(2)}) copy-start(s32[64,2]{0,1:T(2,128)} %param.11) | copy-start | bytes 1540
  0.7 42.4 %collective-permute-start.4 = (bf16[128,4096]{1,0:T(8,128)(2,1)}, bf16[128,4096]{1,0:T(8,128)(2,1)}, u32[]{:S(2)}, u32[]{:S(2)}) collective-permute-start(bf16[128,4096]{1,0:T(8,128)(2,1)} %refs_0_), channel_id=1, source_target_pairs={{0,2},{1,3},{2,0},{3,1},{4,6},{5,7},{6,4},{7,5},{8,10},{9,11},{10,... | collective-permute-start | bytes 3145736 | tf_op jit(solution)/shard_map/ppermute | solution.py:161
  4.7 26.2 %collective-permute-start = (bf16[4,2,128,128]{3,2,1,0:T(8,128)(2,1)S(1)}, bf16[4,2,128,128]{3,2,1,0:T(8,128)(2,1)S(1)}, u32[]{:S(2)}, u32[]{:S(2)}) collective-permute-start(bf16[4,2,128,128]{3,2,1,0:T(8,128)(2,1)S(1)} %broadcast_select_fusion), channel_id=1, source_target_pairs={{0,8},{1,9},{2,10},{3,11},{4,12},{5,13},{6,14},{7,15},{8,0},{9,1},... | collective-permute-start | bytes 786440 | tf_op jit(solution)/shard_map/ppermute | solution.py:161
  9.3 33.7 %collective-permute-start.5 = (bf16[80,4096]{1,0:T(8,128)(2,1)}, bf16[80,4096]{1,0:T(8,128)(2,1)}, u32[]{:S(2)}, u32[]{:S(2)}) collective-permute-start(bf16[80,4096]{1,0:T(8,128)(2,1)} %slice.30), channel_id=1, source_target_pairs={{0,2},{1,3},{2,0},{3,1},{4,6},{5,7},{6,4},{7,5},{8,10},{9,11},{10,... | collective-permute-start | bytes 1966088 | tf_op jit(solution)/shard_map/ppermute | solution.py:161
  9.9 23.1 %collective-permute-start.7 = (bf16[2,4,2,128,128]{4,3,2,1,0:T(8,128)(2,1)S(1)}, bf16[2,4,2,128,128]{4,3,2,1,0:T(8,128)(2,1)S(1)}, u32[]{:S(2)}, u32[]{:S(2)}) collective-permute-start(bf16[2,4,2,128,128]{4,3,2,1,0:T(8,128)(2,1)S(1)} %pad_maximum_fusion.refs_6_.refs_8_), channel_id=1, source_target_pairs={{0,4},{1,5},{2,6},{3,7},{4,8},{5,9},{6,10},{7,11},{8,12},{9,13},{1... | collective-permute-start | bytes 1572872 | tf_op jit(solution)/shard_map/ppermute | solution.py:161
  30.9 12.2 %collective-permute-start.1 = (bf16[2,4,2,128,128]{4,3,2,1,0:T(8,128)(2,1)S(1)}, bf16[2,4,2,128,128]{4,3,2,1,0:T(8,128)(2,1)S(1)}, u32[]{:S(2)}, u32[]{:S(2)}) collective-permute-start(bf16[2,4,2,128,128]{4,3,2,1,0:T(8,128)(2,1)S(1)} %pad_maximum_fusion.refs_6_.refs_8_), channel_id=1, source_target_pairs={{0,12},{1,13},{2,14},{3,15},{4,0},{5,1},{6,2},{7,3},{8,4},{9,5},{1... | collective-permute-start | bytes 1572872 | tf_op jit(solution)/shard_map/ppermute | solution.py:161
  30.9 6.6 %collective-permute-start.2 = (bf16[4,2,128,128]{3,2,1,0:T(8,128)(2,1)S(1)}, bf16[4,2,128,128]{3,2,1,0:T(8,128)(2,1)S(1)}, u32[]{:S(2)}, u32[]{:S(2)}) collective-permute-start(bf16[4,2,128,128]{3,2,1,0:T(8,128)(2,1)S(1)} %collective-permute-done.refs_4_.refs_6_), channel_id=1, source_target_pairs={{0,16},{16,0},{1,17},{17,1},{2,18},{18,2},{3,19},{19,3},{4,20},{20... | collective-permute-start | bytes 786440 | tf_op jit(solution)/shard_map/ppermute | solution.py:161
  43.1 2.9 %collective-permute-start.3 = (bf16[128,4096]{1,0:T(8,128)(2,1)}, bf16[128,4096]{1,0:T(8,128)(2,1)S(1)}, u32[]{:S(2)}, u32[]{:S(2)}) collective-permute-start(bf16[128,4096]{1,0:T(8,128)(2,1)} %refs_0_), channel_id=1, source_target_pairs={{0,1},{1,0},{2,3},{3,2},{4,5},{5,4},{6,7},{7,6},{8,9},{9,8},{10,11... | collective-permute-start | bytes 3145736 | tf_op jit(solution)/shard_map/ppermute | solution.py:161
  43.1 5.9 %collective-permute-start.6 = (bf16[128,4096]{1,0:T(8,128)(2,1)}, bf16[128,4096]{1,0:T(8,128)(2,1)S(1)}, u32[]{:S(2)}, u32[]{:S(2)}) collective-permute-start(bf16[128,4096]{1,0:T(8,128)(2,1)} %collective-permute-done.4.refs_0_), channel_id=1, source_target_pairs={{0,1},{1,0},{2,3},{3,2},{4,5},{5,4},{6,7},{7,6},{8,9},{9,8},{10,11... | collective-permute-start | bytes 3145736 | tf_op jit(solution)/shard_map/ppermute | solution.py:161
  43.6 5.4 %collective-permute-start.8 = (bf16[128,4096]{1,0:T(8,128)(2,1)S(1)}, bf16[128,4096]{1,0:T(8,128)(2,1)S(1)}, u32[]{:S(2)}, u32[]{:S(2)}) collective-permute-start(bf16[128,4096]{1,0:T(8,128)(2,1)S(1)} %copy-done), channel_id=1, source_target_pairs={{0,1},{1,0},{2,3},{3,2},{4,5},{5,4},{6,7},{7,6},{8,9},{9,8},{10,11... | collective-permute-start | bytes 3145736 | tf_op jit(solution)/shard_map/ppermute | solution.py:161
  43.7 15.1 %collective-permute-start.9 = (bf16[48,4096]{1,0:T(8,128)(2,1)S(1)}, bf16[48,4096]{1,0:T(8,128)(2,1)S(1)}, u32[]{:S(2)}, u32[]{:S(2)}) collective-permute-start(bf16[48,4096]{1,0:T(8,128)(2,1)S(1)} %slice.32), channel_id=1, source_target_pairs={{0,2},{1,3},{2,0},{3,1},{4,6},{5,7},{6,4},{7,5},{8,10},{9,11},{10,... | collective-permute-start | bytes 1179656 | tf_op jit(solution)/shard_map/ppermute | solution.py:161
  44.6 14.5 %collective-permute-start.10 = (bf16[80,4096]{1,0:T(8,128)(2,1)}, bf16[80,4096]{1,0:T(8,128)(2,1)S(1)}, u32[]{:S(2)}, u32[]{:S(2)}) collective-permute-start(bf16[80,4096]{1,0:T(8,128)(2,1)} %collective-permute-done.5.refs_2_), channel_id=1, source_target_pairs={{0,1},{1,0},{2,3},{3,2},{4,5},{5,4},{6,7},{7,6},{8,9},{9,8},{10,11... | collective-permute-start | bytes 1966088 | tf_op jit(solution)/shard_map/ppermute | solution.py:161
  48.9 1.2 copy-start.1
  58.8 1.8 %collective-permute-start.11 = (bf16[48,4096]{1,0:T(8,128)(2,1)S(1)}, bf16[48,4096]{1,0:T(8,128)(2,1)S(1)}, u32[]{:S(2)}, u32[]{:S(2)}) collective-permute-start(bf16[48,4096]{1,0:T(8,128)(2,1)S(1)} %collective-permute-done.9.refs_3_), channel_id=1, source_target_pairs={{0,1},{1,0},{2,3},{3,2},{4,5},{5,4},{6,7},{7,6},{8,9},{9,8},{10,11... | collective-permute-start | bytes 1179656 | tf_op jit(solution)/shard_map/ppermute | solution.py:161
  69.9 4.2 %collective-permute-start.12 = (bf16[2,128,4096]{2,1,0:T(8,128)(2,1)S(1)}, bf16[2,128,4096]{2,1,0:T(8,128)(2,1)S(1)}, u32[]{:S(2)}, u32[]{:S(2)}) collective-permute-start(bf16[2,128,4096]{2,1,0:T(8,128)(2,1)S(1)} %get-tuple-element.37), channel_id=1, source_target_pairs={{0,1},{1,0},{2,3},{3,2},{4,5},{5,4},{6,7},{7,6},{8,9},{9,8},{10,11... | collective-permute-start | bytes 6291464 | tf_op jit(solution)/shard_map/ppermute | solution.py:161
  74.9 49.3 %collective-permute-start.13 = (bf16[2,128,4096]{2,1,0:T(8,128)(2,1)S(1)}, bf16[2,128,4096]{2,1,0:T(8,128)(2,1)S(1)}, u32[]{:S(2)}, u32[]{:S(2)}) collective-permute-start(bf16[2,128,4096]{2,1,0:T(8,128)(2,1)S(1)} %get-tuple-element.38), channel_id=1, source_target_pairs={{0,1},{1,0},{2,3},{3,2},{4,5},{5,4},{6,7},{7,6},{8,9},{9,8},{10,11... | collective-permute-start | bytes 6291464 | tf_op jit(solution)/shard_map/ppermute | solution.py:161
  75.1 49.1 %collective-permute-start.14 = (bf16[2,128,4096]{2,1,0:T(8,128)(2,1)S(1)}, bf16[2,128,4096]{2,1,0:T(8,128)(2,1)S(1)}, u32[]{:S(2)}, u32[]{:S(2)}) collective-permute-start(bf16[2,128,4096]{2,1,0:T(8,128)(2,1)S(1)} %add_convert_fusion), channel_id=1, source_target_pairs={{0,2},{1,3},{2,0},{3,1},{4,6},{5,7},{6,4},{7,5},{8,10},{9,11},{10,... | collective-permute-start | bytes 6291464 | tf_op jit(solution)/shard_map/ppermute | solution.py:161
  75.9 15.0 %collective-permute-start.15 = (bf16[2,4,2,128,128]{4,3,2,1,0:T(8,128)(2,1)S(1)}, bf16[2,4,2,128,128]{4,3,2,1,0:T(8,128)(2,1)S(1)}, u32[]{:S(2)}, u32[]{:S(2)}) collective-permute-start(bf16[2,4,2,128,128]{4,3,2,1,0:T(8,128)(2,1)S(1)} %get-tuple-element.41), channel_id=1, source_target_pairs={{0,12},{1,13},{2,14},{3,15},{4,0},{5,1},{6,2},{7,3},{8,4},{9,5},{1... | collective-permute-start | bytes 1572872 | tf_op jit(solution)/shard_map/ppermute | solution.py:161
  78.0 44.9 %collective-permute-start.16 = (bf16[2,4,2,128,128]{4,3,2,1,0:T(8,128)(2,1)S(1)}, bf16[2,4,2,128,128]{4,3,2,1,0:T(8,128)(2,1)S(1)}, u32[]{:S(2)}, u32[]{:S(2)}) collective-permute-start(bf16[2,4,2,128,128]{4,3,2,1,0:T(8,128)(2,1)S(1)} %get-tuple-element.43), channel_id=1, source_target_pairs={{0,8},{1,9},{2,10},{3,11},{4,12},{5,13},{6,14},{7,15},{8,0},{9,1},... | collective-permute-start | bytes 1572872 | tf_op jit(solution)/shard_map/ppermute | solution.py:161
  78.0 44.9 %collective-permute-start.17 = (bf16[2,4,2,128,128]{4,3,2,1,0:T(8,128)(2,1)S(1)}, bf16[2,4,2,128,128]{4,3,2,1,0:T(8,128)(2,1)S(1)}, u32[]{:S(2)}, u32[]{:S(2)}) collective-permute-start(bf16[2,4,2,128,128]{4,3,2,1,0:T(8,128)(2,1)S(1)} %get-tuple-element.45), channel_id=1, source_target_pairs={{0,4},{1,5},{2,6},{3,7},{4,8},{5,9},{6,10},{7,11},{8,12},{9,13},{1... | collective-permute-start | bytes 1572872 | tf_op jit(solution)/shard_map/ppermute | solution.py:161

commit v5 on v4

--- a/solution.py
+++ b/solution.py
@@ -227,10 +227,13 @@
     back = pp(far, y_swap)
     output, grad_tokens = [(own[n].astype(F32) + near[n].astype(F32) + back[n].astype(F32)).astype(BF16)
                            for n in range(2)]
-    total = g_own
-    for recv in received:
-        total = total + recv.astype(F32)
-    return output, grad_tokens, total[0], total[1]
+    grads = []
+    for n in range(2):
+        total = g_own[n]
+        for recv in received:
+            total = total + recv[n].astype(F32)
+        grads.append(total)
+    return output, grad_tokens, grads[0], grads[1]
 
 
 def solution(mesh):

time: 127 us -> 127 us (level)
  no operation moved by 1% of the time
where the time goes in v5:
time: 127 us
  waiting for transfers between devices  83.4 us (66%)
  Pallas kernels  17.8 us (14%)
  starting transfers between devices  15.2 us (12%)
  other arithmetic  5.52 us (4%)
  local copies, waits for them, and re-layouts  3.79 us (3%)
    ppermute x18, waiting for transfers between devices, pp(): return lax.ppermute(v, axis, perm)  83.4 us
    pallas_call x2, Pallas kernels, call(): pl.pallas_call(functools.partial(ffn_kernel, lines, per, side, last), out...  17.8 us
    ppermute x18, starting transfers between devices, pp(): return lax.ppermute(v, axis, perm)  15.2 us
  transfers between devices with their start and end apart: 18, of which 9 were waited for; matrix products, arithmetic and copies ran while one was open for 4% of the time, Pallas kernels for 7%

profile of v5, /device:TPU:0, one launch (start us, length us, event | category | flops | bytes accessed | tf_op | source)
XLA Modules:
  0.0 126.6 jit_solution(5560825227731264437)
XLA Ops:
  0.7 3.0 %collective-permute-start.4 = (bf16[128,4096]{1,0:T(8,128)(2,1)}, bf16[128,4096]{1,0:T(8,128)(2,1)}, u32[]{:S(2)}, u32[]{:S(2)}) collective-permute-start(bf16[128,4096]{1,0:T(8,128)(2,1)} %refs_0_), channel_id=1, source_target_pairs={{0,2},{1,3},{2,0},{3,1},{4,6},{5,7},{6,4},{7,5},{8,10},{9,11},{10,... | collective-permute-start | bytes 3145736 | tf_op jit(solution)/shard_map/ppermute | solution.py:161
  3.7 1.0 broadcast_select_fusion
  4.7 2.7 %collective-permute-start = (bf16[4,2,128,128]{3,2,1,0:T(8,128)(2,1)S(1)}, bf16[4,2,128,128]{3,2,1,0:T(8,128)(2,1)S(1)}, u32[]{:S(2)}, u32[]{:S(2)}) collective-permute-start(bf16[4,2,128,128]{3,2,1,0:T(8,128)(2,1)S(1)} %broadcast_select_fusion), channel_id=1, source_target_pairs={{0,8},{1,9},{2,10},{3,11},{4,12},{5,13},{6,14},{7,15},{8,0},{9,1},... | collective-permute-start | bytes 786440 | tf_op jit(solution)/shard_map/ppermute | solution.py:161
  7.4 2.0 %slice.48 = bf16[80,4096]{1,0:T(8,128)(2,1)} slice(bf16[128,4096]{1,0:T(8,128)(2,1)} %refs_2_), slice={[0:80], [0:4096]} | slice | bytes 1310720 | tf_op jit(solution)/shard_map/slice | solution.py:171
  9.9 1.6 %collective-permute-start.7 = (bf16[2,4,2,128,128]{4,3,2,1,0:T(8,128)(2,1)S(1)}, bf16[2,4,2,128,128]{4,3,2,1,0:T(8,128)(2,1)S(1)}, u32[]{:S(2)}, u32[]{:S(2)}) collective-permute-start(bf16[2,4,2,128,128]{4,3,2,1,0:T(8,128)(2,1)S(1)} %pad_maximum_fusion.refs_6_.refs_8_), channel_id=1, source_target_pairs={{0,4},{1,5},{2,6},{3,7},{4,8},{5,9},{6,10},{7,11},{8,12},{9,13},{1... | collective-permute-start | bytes 1572872 | tf_op jit(solution)/shard_map/ppermute | solution.py:161
  11.5 19.4 %collective-permute-done.refs_4_.refs_6_ = bf16[4,2,128,128]{3,2,1,0:T(8,128)(2,1)S(1)} collective-permute-done((bf16[4,2,128,128]{3,2,1,0:T(8,128)(2,1)S(1)}, bf16[4,2,128,128]{3,2,1,0:T(8,128)(2,1)S(1)}, u32[]{:S(2)}, u32[]{:S(2)}) %collective-permute-start) | collective-permute-done | bytes 262176 | tf_op jit(solution)/shard_map/ppermute | solution.py:161
  30.9 1.5 %collective-permute-start.2 = (bf16[4,2,128,128]{3,2,1,0:T(8,128)(2,1)S(1)}, bf16[4,2,128,128]{3,2,1,0:T(8,128)(2,1)S(1)}, u32[]{:S(2)}, u32[]{:S(2)}) collective-permute-start(bf16[4,2,128,128]{3,2,1,0:T(8,128)(2,1)S(1)} %collective-permute-done.refs_4_.refs_6_), channel_id=1, source_target_pairs={{0,16},{16,0},{1,17},{17,1},{2,18},{18,2},{3,19},{19,3},{4,20},{20... | collective-permute-start | bytes 786440 | tf_op jit(solution)/shard_map/ppermute | solution.py:161
  33.0 4.5 %collective-permute-done.2.refs_5_.refs_7_ = bf16[4,2,128,128]{3,2,1,0:T(8,128)(2,1)S(1)} collective-permute-done((bf16[4,2,128,128]{3,2,1,0:T(8,128)(2,1)S(1)}, bf16[4,2,128,128]{3,2,1,0:T(8,128)(2,1)S(1)}, u32[]{:S(2)}, u32[]{:S(2)}) %collective-permute-start.2) | collective-permute-done | bytes 262176 | tf_op jit(solution)/shard_map/ppermute | solution.py:161
  37.4 5.6 %collective-permute-done.1.refs_8_.refs_10_ = bf16[2,4,2,128,128]{4,3,2,1,0:T(8,128)(2,1)S(1)} collective-permute-done((bf16[2,4,2,128,128]{4,3,2,1,0:T(8,128)(2,1)S(1)}, bf16[2,4,2,128,128]{4,3,2,1,0:T(8,128)(2,1)S(1)}, u32[]{:S(2)}, u32[]{:S(2)}) %collective-permute-start.1) | collective-permute-done | bytes 524320 | tf_op jit(solution)/shard_map/ppermute | solution.py:161
  43.7 0.9 collective-permute-start.9
  44.7 1.2 collective-permute-done.3.refs_1_
  45.9 3.0 %collective-permute-done.6.refs_1_ = bf16[128,4096]{1,0:T(8,128)(2,1)S(1)} collective-permute-done((bf16[128,4096]{1,0:T(8,128)(2,1)}, bf16[128,4096]{1,0:T(8,128)(2,1)S(1)}, u32[]{:S(2)}, u32[]{:S(2)}) %collective-permute-start.6) | collective-permute-done | bytes 1048608 | tf_op jit(solution)/shard_map/ppermute | solution.py:161
  48.9 1.2 copy-done.1
  50.2 8.6 %shard_map.93 = (bf16[2,128,4096]{2,1,0:T(8,128)(2,1)S(1)}, bf16[2,128,4096]{2,1,0:T(8,128)(2,1)S(1)}, f32[4,2,4,2,128,128]{5,4,3,2,1,0:T(8,128)S(1)}) custom-call(s32[260]{0:T(512)S(1)} %concatenate.3.scalars, bf16[128,4096]{1,0:T(8,128)(2,1)S(1)} %copy-done.1, bf16[128,4096]{1,0:T(8,128)(2,1)S(1)} %collective-permute-done.3.refs_1_, ...), custom_call_target="tpu_custom_call" | custom-call | flops 1048576 | bytes 1048576 | tf_op jit(solution)/shard_map/pallas_call | solution.py:203
  59.0 1.6 %collective-permute-done.11.refs_5_ = bf16[48,4096]{1,0:T(8,128)(2,1)S(1)} collective-permute-done((bf16[48,4096]{1,0:T(8,128)(2,1)S(1)}, bf16[48,4096]{1,0:T(8,128)(2,1)S(1)}, u32[]{:S(2)}, u32[]{:S(2)}) %collective-permute-start.11) | collective-permute-done | bytes 393248 | tf_op jit(solution)/shard_map/ppermute | solution.py:161
  60.6 9.2 %shard_map.94 = (bf16[2,128,4096]{2,1,0:T(8,128)(2,1)S(1)}, bf16[2,128,4096]{2,1,0:T(8,128)(2,1)S(1)}, f32[2,4,2,128,128]{4,3,2,1,0:T(8,128)S(1)}, bf16[2,4,2,12...) custom-call(s32[260]{0:T(512)S(1)} %concatenate.3.scalars, ...), custom_call_target="tpu_custom_call" | custom-call | flops 1048576 | bytes 1048576 | tf_op jit(solution)/shard_map/pallas_call | solution.py:203
  70.1 4.0 %collective-permute-done.12 = bf16[2,128,4096]{2,1,0:T(8,128)(2,1)S(1)} collective-permute-done((bf16[2,128,4096]{2,1,0:T(8,128)(2,1)S(1)}, bf16[2,128,4096]{2,1,0:T(8,128)(2,1)S(1)}, u32[]{:S(2)}, u32[]{:S(2)}) %collective-permute-start.12) | collective-permute-done | bytes 2097184 | tf_op jit(solution)/shard_map/ppermute | solution.py:161
  74.0 0.8 add_convert_fusion
  75.1 0.9 collective-permute-start.14
  75.9 2.1 %collective-permute-start.15 = (bf16[2,4,2,128,128]{4,3,2,1,0:T(8,128)(2,1)S(1)}, bf16[2,4,2,128,128]{4,3,2,1,0:T(8,128)(2,1)S(1)}, u32[]{:S(2)}, u32[]{:S(2)}) collective-permute-start(bf16[2,4,2,128,128]{4,3,2,1,0:T(8,128)(2,1)S(1)} %get-tuple-element.41), channel_id=1, source_target_pairs={{0,12},{1,13},{2,14},{3,15},{4,0},{5,1},{6,2},{7,3},{8,4},{9,5},{1... | collective-permute-start | bytes 1572872 | tf_op jit(solution)/shard_map/ppermute | solution.py:161
  78.7 12.2 %collective-permute-done.15 = bf16[2,4,2,128,128]{4,3,2,1,0:T(8,128)(2,1)S(1)} collective-permute-done((bf16[2,4,2,128,128]{4,3,2,1,0:T(8,128)(2,1)S(1)}, bf16[2,4,2,128,128]{4,3,2,1,0:T(8,128)(2,1)S(1)}, u32[]{:S(2)}, u32[]{:S(2)}) %collective-permute-start.15) | collective-permute-done | bytes 524320 | tf_op jit(solution)/shard_map/ppermute | solution.py:161
  90.9 32.0 %collective-permute-done.16 = bf16[2,4,2,128,128]{4,3,2,1,0:T(8,128)(2,1)S(1)} collective-permute-done((bf16[2,4,2,128,128]{4,3,2,1,0:T(8,128)(2,1)S(1)}, bf16[2,4,2,128,128]{4,3,2,1,0:T(8,128)(2,1)S(1)}, u32[]{:S(2)}, u32[]{:S(2)}) %collective-permute-start.16) | collective-permute-done | bytes 524320 | tf_op jit(solution)/shard_map/ppermute | solution.py:161
  122.9 1.2 add_bitcast_fusion
  124.1 2.5 %fusion.1 = (bf16[128,4096]{1,0:T(8,128)(2,1)}, bf16[128,4096]{1,0:T(8,128)(2,1)}) fusion(bf16[2,128,4096]{2,1,0:T(8,128)(2,1)S(1)} %collective-permute-done.14, bf16[2,128,4096]{2,1,0:T(8,128)(2,1)S(1)} %collective-permute-done.13, bf16[2,128,4096]{2,1,0:T(8,128)(2,1)S(1)} %get-tuple-element.31), kind=kLoop, calls=%fused_computation.4 | loop fusion | flops 6291456 | bytes 8388608 | tf_op jit(solution)/shard_map/convert_element_type | solution.py:228
  (38 shorter events, 3.3 us)
Async XLA Ops:
  0.6 9.2 %copy-start.3 = (bf16[4,2,128,128]{3,2,1,0:T(8,128)(2,1)S(1)}, bf16[4,2,128,128]{3,2,1,0:T(8,128)(2,1)}, u32[]{:S(2)}) copy-start(bf16[4,2,128,128]{3,2,1,0:T(8,128)(2,1)} %param.9) | copy-start | bytes 786436
  0.6 9.2 %copy-start.2 = (bf16[4,2,128,128]{3,2,1,0:T(8,128)(2,1)S(1)}, bf16[4,2,128,128]{3,2,1,0:T(8,128)(2,1)}, u32[]{:S(2)}) copy-start(bf16[4,2,128,128]{3,2,1,0:T(8,128)(2,1)} %param.8) | copy-start | bytes 786436
  0.7 42.9 %copy-start = (bf16[128,4096]{1,0:T(8,128)(2,1)S(1)}, bf16[128,4096]{1,0:T(8,128)(2,1)}, u32[]{:S(2)}) copy-start(bf16[128,4096]{1,0:T(8,128)(2,1)} %refs_2_) | copy-start | bytes 3145732
  0.7 31.7 %copy-start.4 = (s32[64,2]{0,1:T(2,128)S(1)}, s32[64,2]{0,1:T(2,128)}, u32[]{:S(2)}) copy-start(s32[64,2]{0,1:T(2,128)} %param.10) | copy-start | bytes 1540
  0.7 31.9 %copy-start.5 = (s32[64,2]{0,1:T(2,128)S(1)}, s32[64,2]{0,1:T(2,128)}, u32[]{:S(2)}) copy-start(s32[64,2]{0,1:T(2,128)} %param.11) | copy-start | bytes 1540
  0.7 42.4 %collective-permute-start.4 = (bf16[128,4096]{1,0:T(8,128)(2,1)}, bf16[128,4096]{1,0:T(8,128)(2,1)}, u32[]{:S(2)}, u32[]{:S(2)}) collective-permute-start(bf16[128,4096]{1,0:T(8,128)(2,1)} %refs_0_), channel_id=1, source_target_pairs={{0,2},{1,3},{2,0},{3,1},{4,6},{5,7},{6,4},{7,5},{8,10},{9,11},{10,... | collective-permute-start | bytes 3145736 | tf_op jit(solution)/shard_map/ppermute | solution.py:161
  4.7 26.2 %collective-permute-start = (bf16[4,2,128,128]{3,2,1,0:T(8,128)(2,1)S(1)}, bf16[4,2,128,128]{3,2,1,0:T(8,128)(2,1)S(1)}, u32[]{:S(2)}, u32[]{:S(2)}) collective-permute-start(bf16[4,2,128,128]{3,2,1,0:T(8,128)(2,1)S(1)} %broadcast_select_fusion), channel_id=1, source_target_pairs={{0,8},{1,9},{2,10},{3,11},{4,12},{5,13},{6,14},{7,15},{8,0},{9,1},... | collective-permute-start | bytes 786440 | tf_op jit(solution)/shard_map/ppermute | solution.py:161
  9.3 33.7 %collective-permute-start.5 = (bf16[80,4096]{1,0:T(8,128)(2,1)}, bf16[80,4096]{1,0:T(8,128)(2,1)}, u32[]{:S(2)}, u32[]{:S(2)}) collective-permute-start(bf16[80,4096]{1,0:T(8,128)(2,1)} %slice.48), channel_id=1, source_target_pairs={{0,2},{1,3},{2,0},{3,1},{4,6},{5,7},{6,4},{7,5},{8,10},{9,11},{10,... | collective-permute-start | bytes 1966088 | tf_op jit(solution)/shard_map/ppermute | solution.py:161
  9.9 23.1 %collective-permute-start.7 = (bf16[2,4,2,128,128]{4,3,2,1,0:T(8,128)(2,1)S(1)}, bf16[2,4,2,128,128]{4,3,2,1,0:T(8,128)(2,1)S(1)}, u32[]{:S(2)}, u32[]{:S(2)}) collective-permute-start(bf16[2,4,2,128,128]{4,3,2,1,0:T(8,128)(2,1)S(1)} %pad_maximum_fusion.refs_6_.refs_8_), channel_id=1, source_target_pairs={{0,4},{1,5},{2,6},{3,7},{4,8},{5,9},{6,10},{7,11},{8,12},{9,13},{1... | collective-permute-start | bytes 1572872 | tf_op jit(solution)/shard_map/ppermute | solution.py:161
  30.9 12.2 %collective-permute-start.1 = (bf16[2,4,2,128,128]{4,3,2,1,0:T(8,128)(2,1)S(1)}, bf16[2,4,2,128,128]{4,3,2,1,0:T(8,128)(2,1)S(1)}, u32[]{:S(2)}, u32[]{:S(2)}) collective-permute-start(bf16[2,4,2,128,128]{4,3,2,1,0:T(8,128)(2,1)S(1)} %pad_maximum_fusion.refs_6_.refs_8_), channel_id=1, source_target_pairs={{0,12},{1,13},{2,14},{3,15},{4,0},{5,1},{6,2},{7,3},{8,4},{9,5},{1... | collective-permute-start | bytes 1572872 | tf_op jit(solution)/shard_map/ppermute | solution.py:161
  30.9 6.6 %collective-permute-start.2 = (bf16[4,2,128,128]{3,2,1,0:T(8,128)(2,1)S(1)}, bf16[4,2,128,128]{3,2,1,0:T(8,128)(2,1)S(1)}, u32[]{:S(2)}, u32[]{:S(2)}) collective-permute-start(bf16[4,2,128,128]{3,2,1,0:T(8,128)(2,1)S(1)} %collective-permute-done.refs_4_.refs_6_), channel_id=1, source_target_pairs={{0,16},{16,0},{1,17},{17,1},{2,18},{18,2},{3,19},{19,3},{4,20},{20... | collective-permute-start | bytes 786440 | tf_op jit(solution)/shard_map/ppermute | solution.py:161
  43.1 2.9 %collective-permute-start.3 = (bf16[128,4096]{1,0:T(8,128)(2,1)}, bf16[128,4096]{1,0:T(8,128)(2,1)S(1)}, u32[]{:S(2)}, u32[]{:S(2)}) collective-permute-start(bf16[128,4096]{1,0:T(8,128)(2,1)} %refs_0_), channel_id=1, source_target_pairs={{0,1},{1,0},{2,3},{3,2},{4,5},{5,4},{6,7},{7,6},{8,9},{9,8},{10,11... | collective-permute-start | bytes 3145736 | tf_op jit(solution)/shard_map/ppermute | solution.py:161
  43.1 5.9 %collective-permute-start.6 = (bf16[128,4096]{1,0:T(8,128)(2,1)}, bf16[128,4096]{1,0:T(8,128)(2,1)S(1)}, u32[]{:S(2)}, u32[]{:S(2)}) collective-permute-start(bf16[128,4096]{1,0:T(8,128)(2,1)} %collective-permute-done.4.refs_0_), channel_id=1, source_target_pairs={{0,1},{1,0},{2,3},{3,2},{4,5},{5,4},{6,7},{7,6},{8,9},{9,8},{10,11... | collective-permute-start | bytes 3145736 | tf_op jit(solution)/shard_map/ppermute | solution.py:161
  43.6 5.4 %collective-permute-start.8 = (bf16[128,4096]{1,0:T(8,128)(2,1)S(1)}, bf16[128,4096]{1,0:T(8,128)(2,1)S(1)}, u32[]{:S(2)}, u32[]{:S(2)}) collective-permute-start(bf16[128,4096]{1,0:T(8,128)(2,1)S(1)} %copy-done), channel_id=1, source_target_pairs={{0,1},{1,0},{2,3},{3,2},{4,5},{5,4},{6,7},{7,6},{8,9},{9,8},{10,11... | collective-permute-start | bytes 3145736 | tf_op jit(solution)/shard_map/ppermute | solution.py:161
  43.7 15.1 %collective-permute-start.9 = (bf16[48,4096]{1,0:T(8,128)(2,1)S(1)}, bf16[48,4096]{1,0:T(8,128)(2,1)S(1)}, u32[]{:S(2)}, u32[]{:S(2)}) collective-permute-start(bf16[48,4096]{1,0:T(8,128)(2,1)S(1)} %slice.50), channel_id=1, source_target_pairs={{0,2},{1,3},{2,0},{3,1},{4,6},{5,7},{6,4},{7,5},{8,10},{9,11},{10,... | collective-permute-start | bytes 1179656 | tf_op jit(solution)/shard_map/ppermute | solution.py:161
  44.6 14.5 %collective-permute-start.10 = (bf16[80,4096]{1,0:T(8,128)(2,1)}, bf16[80,4096]{1,0:T(8,128)(2,1)S(1)}, u32[]{:S(2)}, u32[]{:S(2)}) collective-permute-start(bf16[80,4096]{1,0:T(8,128)(2,1)} %collective-permute-done.5.refs_2_), channel_id=1, source_target_pairs={{0,1},{1,0},{2,3},{3,2},{4,5},{5,4},{6,7},{7,6},{8,9},{9,8},{10,11... | collective-permute-start | bytes 1966088 | tf_op jit(solution)/shard_map/ppermute | solution.py:161
  48.9 1.2 copy-start.1
  58.8 1.8 %collective-permute-start.11 = (bf16[48,4096]{1,0:T(8,128)(2,1)S(1)}, bf16[48,4096]{1,0:T(8,128)(2,1)S(1)}, u32[]{:S(2)}, u32[]{:S(2)}) collective-permute-start(bf16[48,4096]{1,0:T(8,128)(2,1)S(1)} %collective-permute-done.9.refs_3_), channel_id=1, source_target_pairs={{0,1},{1,0},{2,3},{3,2},{4,5},{5,4},{6,7},{7,6},{8,9},{9,8},{10,11... | collective-permute-start | bytes 1179656 | tf_op jit(solution)/shard_map/ppermute | solution.py:161
  69.8 4.2 %collective-permute-start.12 = (bf16[2,128,4096]{2,1,0:T(8,128)(2,1)S(1)}, bf16[2,128,4096]{2,1,0:T(8,128)(2,1)S(1)}, u32[]{:S(2)}, u32[]{:S(2)}) collective-permute-start(bf16[2,128,4096]{2,1,0:T(8,128)(2,1)S(1)} %get-tuple-element.37), channel_id=1, source_target_pairs={{0,1},{1,0},{2,3},{3,2},{4,5},{5,4},{6,7},{7,6},{8,9},{9,8},{10,11... | collective-permute-start | bytes 6291464 | tf_op jit(solution)/shard_map/ppermute | solution.py:161
  74.8 49.3 %collective-permute-start.13 = (bf16[2,128,4096]{2,1,0:T(8,128)(2,1)S(1)}, bf16[2,128,4096]{2,1,0:T(8,128)(2,1)S(1)}, u32[]{:S(2)}, u32[]{:S(2)}) collective-permute-start(bf16[2,128,4096]{2,1,0:T(8,128)(2,1)S(1)} %get-tuple-element.38), channel_id=1, source_target_pairs={{0,1},{1,0},{2,3},{3,2},{4,5},{5,4},{6,7},{7,6},{8,9},{9,8},{10,11... | collective-permute-start | bytes 6291464 | tf_op jit(solution)/shard_map/ppermute | solution.py:161
  75.1 49.1 %collective-permute-start.14 = (bf16[2,128,4096]{2,1,0:T(8,128)(2,1)S(1)}, bf16[2,128,4096]{2,1,0:T(8,128)(2,1)S(1)}, u32[]{:S(2)}, u32[]{:S(2)}) collective-permute-start(bf16[2,128,4096]{2,1,0:T(8,128)(2,1)S(1)} %add_convert_fusion), channel_id=1, source_target_pairs={{0,2},{1,3},{2,0},{3,1},{4,6},{5,7},{6,4},{7,5},{8,10},{9,11},{10,... | collective-permute-start | bytes 6291464 | tf_op jit(solution)/shard_map/ppermute | solution.py:161
  75.9 14.9 %collective-permute-start.15 = (bf16[2,4,2,128,128]{4,3,2,1,0:T(8,128)(2,1)S(1)}, bf16[2,4,2,128,128]{4,3,2,1,0:T(8,128)(2,1)S(1)}, u32[]{:S(2)}, u32[]{:S(2)}) collective-permute-start(bf16[2,4,2,128,128]{4,3,2,1,0:T(8,128)(2,1)S(1)} %get-tuple-element.41), channel_id=1, source_target_pairs={{0,12},{1,13},{2,14},{3,15},{4,0},{5,1},{6,2},{7,3},{8,4},{9,5},{1... | collective-permute-start | bytes 1572872 | tf_op jit(solution)/shard_map/ppermute | solution.py:161
  78.0 44.9 %collective-permute-start.16 = (bf16[2,4,2,128,128]{4,3,2,1,0:T(8,128)(2,1)S(1)}, bf16[2,4,2,128,128]{4,3,2,1,0:T(8,128)(2,1)S(1)}, u32[]{:S(2)}, u32[]{:S(2)}) collective-permute-start(bf16[2,4,2,128,128]{4,3,2,1,0:T(8,128)(2,1)S(1)} %get-tuple-element.43), channel_id=1, source_target_pairs={{0,8},{1,9},{2,10},{3,11},{4,12},{5,13},{6,14},{7,15},{8,0},{9,1},... | collective-permute-start | bytes 1572872 | tf_op jit(solution)/shard_map/ppermute | solution.py:161
  78.0 44.9 %collective-permute-start.17 = (bf16[2,4,2,128,128]{4,3,2,1,0:T(8,128)(2,1)S(1)}, bf16[2,4,2,128,128]{4,3,2,1,0:T(8,128)(2,1)S(1)}, u32[]{:S(2)}, u32[]{:S(2)}) collective-permute-start(bf16[2,4,2,128,128]{4,3,2,1,0:T(8,128)(2,1)S(1)} %get-tuple-element.45), channel_id=1, source_target_pairs={{0,4},{1,5},{2,6},{3,7},{4,8},{5,9},{6,10},{7,11},{8,12},{9,13},{1... | collective-permute-start | bytes 1572872 | tf_op jit(solution)/shard_map/ppermute | solution.py:161

commit v6 on v5

--- a/solution.py
+++ b/solution.py
@@ -222,9 +222,9 @@
         x_far, x_diag, *c_far, *c_diag, *weights, g_all)
 
     far = (far.astype(F32) + pp(diagonal, core_swap).astype(F32)).astype(BF16)
-    received = [pp(after(g, far), turn(-r)) for r, g in enumerate(g_send, 1)]
+    back = pp(far, y_swap)
+    received = [pp(g, turn(-r)) for r, g in enumerate(g_send, 1)]
     near = pp(after(near, far), core_swap)
-    back = pp(far, y_swap)
     output, grad_tokens = [(own[n].astype(F32) + near[n].astype(F32) + back[n].astype(F32)).astype(BF16)
                            for n in range(2)]
     grads = []

time: 127 us -> 127 us (level)
  no operation moved by 1% of the time
where the time goes in v6:
time: 127 us
  waiting for transfers between devices  83.5 us (66%)
  Pallas kernels  17.9 us (14%)
  starting transfers between devices  15.1 us (12%)
  other arithmetic  5.52 us (4%)
  local copies, waits for them, and re-layouts  3.79 us (3%)
    ppermute x18, waiting for transfers between devices, pp(): return lax.ppermute(v, axis, perm)  83.5 us
    pallas_call x2, Pallas kernels, call(): pl.pallas_call(functools.partial(ffn_kernel, lines, per, side, last), out...  17.9 us
    ppermute x18, starting transfers between devices, pp(): return lax.ppermute(v, axis, perm)  15.1 us
  transfers between devices with their start and end apart: 18, of which 9 were waited for; matrix products, arithmetic and copies ran while one was open for 4% of the time, Pallas kernels for 7%

profile of v6, /device:TPU:0, one launch (start us, length us, event | category | flops | bytes accessed | tf_op | source)
XLA Modules:
  0.0 126.6 jit_solution(15645323395589929044)
XLA Ops:
  0.7 3.0 %collective-permute-start.4 = (bf16[128,4096]{1,0:T(8,128)(2,1)}, bf16[128,4096]{1,0:T(8,128)(2,1)}, u32[]{:S(2)}, u32[]{:S(2)}) collective-permute-start(bf16[128,4096]{1,0:T(8,128)(2,1)} %refs_0_), channel_id=1, source_target_pairs={{0,2},{1,3},{2,0},{3,1},{4,6},{5,7},{6,4},{7,5},{8,10},{9,11},{10,... | collective-permute-start | bytes 3145736 | tf_op jit(solution)/shard_map/ppermute | solution.py:161
  3.7 1.0 broadcast_select_fusion
  4.7 2.7 %collective-permute-start = (bf16[4,2,128,128]{3,2,1,0:T(8,128)(2,1)S(1)}, bf16[4,2,128,128]{3,2,1,0:T(8,128)(2,1)S(1)}, u32[]{:S(2)}, u32[]{:S(2)}) collective-permute-start(bf16[4,2,128,128]{3,2,1,0:T(8,128)(2,1)S(1)} %broadcast_select_fusion), channel_id=1, source_target_pairs={{0,8},{1,9},{2,10},{3,11},{4,12},{5,13},{6,14},{7,15},{8,0},{9,1},... | collective-permute-start | bytes 786440 | tf_op jit(solution)/shard_map/ppermute | solution.py:161
  7.4 2.0 %slice.48 = bf16[80,4096]{1,0:T(8,128)(2,1)} slice(bf16[128,4096]{1,0:T(8,128)(2,1)} %refs_2_), slice={[0:80], [0:4096]} | slice | bytes 1310720 | tf_op jit(solution)/shard_map/slice | solution.py:171
  9.9 1.6 %collective-permute-start.7 = (bf16[2,4,2,128,128]{4,3,2,1,0:T(8,128)(2,1)S(1)}, bf16[2,4,2,128,128]{4,3,2,1,0:T(8,128)(2,1)S(1)}, u32[]{:S(2)}, u32[]{:S(2)}) collective-permute-start(bf16[2,4,2,128,128]{4,3,2,1,0:T(8,128)(2,1)S(1)} %pad_maximum_fusion.refs_6_.refs_8_), channel_id=1, source_target_pairs={{0,4},{1,5},{2,6},{3,7},{4,8},{5,9},{6,10},{7,11},{8,12},{9,13},{1... | collective-permute-start | bytes 1572872 | tf_op jit(solution)/shard_map/ppermute | solution.py:161
  11.5 19.4 %collective-permute-done.refs_4_.refs_6_ = bf16[4,2,128,128]{3,2,1,0:T(8,128)(2,1)S(1)} collective-permute-done((bf16[4,2,128,128]{3,2,1,0:T(8,128)(2,1)S(1)}, bf16[4,2,128,128]{3,2,1,0:T(8,128)(2,1)S(1)}, u32[]{:S(2)}, u32[]{:S(2)}) %collective-permute-start) | collective-permute-done | bytes 262176 | tf_op jit(solution)/shard_map/ppermute | solution.py:161
  30.9 1.5 %collective-permute-start.2 = (bf16[4,2,128,128]{3,2,1,0:T(8,128)(2,1)S(1)}, bf16[4,2,128,128]{3,2,1,0:T(8,128)(2,1)S(1)}, u32[]{:S(2)}, u32[]{:S(2)}) collective-permute-start(bf16[4,2,128,128]{3,2,1,0:T(8,128)(2,1)S(1)} %collective-permute-done.refs_4_.refs_6_), channel_id=1, source_target_pairs={{0,16},{16,0},{1,17},{17,1},{2,18},{18,2},{3,19},{19,3},{4,20},{20... | collective-permute-start | bytes 786440 | tf_op jit(solution)/shard_map/ppermute | solution.py:161
  33.0 4.5 %collective-permute-done.2.refs_5_.refs_7_ = bf16[4,2,128,128]{3,2,1,0:T(8,128)(2,1)S(1)} collective-permute-done((bf16[4,2,128,128]{3,2,1,0:T(8,128)(2,1)S(1)}, bf16[4,2,128,128]{3,2,1,0:T(8,128)(2,1)S(1)}, u32[]{:S(2)}, u32[]{:S(2)}) %collective-permute-start.2) | collective-permute-done | bytes 262176 | tf_op jit(solution)/shard_map/ppermute | solution.py:161
  37.4 5.6 %collective-permute-done.1.refs_8_.refs_10_ = bf16[2,4,2,128,128]{4,3,2,1,0:T(8,128)(2,1)S(1)} collective-permute-done((bf16[2,4,2,128,128]{4,3,2,1,0:T(8,128)(2,1)S(1)}, bf16[2,4,2,128,128]{4,3,2,1,0:T(8,128)(2,1)S(1)}, u32[]{:S(2)}, u32[]{:S(2)}) %collective-permute-start.1) | collective-permute-done | bytes 524320 | tf_op jit(solution)/shard_map/ppermute | solution.py:161
  43.7 0.9 collective-permute-start.9
  44.7 1.2 collective-permute-done.3.refs_1_
  45.9 3.0 %collective-permute-done.6.refs_1_ = bf16[128,4096]{1,0:T(8,128)(2,1)S(1)} collective-permute-done((bf16[128,4096]{1,0:T(8,128)(2,1)}, bf16[128,4096]{1,0:T(8,128)(2,1)S(1)}, u32[]{:S(2)}, u32[]{:S(2)}) %collective-permute-start.6) | collective-permute-done | bytes 1048608 | tf_op jit(solution)/shard_map/ppermute | solution.py:161
  48.9 1.2 copy-done.1
  50.2 8.6 %shard_map.93 = (bf16[2,128,4096]{2,1,0:T(8,128)(2,1)S(1)}, bf16[2,128,4096]{2,1,0:T(8,128)(2,1)S(1)}, f32[4,2,4,2,128,128]{5,4,3,2,1,0:T(8,128)S(1)}) custom-call(s32[260]{0:T(512)S(1)} %concatenate.3.scalars, bf16[128,4096]{1,0:T(8,128)(2,1)S(1)} %copy-done.1, bf16[128,4096]{1,0:T(8,128)(2,1)S(1)} %collective-permute-done.3.refs_1_, ...), custom_call_target="tpu_custom_call" | custom-call | flops 1048576 | bytes 1048576 | tf_op jit(solution)/shard_map/pallas_call | solution.py:203
  59.0 1.6 %collective-permute-done.11.refs_5_ = bf16[48,4096]{1,0:T(8,128)(2,1)S(1)} collective-permute-done((bf16[48,4096]{1,0:T(8,128)(2,1)S(1)}, bf16[48,4096]{1,0:T(8,128)(2,1)S(1)}, u32[]{:S(2)}, u32[]{:S(2)}) %collective-permute-start.11) | collective-permute-done | bytes 393248 | tf_op jit(solution)/shard_map/ppermute | solution.py:161
  60.6 9.2 %shard_map.94 = (bf16[2,128,4096]{2,1,0:T(8,128)(2,1)S(1)}, bf16[2,128,4096]{2,1,0:T(8,128)(2,1)S(1)}, f32[2,4,2,128,128]{4,3,2,1,0:T(8,128)S(1)}, bf16[2,4,2,12...) custom-call(s32[260]{0:T(512)S(1)} %concatenate.3.scalars, ...), custom_call_target="tpu_custom_call" | custom-call | flops 1048576 | bytes 1048576 | tf_op jit(solution)/shard_map/pallas_call | solution.py:203
  70.0 4.1 %collective-permute-done.12 = bf16[2,128,4096]{2,1,0:T(8,128)(2,1)S(1)} collective-permute-done((bf16[2,128,4096]{2,1,0:T(8,128)(2,1)S(1)}, bf16[2,128,4096]{2,1,0:T(8,128)(2,1)S(1)}, u32[]{:S(2)}, u32[]{:S(2)}) %collective-permute-start.12) | collective-permute-done | bytes 2097184 | tf_op jit(solution)/shard_map/ppermute | solution.py:161
  74.1 0.8 add_convert_fusion
  75.1 0.8 collective-permute-start.14
  75.9 2.1 %collective-permute-start.15 = (bf16[2,4,2,128,128]{4,3,2,1,0:T(8,128)(2,1)S(1)}, bf16[2,4,2,128,128]{4,3,2,1,0:T(8,128)(2,1)S(1)}, u32[]{:S(2)}, u32[]{:S(2)}) collective-permute-start(bf16[2,4,2,128,128]{4,3,2,1,0:T(8,128)(2,1)S(1)} %get-tuple-element.37), channel_id=1, source_target_pairs={{0,12},{1,13},{2,14},{3,15},{4,0},{5,1},{6,2},{7,3},{8,4},{9,5},{1... | collective-permute-start | bytes 1572872 | tf_op jit(solution)/shard_map/ppermute | solution.py:161
  78.7 12.2 %collective-permute-done.15 = bf16[2,4,2,128,128]{4,3,2,1,0:T(8,128)(2,1)S(1)} collective-permute-done((bf16[2,4,2,128,128]{4,3,2,1,0:T(8,128)(2,1)S(1)}, bf16[2,4,2,128,128]{4,3,2,1,0:T(8,128)(2,1)S(1)}, u32[]{:S(2)}, u32[]{:S(2)}) %collective-permute-start.15) | collective-permute-done | bytes 524320 | tf_op jit(solution)/shard_map/ppermute | solution.py:161
  90.9 32.0 %collective-permute-done.16 = bf16[2,4,2,128,128]{4,3,2,1,0:T(8,128)(2,1)S(1)} collective-permute-done((bf16[2,4,2,128,128]{4,3,2,1,0:T(8,128)(2,1)S(1)}, bf16[2,4,2,128,128]{4,3,2,1,0:T(8,128)(2,1)S(1)}, u32[]{:S(2)}, u32[]{:S(2)}) %collective-permute-start.16) | collective-permute-done | bytes 524320 | tf_op jit(solution)/shard_map/ppermute | solution.py:161
  122.8 1.2 add_bitcast_fusion
  124.1 2.5 %fusion.1 = (bf16[128,4096]{1,0:T(8,128)(2,1)}, bf16[128,4096]{1,0:T(8,128)(2,1)}) fusion(bf16[2,128,4096]{2,1,0:T(8,128)(2,1)S(1)} %collective-permute-done.14, bf16[2,128,4096]{2,1,0:T(8,128)(2,1)S(1)} %collective-permute-done.13, bf16[2,128,4096]{2,1,0:T(8,128)(2,1)S(1)} %get-tuple-element.28), kind=kLoop, calls=%fused_computation.4 | loop fusion | flops 6291456 | bytes 8388608 | tf_op jit(solution)/shard_map/convert_element_type | solution.py:228
  (38 shorter events, 3.2 us)
Async XLA Ops:
  0.6 9.2 %copy-start.3 = (bf16[4,2,128,128]{3,2,1,0:T(8,128)(2,1)S(1)}, bf16[4,2,128,128]{3,2,1,0:T(8,128)(2,1)}, u32[]{:S(2)}) copy-start(bf16[4,2,128,128]{3,2,1,0:T(8,128)(2,1)} %param.9) | copy-start | bytes 786436
  0.6 9.2 %copy-start.2 = (bf16[4,2,128,128]{3,2,1,0:T(8,128)(2,1)S(1)}, bf16[4,2,128,128]{3,2,1,0:T(8,128)(2,1)}, u32[]{:S(2)}) copy-start(bf16[4,2,128,128]{3,2,1,0:T(8,128)(2,1)} %param.8) | copy-start | bytes 786436
  0.7 42.9 %copy-start = (bf16[128,4096]{1,0:T(8,128)(2,1)S(1)}, bf16[128,4096]{1,0:T(8,128)(2,1)}, u32[]{:S(2)}) copy-start(bf16[128,4096]{1,0:T(8,128)(2,1)} %refs_2_) | copy-start | bytes 3145732
  0.7 31.7 %copy-start.4 = (s32[64,2]{0,1:T(2,128)S(1)}, s32[64,2]{0,1:T(2,128)}, u32[]{:S(2)}) copy-start(s32[64,2]{0,1:T(2,128)} %param.10) | copy-start | bytes 1540
  0.7 31.9 %copy-start.5 = (s32[64,2]{0,1:T(2,128)S(1)}, s32[64,2]{0,1:T(2,128)}, u32[]{:S(2)}) copy-start(s32[64,2]{0,1:T(2,128)} %param.11) | copy-start | bytes 1540
  0.7 42.4 %collective-permute-start.4 = (bf16[128,4096]{1,0:T(8,128)(2,1)}, bf16[128,4096]{1,0:T(8,128)(2,1)}, u32[]{:S(2)}, u32[]{:S(2)}) collective-permute-start(bf16[128,4096]{1,0:T(8,128)(2,1)} %refs_0_), channel_id=1, source_target_pairs={{0,2},{1,3},{2,0},{3,1},{4,6},{5,7},{6,4},{7,5},{8,10},{9,11},{10,... | collective-permute-start | bytes 3145736 | tf_op jit(solution)/shard_map/ppermute | solution.py:161
  4.7 26.2 %collective-permute-start = (bf16[4,2,128,128]{3,2,1,0:T(8,128)(2,1)S(1)}, bf16[4,2,128,128]{3,2,1,0:T(8,128)(2,1)S(1)}, u32[]{:S(2)}, u32[]{:S(2)}) collective-permute-start(bf16[4,2,128,128]{3,2,1,0:T(8,128)(2,1)S(1)} %broadcast_select_fusion), channel_id=1, source_target_pairs={{0,8},{1,9},{2,10},{3,11},{4,12},{5,13},{6,14},{7,15},{8,0},{9,1},... | collective-permute-start | bytes 786440 | tf_op jit(solution)/shard_map/ppermute | solution.py:161
  9.3 33.7 %collective-permute-start.5 = (bf16[80,4096]{1,0:T(8,128)(2,1)}, bf16[80,4096]{1,0:T(8,128)(2,1)}, u32[]{:S(2)}, u32[]{:S(2)}) collective-permute-start(bf16[80,4096]{1,0:T(8,128)(2,1)} %slice.48), channel_id=1, source_target_pairs={{0,2},{1,3},{2,0},{3,1},{4,6},{5,7},{6,4},{7,5},{8,10},{9,11},{10,... | collective-permute-start | bytes 1966088 | tf_op jit(solution)/shard_map/ppermute | solution.py:161
  9.9 23.1 %collective-permute-start.7 = (bf16[2,4,2,128,128]{4,3,2,1,0:T(8,128)(2,1)S(1)}, bf16[2,4,2,128,128]{4,3,2,1,0:T(8,128)(2,1)S(1)}, u32[]{:S(2)}, u32[]{:S(2)}) collective-permute-start(bf16[2,4,2,128,128]{4,3,2,1,0:T(8,128)(2,1)S(1)} %pad_maximum_fusion.refs_6_.refs_8_), channel_id=1, source_target_pairs={{0,4},{1,5},{2,6},{3,7},{4,8},{5,9},{6,10},{7,11},{8,12},{9,13},{1... | collective-permute-start | bytes 1572872 | tf_op jit(solution)/shard_map/ppermute | solution.py:161
  30.9 12.2 %collective-permute-start.1 = (bf16[2,4,2,128,128]{4,3,2,1,0:T(8,128)(2,1)S(1)}, bf16[2,4,2,128,128]{4,3,2,1,0:T(8,128)(2,1)S(1)}, u32[]{:S(2)}, u32[]{:S(2)}) collective-permute-start(bf16[2,4,2,128,128]{4,3,2,1,0:T(8,128)(2,1)S(1)} %pad_maximum_fusion.refs_6_.refs_8_), channel_id=1, source_target_pairs={{0,12},{1,13},{2,14},{3,15},{4,0},{5,1},{6,2},{7,3},{8,4},{9,5},{1... | collective-permute-start | bytes 1572872 | tf_op jit(solution)/shard_map/ppermute | solution.py:161
  30.9 6.6 %collective-permute-start.2 = (bf16[4,2,128,128]{3,2,1,0:T(8,128)(2,1)S(1)}, bf16[4,2,128,128]{3,2,1,0:T(8,128)(2,1)S(1)}, u32[]{:S(2)}, u32[]{:S(2)}) collective-permute-start(bf16[4,2,128,128]{3,2,1,0:T(8,128)(2,1)S(1)} %collective-permute-done.refs_4_.refs_6_), channel_id=1, source_target_pairs={{0,16},{16,0},{1,17},{17,1},{2,18},{18,2},{3,19},{19,3},{4,20},{20... | collective-permute-start | bytes 786440 | tf_op jit(solution)/shard_map/ppermute | solution.py:161
  43.1 2.9 %collective-permute-start.3 = (bf16[128,4096]{1,0:T(8,128)(2,1)}, bf16[128,4096]{1,0:T(8,128)(2,1)S(1)}, u32[]{:S(2)}, u32[]{:S(2)}) collective-permute-start(bf16[128,4096]{1,0:T(8,128)(2,1)} %refs_0_), channel_id=1, source_target_pairs={{0,1},{1,0},{2,3},{3,2},{4,5},{5,4},{6,7},{7,6},{8,9},{9,8},{10,11... | collective-permute-start | bytes 3145736 | tf_op jit(solution)/shard_map/ppermute | solution.py:161
  43.1 5.9 %collective-permute-start.6 = (bf16[128,4096]{1,0:T(8,128)(2,1)}, bf16[128,4096]{1,0:T(8,128)(2,1)S(1)}, u32[]{:S(2)}, u32[]{:S(2)}) collective-permute-start(bf16[128,4096]{1,0:T(8,128)(2,1)} %collective-permute-done.4.refs_0_), channel_id=1, source_target_pairs={{0,1},{1,0},{2,3},{3,2},{4,5},{5,4},{6,7},{7,6},{8,9},{9,8},{10,11... | collective-permute-start | bytes 3145736 | tf_op jit(solution)/shard_map/ppermute | solution.py:161
  43.6 5.4 %collective-permute-start.8 = (bf16[128,4096]{1,0:T(8,128)(2,1)S(1)}, bf16[128,4096]{1,0:T(8,128)(2,1)S(1)}, u32[]{:S(2)}, u32[]{:S(2)}) collective-permute-start(bf16[128,4096]{1,0:T(8,128)(2,1)S(1)} %copy-done), channel_id=1, source_target_pairs={{0,1},{1,0},{2,3},{3,2},{4,5},{5,4},{6,7},{7,6},{8,9},{9,8},{10,11... | collective-permute-start | bytes 3145736 | tf_op jit(solution)/shard_map/ppermute | solution.py:161
  43.7 15.1 %collective-permute-start.9 = (bf16[48,4096]{1,0:T(8,128)(2,1)S(1)}, bf16[48,4096]{1,0:T(8,128)(2,1)S(1)}, u32[]{:S(2)}, u32[]{:S(2)}) collective-permute-start(bf16[48,4096]{1,0:T(8,128)(2,1)S(1)} %slice.50), channel_id=1, source_target_pairs={{0,2},{1,3},{2,0},{3,1},{4,6},{5,7},{6,4},{7,5},{8,10},{9,11},{10,... | collective-permute-start | bytes 1179656 | tf_op jit(solution)/shard_map/ppermute | solution.py:161
  44.6 14.5 %collective-permute-start.10 = (bf16[80,4096]{1,0:T(8,128)(2,1)}, bf16[80,4096]{1,0:T(8,128)(2,1)S(1)}, u32[]{:S(2)}, u32[]{:S(2)}) collective-permute-start(bf16[80,4096]{1,0:T(8,128)(2,1)} %collective-permute-done.5.refs_2_), channel_id=1, source_target_pairs={{0,1},{1,0},{2,3},{3,2},{4,5},{5,4},{6,7},{7,6},{8,9},{9,8},{10,11... | collective-permute-start | bytes 1966088 | tf_op jit(solution)/shard_map/ppermute | solution.py:161
  48.9 1.2 copy-start.1
  58.8 1.8 %collective-permute-start.11 = (bf16[48,4096]{1,0:T(8,128)(2,1)S(1)}, bf16[48,4096]{1,0:T(8,128)(2,1)S(1)}, u32[]{:S(2)}, u32[]{:S(2)}) collective-permute-start(bf16[48,4096]{1,0:T(8,128)(2,1)S(1)} %collective-permute-done.9.refs_3_), channel_id=1, source_target_pairs={{0,1},{1,0},{2,3},{3,2},{4,5},{5,4},{6,7},{7,6},{8,9},{9,8},{10,11... | collective-permute-start | bytes 1179656 | tf_op jit(solution)/shard_map/ppermute | solution.py:161
  69.9 4.2 %collective-permute-start.12 = (bf16[2,128,4096]{2,1,0:T(8,128)(2,1)S(1)}, bf16[2,128,4096]{2,1,0:T(8,128)(2,1)S(1)}, u32[]{:S(2)}, u32[]{:S(2)}) collective-permute-start(bf16[2,128,4096]{2,1,0:T(8,128)(2,1)S(1)} %get-tuple-element.34), channel_id=1, source_target_pairs={{0,1},{1,0},{2,3},{3,2},{4,5},{5,4},{6,7},{7,6},{8,9},{9,8},{10,11... | collective-permute-start | bytes 6291464 | tf_op jit(solution)/shard_map/ppermute | solution.py:161
  74.9 49.2 %collective-permute-start.13 = (bf16[2,128,4096]{2,1,0:T(8,128)(2,1)S(1)}, bf16[2,128,4096]{2,1,0:T(8,128)(2,1)S(1)}, u32[]{:S(2)}, u32[]{:S(2)}) collective-permute-start(bf16[2,128,4096]{2,1,0:T(8,128)(2,1)S(1)} %get-tuple-element.35), channel_id=1, source_target_pairs={{0,1},{1,0},{2,3},{3,2},{4,5},{5,4},{6,7},{7,6},{8,9},{9,8},{10,11... | collective-permute-start | bytes 6291464 | tf_op jit(solution)/shard_map/ppermute | solution.py:161
  75.1 49.0 %collective-permute-start.14 = (bf16[2,128,4096]{2,1,0:T(8,128)(2,1)S(1)}, bf16[2,128,4096]{2,1,0:T(8,128)(2,1)S(1)}, u32[]{:S(2)}, u32[]{:S(2)}) collective-permute-start(bf16[2,128,4096]{2,1,0:T(8,128)(2,1)S(1)} %add_convert_fusion), channel_id=1, source_target_pairs={{0,2},{1,3},{2,0},{3,1},{4,6},{5,7},{6,4},{7,5},{8,10},{9,11},{10,... | collective-permute-start | bytes 6291464 | tf_op jit(solution)/shard_map/ppermute | solution.py:161
  75.9 15.0 %collective-permute-start.15 = (bf16[2,4,2,128,128]{4,3,2,1,0:T(8,128)(2,1)S(1)}, bf16[2,4,2,128,128]{4,3,2,1,0:T(8,128)(2,1)S(1)}, u32[]{:S(2)}, u32[]{:S(2)}) collective-permute-start(bf16[2,4,2,128,128]{4,3,2,1,0:T(8,128)(2,1)S(1)} %get-tuple-element.37), channel_id=1, source_target_pairs={{0,12},{1,13},{2,14},{3,15},{4,0},{5,1},{6,2},{7,3},{8,4},{9,5},{1... | collective-permute-start | bytes 1572872 | tf_op jit(solution)/shard_map/ppermute | solution.py:161
  78.0 44.8 %collective-permute-start.16 = (bf16[2,4,2,128,128]{4,3,2,1,0:T(8,128)(2,1)S(1)}, bf16[2,4,2,128,128]{4,3,2,1,0:T(8,128)(2,1)S(1)}, u32[]{:S(2)}, u32[]{:S(2)}) collective-permute-start(bf16[2,4,2,128,128]{4,3,2,1,0:T(8,128)(2,1)S(1)} %get-tuple-element.38), channel_id=1, source_target_pairs={{0,8},{1,9},{2,10},{3,11},{4,12},{5,13},{6,14},{7,15},{8,0},{9,1},... | collective-permute-start | bytes 1572872 | tf_op jit(solution)/shard_map/ppermute | solution.py:161
  78.0 44.8 %collective-permute-start.17 = (bf16[2,4,2,128,128]{4,3,2,1,0:T(8,128)(2,1)S(1)}, bf16[2,4,2,128,128]{4,3,2,1,0:T(8,128)(2,1)S(1)}, u32[]{:S(2)}, u32[]{:S(2)}) collective-permute-start(bf16[2,4,2,128,128]{4,3,2,1,0:T(8,128)(2,1)S(1)} %get-tuple-element.39), channel_id=1, source_target_pairs={{0,4},{1,5},{2,6},{3,7},{4,8},{5,9},{6,10},{7,11},{8,12},{9,13},{1... | collective-permute-start | bytes 1572872 | tf_op jit(solution)/shard_map/ppermute | solution.py:161
